TPU v7x, 32 devices: a whole 2x2x4 slice. The times are simulated.
32 devices in a mesh: dp: 8 (over z, y), mp: 4 (over x, core).
Axes of the slice: x: 2, y: 2, z: 4, core: 2. Of those that a mesh axis runs over, the one named last changes fastest.
Arguments:
- tokens: bfloat16 [256, 5120], P('dp'), may hold values from -14 to 14
- parent_keys: bfloat16 [64, 256, 1024], P('dp', None, 'mp'), may hold values from -56 to 56
- parent_values: bfloat16 [64, 256, 1024], P('dp', None, 'mp'), may hold values from -24 to 24
- parent_blocks: int32 [64], replicated, may hold values from 1 to 2
- child_parent: int32 [256], replicated, may hold values from 0 to 63, as said below
- child_count: int32 [8], P('dp'), may hold values from 24 to 32, as said below
- node_shard: int32 [256], replicated, may hold values from 0 to 7, as said below
- attn_gain: float32 [5120], replicated, may hold values from 0.5 to 1.5
- w_query: bfloat16 [5120, 3072], P(None, 'mp'), may hold values from -1 to 1
- w_key: bfloat16 [5120, 1024], P(None, 'mp'), may hold values from -1 to 1
- w_value: bfloat16 [5120, 1024], P(None, 'mp'), may hold values from -0.078125 to 0.078125
- w_out: bfloat16 [3072, 5120], P('mp'), may hold values from -0.109375 to 0.109375
- reward_up: bfloat16 [8, 5120, 512], P('dp', 'mp'), may hold values from -0.078125 to 0.078125
- reward_out: float32 [8, 512], P('dp'), may hold values from -0.25 to 0.25
Outputs:
- rewards: float32 [8, 384], P(None, 'dp')
Inputs may be any that keep to these rules, and one draw needn't show every extreme that they name: `child_parent`: the children of one index of dp name parents of one index of dp at most 8 times, and exactly 8 times for some pair at every index. `child_count`: every index of dp holds 24 or more live children, and some index holds 32. `node_shard`: the children of one index of dp name one shard at most 6 times, exactly 6 times for some shard at every index.
All inputs are finite; a program needn't handle non-finite values.
Results may differ from a plain program's by a relative error of at most 0.015.
Values may be sent and summed in bfloat16 or wider, within the bound.
No kernel may reach another device: no remote copies, remote signals or barrier semaphores. Data moves between devices by JAX's collectives and lax.ppermute only.
A program may use at most 128 MiB of HBM per device.

v0:
```python
import functools
import math

import jax
import jax.numpy as jnp
from jax import lax
from jax.experimental import pallas as pl
from jax.experimental.pallas import tpu as pltpu
from jax.sharding import PartitionSpec as P

D = 5120
HEADS = 24
KVH = 8
HD = 128
STEPS = 8
GROUP = HEADS // KVH
CHUNK = 512
COLUMNS = 256
ROWS = 64
MASKED = -1e30
EXPONENT = HD ** (-0.5) * math.log2(math.e)
VMEM = pltpu.VMEM
NOTES = 128
LIVE, RANK, SHARD, PARENT, SOURCE = range(5)


def dot(a, b):
    return jnp.dot(a, b, preferred_element_type=jnp.float32)


def held(x):
    return pltpu.with_memory_space_constraint(x, VMEM)


def far(x):
    return pltpu.with_memory_space_constraint(x, pltpu.HBM)


def struct(shape, dtype=jnp.bfloat16):
    return jax.ShapeDtypeStruct(shape, dtype)


WHOLE = pl.BlockSpec(memory_space=VMEM)
FAR = pl.BlockSpec(memory_space=pltpu.HBM)
SMALL = pl.CostEstimate(flops=0, bytes_accessed=0, transcendentals=0)
SCALARS = pl.BlockSpec(memory_space=pltpu.SMEM)


def coordinates():
    me = lax.axis_index("mp")
    return lax.rem(me, 2), lax.axis_index("dp"), me


def dispatch_kernel(parents, groups, count, parent_far, shard_far, tokens_far, reward_far, *rest):
    core, own, me = coordinates()
    blocks, near = rest[:groups], rest[groups:]
    parent_row, shard_row, tokens, reward_out, sems = near
    children, half = tokens.shape
    sources = (parent_far, shard_far, tokens_far.at[:, pl.ds(pl.multiple_of(core * half, half), half)], reward_far)
    copies = [pltpu.make_async_copy(a, b, sems.at[i]) for i, (a, b) in enumerate(zip(sources, near))]
    for copy in copies:
        copy.start()
    for copy in copies:
        copy.wait()
    capacity = blocks[0].shape[0]
    everyone = parent_row.shape[1]
    int32, float32, bfloat16 = jnp.int32, jnp.float32, jnp.bfloat16

    mine = lax.broadcasted_iota(int32, (everyone, children), 0) - own * children
    mine = (mine == lax.broadcasted_iota(int32, (everyone, children), 1)).astype(float32).astype(bfloat16)

    def row_and_column(table):
        table = table[...].astype(float32).astype(bfloat16)
        column = lax.dot_general(mine, table, (((0,), (1,)), ((), ())), preferred_element_type=float32)
        return dot(table, mine).astype(int32), column.astype(int32)

    parent, parent_c = row_and_column(parent_row)
    shard, shard_c = row_and_column(shard_row)
    source, source_c = lax.div(parent, parents), lax.div(parent_c, parents)
    first = lax.broadcasted_iota(int32, (children, children), 0)
    second = lax.broadcasted_iota(int32, (children, children), 1)
    live = lax.broadcasted_iota(int32, (1, children), 1) < count[0]
    live_c = lax.broadcasted_iota(int32, (children, 1), 0) < count[0]
    rank = jnp.sum(jnp.where((source_c == source) & (first < second) & live_c, 1, 0), 0, keepdims=True)
    slot = (source ^ own) * capacity + rank
    slot = jnp.where(live, slot, -1)
    reward_rank = jnp.sum(jnp.where((shard_c == shard) & (second < first) & live, 1, 0), 1, keepdims=True)
    lane = lax.broadcasted_iota(int32, (children, NOTES), 1)
    notes = jnp.where(lane == LIVE, live_c.astype(int32), 0)
    for at, value in ((RANK, reward_rank), (SHARD, shard_c), (PARENT, lax.rem(parent_c, parents)), (SOURCE, own)):
        notes = jnp.where(lane == at, value, notes)

    width = blocks[0].shape[1] - half - NOTES
    hidden = (width - 128) // 3
    rest = jnp.zeros((1, hidden), float32)
    for m in range(reward_out.shape[1] // hidden):
        rest = rest + jnp.where(me == m, reward_out[:, m * hidden : (m + 1) * hidden], 0.0)
    parts = []
    for _ in range(3):
        parts.append(rest.astype(bfloat16).astype(float32))
        rest = rest - parts[-1]
    parts.append(jnp.full((1, 128), 1, int32).astype(float32) * count[0].astype(float32))
    shared = jnp.broadcast_to(jnp.concatenate(parts, 1), (capacity, width))

    rows = lax.broadcasted_iota(int32, (groups * capacity, children), 0)
    put = (rows == slot).astype(float32).astype(bfloat16)
    token_rows = dot(put, tokens[...])
    note_rows = dot(put, notes.astype(float32).astype(bfloat16))
    for k, block in enumerate(blocks):
        at = slice(k * capacity, (k + 1) * capacity)
        block[...] = jnp.concatenate([token_rows[at], note_rows[at], shared], 1).astype(bfloat16)


def dispatch(parents, child_count, child_parent, node_shard, tokens, reward_out, groups, capacity, hidden):
    children, half = tokens.shape[0], tokens.shape[1] // 2
    tables = (child_parent[None], node_shard[None])
    return pl.pallas_call(
        functools.partial(dispatch_kernel, parents, groups),
        out_shape=(struct((capacity, half + NOTES + 3 * hidden + 128)),) * groups,
        in_specs=[SCALARS] + [FAR] * 4,
        out_specs=(WHOLE,) * groups,
        scratch_shapes=[VMEM(x.shape, x.dtype) for x in tables]
        + [VMEM((children, half), tokens.dtype), VMEM(reward_out.shape, reward_out.dtype)]
        + [pltpu.SemaphoreType.DMA((4,))],
        compiler_params=pltpu.CompilerParams(vmem_limit_bytes=8 << 20),
        cost_estimate=SMALL,
        name="dispatch",
    )(child_count, *map(far, (*tables, tokens, reward_out)))


def pack_kernel(offset, hidden, prefix, blocks_held, parent_row, *rest):
    blocks, (row, notes, bias, scale, over) = rest[:-5], rest[-5:]
    _, own, _ = coordinates()
    groups, capacity = len(blocks), blocks[0].shape[0]
    rows, half = row.shape
    slots = groups * capacity
    arrived = jnp.concatenate([block[...].astype(jnp.float32) for block in blocks], 0)
    live = arrived[:, half + LIVE : half + LIVE + 1]
    first = lax.broadcasted_iota(jnp.int32, (slots, slots), 0)
    second = lax.broadcasted_iota(jnp.int32, (slots, slots), 1)
    place = jnp.sum(jnp.where(first < second, live, 0.0), 0, keepdims=True)
    kept = jnp.sum(jnp.where(first == second, live, 0.0), 0, keepdims=True) > 0.5
    wanted = lax.broadcasted_iota(jnp.int32, (rows, slots), 0) + offset
    take = (wanted == place.astype(jnp.int32)) & kept
    take = take.astype(jnp.float32).astype(jnp.bfloat16)
    row[...] = dot(take, arrived[:, :half].astype(jnp.bfloat16)).astype(jnp.bfloat16)
    note = dot(take, arrived[:, half : half + NOTES].astype(jnp.bfloat16))
    notes[...] = note
    parent = note[:, PARENT : PARENT + 1].astype(jnp.int32)
    parents = bias.shape[1] // prefix
    position = lax.broadcasted_iota(jnp.int32, (rows, prefix), 1)
    for p in range(parents):
        usable = (parent == p) & (position < blocks_held[own * parents + p] * 128)
        bias[:, p * prefix : (p + 1) * prefix] = jnp.where(usable, 0.0, MASKED)
    base = half + NOTES
    child = lax.broadcasted_iota(jnp.int32, parent_row.shape, 1)
    children = parent_row.shape[1] // groups
    at, child = lax.div(child, children), lax.rem(child, children)
    count = jnp.zeros(parent_row.shape, jnp.float32)
    for k in range(groups):
        head = arrived[k * capacity : k * capacity + 1, base:]
        scale[pl.ds(own ^ k, 1), :] = head[:, :hidden] + head[:, hidden : 2 * hidden] + head[:, 2 * hidden : 3 * hidden]
        count = jnp.where(at == (own ^ k), head[:, 3 * hidden : 3 * hidden + 1], count)
    source = lax.div(parent_row[...], parents)
    going = child < count.astype(jnp.int32)
    most = jnp.zeros((1, 1), jnp.float32)
    for d in range(groups):
        load = jnp.sum(jnp.where((source == d) & going, 1.0, 0.0), 1, keepdims=True)
        most = jnp.maximum(most, load)
    over[...] = jnp.broadcast_to((most > rows).astype(jnp.int32), over.shape)


def pack(offset, rows, hidden, prefix, blocks_held, child_parent, blocks):
    half = D // 2
    groups = len(blocks)
    parents = blocks_held.shape[0] // groups
    return pl.pallas_call(
        functools.partial(pack_kernel, offset, hidden, prefix),
        out_shape=(
            struct((rows, half)),
            struct((rows, NOTES), jnp.float32),
            struct((rows, parents * prefix), jnp.float32),
            struct((groups, hidden), jnp.float32),
            struct((8, 128), jnp.int32),
        ),
        in_specs=[SCALARS] + [WHOLE] * (1 + groups),
        out_specs=[WHOLE] * 5,
        compiler_params=pltpu.CompilerParams(vmem_limit_bytes=12 << 20),
        cost_estimate=SMALL,
        name="pack",
    )(blocks_held, child_parent[None], *blocks)


def project(attn, w_out, out, first):
    width = out.shape[1]

    @pl.loop(0, width // CHUNK)
    def _(i):
        columns = pl.ds(pl.multiple_of(first + i * CHUNK, CHUNK), CHUNK)
        out[:, pl.ds(pl.multiple_of(i * CHUNK, CHUNK), CHUNK)] = dot(
            attn[...], w_out[:, columns]
        )[: out.shape[0]].astype(out.dtype)


def step_kernel(step, own, peer, gain, w_query, w_key, w_value, keys, values, bias, w_out, *rest):
    past_keys, past_values = rest[:step], rest[step : 2 * step]
    rest = rest[2 * step :]
    half = own.shape[1]
    slots = own.shape[0]
    q_cols, kv_cols = w_query.shape[1], w_key.shape[1]
    kv_heads = kv_cols // HD
    ready = {}
    if step == 0:
        part, attn, key_now, value_now, norm, *kept, normed, query, sems = rest
        moves = [(w_query, kept[0], at, min(at + COLUMNS, q_cols)) for at in range(0, q_cols, COLUMNS)]
        moves += [(w, v, 0, w.shape[1]) for w, v in zip((w_key, w_value, keys, values, w_out), kept[1:])]
        for i, (source, target, at, end) in enumerate(moves):
            copy = pltpu.make_async_copy(source.at[:, at:end], target.at[:, at:end], sems.at[i])
            copy.start()
            ready[i] = copy
        w_query, w_key, w_value, keys, values, w_out = kept
    else:
        part, attn, key_now, value_now, norm, normed, query = rest
    arrivals = iter(ready.values())

    def arrive():
        for copy in arrivals:
            copy.wait()
            break

    core, _, _ = coordinates()
    first = core == 0
    low = jnp.where(first, own[...], peer[...]).astype(jnp.float32)
    high = jnp.where(first, peer[...], own[...]).astype(jnp.float32)
    squares = jnp.sum(low * low, -1, keepdims=True) + jnp.sum(high * high, -1, keepdims=True)
    factor = lax.rsqrt(squares / D + 1e-06)
    norm[...] = jnp.broadcast_to(factor, norm.shape)
    normed[:slots, :half] = (low * factor * gain[:, :half]).astype(jnp.bfloat16)
    normed[:slots, half:] = (high * factor * gain[:, half:]).astype(jnp.bfloat16)
    if normed.shape[0] > slots:
        normed[slots:, :] = jnp.zeros((normed.shape[0] - slots, D), jnp.bfloat16)
    for at in range(0, q_cols, COLUMNS):
        end = min(at + COLUMNS, q_cols)
        arrive()
        query[:, at:end] = dot(normed[...], w_query[:, at:end])
    arrive()
    query[:, q_cols : q_cols + kv_cols] = dot(normed[...], w_key[...])
    arrive()
    query[:, q_cols + kv_cols :] = dot(normed[...], w_value[...])
    arrive()
    arrive()
    key_now[...] = query[:slots, q_cols : q_cols + kv_cols].astype(jnp.bfloat16)
    value_now[...] = query[:slots, q_cols + kv_cols :].astype(jnp.bfloat16)
    recent = slots * (step + 1)
    row = lax.broadcasted_iota(jnp.int32, (GROUP * slots, recent), 0)
    column = lax.broadcasted_iota(jnp.int32, (GROUP * slots, recent), 1)
    same = lax.rem(row, slots) == lax.rem(column, slots)
    for head in range(kv_heads):
        lanes = slice(head * HD, (head + 1) * HD)
        q = jnp.concatenate(
            [query[:slots, (head * GROUP + g) * HD : (head * GROUP + g + 1) * HD] for g in range(GROUP)], 0
        ).astype(jnp.bfloat16)
        k_new = jnp.concatenate([k[:, lanes] for k in past_keys] + [key_now[:, lanes]], 0)
        v_new = jnp.concatenate([v[:, lanes] for v in past_values] + [value_now[:, lanes]], 0)
        contract = (((1,), (1,)), ((), ()))
        s_old = lax.dot_general(q, keys[:, lanes], contract, preferred_element_type=jnp.float32)
        s_old = s_old + jnp.concatenate([bias[...]] * GROUP, 0)
        s_new = lax.dot_general(q, k_new, contract, preferred_element_type=jnp.float32)
        s_new = jnp.where(same, s_new, MASKED)
        top = jnp.maximum(jnp.max(s_old, -1, keepdims=True), jnp.max(s_new, -1, keepdims=True))
        p_old = jnp.exp2(s_old * EXPONENT - top * EXPONENT)
        p_new = jnp.exp2(s_new * EXPONENT - top * EXPONENT)
        total = jnp.sum(p_old, -1, keepdims=True) + jnp.sum(p_new, -1, keepdims=True)
        summed = dot(p_old.astype(jnp.bfloat16), values[:, lanes]) + dot(p_new.astype(jnp.bfloat16), v_new)
        result = (summed / total).astype(jnp.bfloat16)
        for g in range(GROUP):
            at = (head * GROUP + g) * HD
            attn[:slots, at : at + HD] = result[g * slots : (g + 1) * slots]
    if attn.shape[0] > slots:
        attn[slots:, :] = jnp.zeros((attn.shape[0] - slots, q_cols), jnp.bfloat16)
    arrive()
    project(attn, w_out, part, (1 - core) * half)


def expand(step, own, peer, gain, w_query, w_key, w_value, keys, values, bias, w_out, past_keys, past_values):
    slots, half = own.shape
    kv_cols = w_key.shape[1]
    q_cols = w_query.shape[1]
    padded = -(-slots // ROWS) * ROWS
    weights = (w_query, w_key, w_value, keys, values, w_out)
    kept, sems = [], []
    place = WHOLE
    if step == 0:
        kept = [VMEM(w.shape, w.dtype) for w in weights]
        sems = [pltpu.SemaphoreType.DMA((-(-q_cols // COLUMNS) + 5,))]
        place = pl.BlockSpec(memory_space=pl.ANY)
    return pl.pallas_call(
        functools.partial(step_kernel, step),
        out_shape=(
            struct((slots, half)), struct((padded, q_cols)), struct((slots, kv_cols)), struct((slots, kv_cols)),
            struct((slots, 128), jnp.float32), *kept
        ),
        in_specs=[WHOLE] * 3 + [place] * 5 + [WHOLE, place] + [WHOLE] * (2 * step),
        out_specs=[WHOLE] * (5 + len(kept)),
        scratch_shapes=[VMEM((padded, D), jnp.bfloat16), VMEM((padded, q_cols + 2 * kv_cols), jnp.float32)] + sems,
        compiler_params=pltpu.CompilerParams(vmem_limit_bytes=16 << 20),
        cost_estimate=SMALL,
        name="expand",
    )(own, peer, gain, w_query, w_key, w_value, keys, values, bias, w_out, *past_keys, *past_values)


def project_kernel(attn, w_out, part):
    core, _, _ = coordinates()
    project(attn, w_out, part, core * part.shape[1])


def project_own(rows, attn, w_out):
    return pl.pallas_call(
        project_kernel,
        out_shape=struct((rows, w_out.shape[1] // 2), jnp.float32),
        in_specs=[WHOLE, WHOLE],
        out_specs=WHOLE,
        compiler_params=pltpu.CompilerParams(vmem_limit_bytes=8 << 20),
        cost_estimate=SMALL,
        name="project_own",
    )(attn, w_out)


def score_kernel(steps, load, cuts, mp, notes, *refs):
    take = lambda count: [refs.pop(0) for _ in range(count)]
    refs = list(refs)
    ups, own_rows, peer_rows, blocks = take(cuts), take(steps), take(steps), take(mp)
    kept = take(cuts * load)
    flat, total, *sems = refs
    groups, depth, hidden = ups[0].shape
    rows = own_rows[0].shape[0]
    core, _, me = coordinates()
    for t in range(steps):
        target = flat.at[t * rows : (t + 1) * rows]
        for m in range(mp):
            at = m % (mp // 2) * depth * cuts
            for c in range(2):
                source = (own_rows if m // (mp // 2) == c else peer_rows)[t].at[:, at : at + depth * cuts]

                @pl.when((me == m) & (core == c))
                def _():
                    if load:
                        pltpu.make_async_copy(source, target, sems[0].at[t]).start()
                    else:
                        target[...] = source[...]

    copies = {}
    if load:
        for r in range(groups):
            for i in range(cuts):
                copies[r, i] = pltpu.make_async_copy(ups[i].at[r], kept[i].at[r], sems[1].at[r, i])
                copies[r, i].start()
        ups = kept
        for t in range(steps):
            target = flat.at[t * rows : (t + 1) * rows]
            pltpu.make_async_copy(target, target, sems[0].at[t]).wait()
    shard = jnp.concatenate([notes[:, SHARD : SHARD + 1].astype(jnp.int32)] * steps, 0)
    for r in range(groups):
        for i in range(cuts):
            if load:
                copies[r, i].wait()
        for at in range(0, hidden, COLUMNS):
            end = min(at + COLUMNS, hidden)
            z = sum(dot(flat[:, i * depth : (i + 1) * depth], ups[i][r, :, at:end]) for i in range(cuts))
            here = jnp.where(shard == r, z, 0.0)
            total[:, at:end] = here if r == 0 else total[:, at:end] + here
    width = hidden // mp
    for j, block in enumerate(blocks):
        for m in range(mp):

            @pl.when((me ^ j) == m)
            def _():
                block[...] = total[:, m * width : (m + 1) * width].astype(jnp.bfloat16)


def score(mp, notes, ups, own_rows, peer_rows, load):
    steps, cuts = len(own_rows), len(ups)
    groups, depth, hidden = ups[0].shape
    count = steps * own_rows[0].shape[0]
    block = struct((count, hidden // mp))
    place = FAR if load else WHOLE
    return pl.pallas_call(
        functools.partial(score_kernel, steps, load, cuts, mp),
        out_shape=(block,) * mp + tuple(VMEM(up.shape, up.dtype) for up in ups) * load,
        in_specs=[WHOLE] + [place] * (cuts + 2 * steps),
        out_specs=(WHOLE,) * (mp + cuts * load),
        scratch_shapes=[VMEM((count, depth * cuts), jnp.bfloat16), VMEM((count, hidden), jnp.float32)]
        + [pltpu.SemaphoreType.DMA((steps,)), pltpu.SemaphoreType.DMA((groups, cuts))] * load,
        compiler_params=pltpu.CompilerParams(vmem_limit_bytes=16 << 20),
        cost_estimate=SMALL,
        name="score",
    )(notes, *(map(far, (*ups, *own_rows, *peer_rows)) if load else (*ups, *own_rows, *peer_rows)))


def scores_of(notes, scale, parts, factors):
    rows = notes.shape[0]
    shard = notes[:, SHARD : SHARD + 1].astype(jnp.int32)
    gain = jnp.zeros((rows, scale.shape[1]), jnp.float32)
    for r in range(scale.shape[0]):
        gain = gain + jnp.where(shard == r, scale[r : r + 1, :], 0.0)
    values = []
    for t, factor in enumerate(factors):
        z = sum(part[t * rows : (t + 1) * rows, :].astype(jnp.float32) for part in parts) * factor
        values.append(jnp.sum(z * jax.nn.sigmoid(z) * gain, -1, keepdims=True))
    return values


def finish_kernel(steps, notes, scale, *refs):
    norms, parts, out = refs[:steps], refs[steps:-1], refs[-1]
    lane = lax.broadcasted_iota(jnp.int32, out.shape, 1)
    total = jnp.zeros(out.shape, jnp.float32)
    for t, value in enumerate(scores_of(notes, scale, parts, [norm[:, :1] for norm in norms])):
        total = jnp.where(lane == t, value, total)
    out[...] = total


def finish(notes, scale, norms, parts):
    return pl.pallas_call(
        functools.partial(finish_kernel, len(norms)),
        out_shape=struct((notes.shape[0], 128), jnp.float32),
        in_specs=[WHOLE] * (2 + len(norms) + len(parts)),
        out_specs=WHOLE,
        compiler_params=pltpu.CompilerParams(vmem_limit_bytes=12 << 20),
        cost_estimate=SMALL,
        name="finish",
    )(notes, scale, *norms, *parts)


def place_kernel(groups, cap, before, notes, scale, own_row, peer_row, *refs):
    parts, table = refs[:-1], refs[-1]
    rows = notes.shape[0]
    values = [before[:, t : t + 1] for t in range(STEPS - 1)]
    low, high = own_row[...].astype(jnp.float32), peer_row[...].astype(jnp.float32)
    squares = jnp.sum(low * low, -1, keepdims=True) + jnp.sum(high * high, -1, keepdims=True)
    values += scores_of(notes, scale, parts, [lax.rsqrt(squares / D + 1e-06)])
    number = lambda lane: notes[:, lane : lane + 1].astype(jnp.int32)
    shard, at = number(SHARD), number(SOURCE) * cap + number(RANK)
    live = notes[:, LIVE : LIVE + 1] > 0.5
    column = lax.broadcasted_iota(jnp.int32, (rows, table.shape[1]), 1)
    for r in range(groups):
        spots = (column == at) & (shard == r) & live
        for t, value in enumerate(values):
            table[r * STEPS + t : r * STEPS + t + 1, :] = jnp.sum(jnp.where(spots, value, 0.0), 0, keepdims=True)


def place(groups, cap, before, notes, scale, own_row, peer_row, parts):
    return pl.pallas_call(
        functools.partial(place_kernel, groups, cap),
        out_shape=struct((groups * STEPS, -(-groups * cap // 128) * 128), jnp.float32),
        in_specs=[WHOLE] * (5 + len(parts)),
        out_specs=WHOLE,
        compiler_params=pltpu.CompilerParams(vmem_limit_bytes=12 << 20),
        cost_estimate=SMALL,
        name="place",
    )(before, notes, scale, own_row, peer_row, *parts)


def shards(
    tokens,
    parent_keys,
    parent_values,
    parent_blocks,
    child_parent,
    child_count,
    node_shard,
    attn_gain,
    w_query,
    w_key,
    w_value,
    w_out,
    reward_up,
    reward_out,
):
    groups, mp = lax.axis_size("dp"), lax.axis_size("mp")
    children, width = tokens.shape
    parents, prefix, kv_cols = parent_keys.shape
    capacity = max(2, 2 * children // groups)
    reward_cap = max(2, 3 * children // (2 * groups))
    slots = groups * capacity
    rows = min(slots, 3 * children // 2)
    hidden = reward_out.shape[1] // mp
    pairs = lambda count, k: [(i, i ^ k) for i in range(count)]
    swap = pairs(mp, 1)
    shift = lambda count, k: [(i, (i + k) % count) for i in range(count)]

    ups = [lax.all_gather(reward_up[0], "dp", axis=0)]

    blocks = dispatch(parents, child_count, child_parent, node_shard, tokens, reward_out, groups, capacity, hidden)
    blocks = [blocks[0]] + [lax.ppermute(blocks[k], "dp", pairs(groups, k)) for k in range(1, groups)]

    keys = parent_keys.reshape(parents * prefix, kv_cols)
    values = parent_values.reshape(parents * prefix, kv_cols)
    raw = (w_query, w_key, w_value, keys, values, w_out)
    gain = attn_gain.reshape(1, width)

    def run(offset, blocks, raw, ups, gain, child_parent, parent_blocks):
        row_own, notes, bias, scale, over = pack(
            offset, rows, hidden, prefix, parent_blocks, child_parent, blocks
        )
        weights = raw
        state = row_own.astype(jnp.float32)
        row_peer = lax.ppermute(row_own, "mp", swap)
        past_keys, past_values, rows_own, rows_peer, norms = [], [], [], [], []

        def products(first, last, ups, load):
            sums = score(mp, notes, ups, rows_own[first:last], rows_peer[first:last], load)
            return sums[:mp], [held(up) for up in sums[mp:]]

        send = lambda sums: [sums[0]] + [lax.ppermute(sums[k], "mp", pairs(mp, k)) for k in range(1, mp)]
        for step in range(STEPS):
            w_query, w_key, w_value, keys, values, w_out = weights
            part, attn, key_now, value_now, norm, *kept = expand(
                step, row_own, row_peer, gain, w_query, w_key, w_value, keys, values, bias, w_out,
                past_keys, past_values,
            )
            if step == 0:
                weights = [held(x) for x in kept]
            norms.append(norm)
            past_keys.append(key_now)
            past_values.append(value_now)
            from_peer = lax.ppermute(part, "mp", swap)
            chip = project_own(rows, attn, weights[-1]) + from_peer.astype(jnp.float32)
            sent = chip.astype(jnp.bfloat16)
            others = [lax.ppermute(sent, "mp", shift(mp, k)) for k in range(2, mp, 2)]
            if step + 1 == STEPS:
                _, ups = lax.optimization_barrier((sent, ups))
                before, ups = products(0, step, ups, True)
                others, before = lax.optimization_barrier((others, before))
            for other in others:
                chip = chip + other.astype(jnp.float32)
            state = state + chip
            row_own = state.astype(jnp.bfloat16)
            row_peer = lax.ppermute(row_own, "mp", swap)
            rows_own.append(row_own)
            rows_peer.append(row_peer)
        before = send(before)
        last, _ = products(step, STEPS, ups, False)
        last, over = lax.optimization_barrier((send(last), over[0, 0]))
        before = finish(notes, scale, norms[1:], before)
        return place(groups, reward_cap, before, notes, scale, row_own, row_peer, last), over

    operands = (blocks, raw, ups, gain, child_parent, parent_blocks)

    table, over = run(0, *operands)
    if rows < slots:
        table, operands = lax.optimization_barrier((table, operands))
        again = lambda table, operands: table + run(rows, *operands)[0]
        table = lax.cond(over > 0, again, lambda table, operands: table, table, operands)

    table = lax.all_to_all(table, "dp", split_axis=0, concat_axis=0, tiled=True)
    total = jnp.sum(table.reshape(groups, STEPS, -1), 0)[:, : groups * reward_cap]
    total = total + lax.ppermute(total, "mp", swap)
    result = total
    for k in range(2, mp, 2):
        result = result + lax.ppermute(total, "mp", shift(mp, k))
    return result


def solution(mesh):
    placed = (
        P("dp", None),
        P("dp", None, "mp"),
        P("dp", None, "mp"),
        P(),
        P(),
        P("dp"),
        P(),
        P(),
        P(None, "mp"),
        P(None, "mp"),
        P(None, "mp"),
        P("mp", None),
        P("dp", "mp", None),
        P("dp", None),
    )
    return jax.shard_map(
        shards, mesh=mesh, in_specs=placed, out_specs=P(None, "dp"), check_vma=False
    )
```

profile of v0, /device:TPU:0, one launch (start us, length us, event | category | flops | bytes accessed | tf_op | source)
XLA Modules:
  0.0 216.5 jit_solution(12489595393973341163)
XLA Ops:
  9.4 3.0 %collective-permute-start.31 = (bf16[8,3200]{1,0:T(8,128)(2,1)S(1)}, bf16[8,3200]{1,0:T(8,128)(2,1)S(1)}, u32[]{:S(2)}, u32[]{:S(2)}) collective-permute-start(bf16[8,3200]{1,0:T(8,128)(2,1)S(1)} %get-tuple-element.228), channel_id=1, source_target_pairs={{0,4},{4,0},{8,12},{12,8},{16,20},{20,16},{24,28},{28,24},{1,5},{5... | collective-permute-start | bytes 153608 | tf_op jit(solution)/shard_map/ppermute | solution.py:494
  12.4 1.6 collective-permute-start.32
  14.0 3.0 %collective-permute-start.34 = (bf16[8,3200]{1,0:T(8,128)(2,1)S(1)}, bf16[8,3200]{1,0:T(8,128)(2,1)S(1)}, u32[]{:S(2)}, u32[]{:S(2)}) collective-permute-start(bf16[8,3200]{1,0:T(8,128)(2,1)S(1)} %get-tuple-element.231), channel_id=1, source_target_pairs={{0,16},{4,20},{8,24},{12,28},{16,0},{20,4},{24,8},{28,12},{1,17},{... | collective-permute-start | bytes 153608 | tf_op jit(solution)/shard_map/ppermute | solution.py:494
  18.3 3.6 %collective-permute-start.36 = (bf16[8,3200]{1,0:T(8,128)(2,1)S(1)}, bf16[8,3200]{1,0:T(8,128)(2,1)S(1)}, u32[]{:S(2)}, u32[]{:S(2)}) collective-permute-start(bf16[8,3200]{1,0:T(8,128)(2,1)S(1)} %get-tuple-element.233), channel_id=1, source_target_pairs={{0,24},{4,28},{8,16},{12,20},{16,8},{20,12},{24,0},{28,4},{1,25},{... | collective-permute-start | bytes 153608 | tf_op jit(solution)/shard_map/ppermute | solution.py:494
  22.0 3.1 %collective-permute-done.35.rest_5_ = bf16[8,3200]{1,0:T(8,128)(2,1)S(1)} collective-permute-done((bf16[8,3200]{1,0:T(8,128)(2,1)S(1)}, bf16[8,3200]{1,0:T(8,128)(2,1)S(1)}, u32[]{:S(2)}, u32[]{:S(2)}) %collective-permute-start.35) | collective-permute-done | bytes 51232 | tf_op jit(solution)/shard_map/ppermute | solution.py:494
  25.1 4.5 %collective-permute-done.37.rest_7_ = bf16[8,3200]{1,0:T(8,128)(2,1)S(1)} collective-permute-done((bf16[8,3200]{1,0:T(8,128)(2,1)S(1)}, bf16[8,3200]{1,0:T(8,128)(2,1)S(1)}, u32[]{:S(2)}, u32[]{:S(2)}) %collective-permute-start.37) | collective-permute-done | bytes 51232 | tf_op jit(solution)/shard_map/ppermute | solution.py:494
  32.3 10.9 %expand.24 = (bf16[48,2560]{1,0:T(8,128)(2,1)S(1)}, bf16[64,768]{1,0:T(8,128)(2,1)S(1)}, bf16[48,256]{1,0:T(8,128)(2,1)S(1)}, bf16[48,256]{1,0:T(8,128)(2,1)S(1)...) custom-call(bf16[48,2560]{1,0:T(8,128)(2,1)S(1)} %get-tuple-element., ...), custom_call_target="tpu_custom_call" | custom-call | tf_op jit(solution)/shard_map/expand/pallas_call | solution.py:297
  44.9 1.6 collective-permute-start.40
  46.4 6.7 %collective-permute-done.40 = bf16[48,2560]{1,0:T(8,128)(2,1)S(1)} collective-permute-done((bf16[48,2560]{1,0:T(8,128)(2,1)S(1)}, bf16[48,2560]{1,0:T(8,128)(2,1)S(1)}, u32[]{:S(2)}, u32[]{:S(2)}) %collective-permute-start.40) | collective-permute-done | bytes 245792 | tf_op jit(solution)/shard_map/ppermute | solution.py:529
  54.8 5.4 %expand.25 = (bf16[48,2560]{1,0:T(8,128)(2,1)S(1)}, bf16[64,768]{1,0:T(8,128)(2,1)S(1)}, bf16[48,256]{1,0:T(8,128)(2,1)S(1)}, bf16[48,256]{1,0:T(8,128)(2,1)S(1)}, f32[48,128]{1,0:T(8,128)S(1)}) custom-call(bf16[48,2560]{1,0:T(8,128)(2,1)S(1)} %fusion.20.own.refs_1_, bf16[48,2560]{1,0:T(8,128)(2,1)S(1)} %collective-permute-done.41.peer.refs_8_, ...), custom_call_target="tpu_custom_call" | custom-call | tf_op jit(solution)/shard_map/expand/pallas_call | solution.py:297
  63.4 6.7 %collective-permute-done.43 = bf16[48,2560]{1,0:T(8,128)(2,1)S(1)} collective-permute-done((bf16[48,2560]{1,0:T(8,128)(2,1)S(1)}, bf16[48,2560]{1,0:T(8,128)(2,1)S(1)}, u32[]{:S(2)}, u32[]{:S(2)}) %collective-permute-start.43) | collective-permute-done | bytes 245792 | tf_op jit(solution)/shard_map/ppermute | solution.py:529
  71.9 5.4 %expand.26 = (bf16[48,2560]{1,0:T(8,128)(2,1)S(1)}, bf16[64,768]{1,0:T(8,128)(2,1)S(1)}, bf16[48,256]{1,0:T(8,128)(2,1)S(1)}, bf16[48,256]{1,0:T(8,128)(2,1)S(1)}, f32[48,128]{1,0:T(8,128)S(1)}) custom-call(bf16[48,2560]{1,0:T(8,128)(2,1)S(1)} %get-tuple-element.332.own.refs_2_, bf16[48,2560]{1,0:T(8,128)(2,1)S(1)} %collective-permute-done.44.peer.refs_9_, ...), custom_call_target="tpu_custom_call" | custom-call | tf_op jit(solution)/shard_map/expand/pallas_call | solution.py:297
  79.0 1.6 collective-permute-start.46
  80.5 6.7 %collective-permute-done.46 = bf16[48,2560]{1,0:T(8,128)(2,1)S(1)} collective-permute-done((bf16[48,2560]{1,0:T(8,128)(2,1)S(1)}, bf16[48,2560]{1,0:T(8,128)(2,1)S(1)}, u32[]{:S(2)}, u32[]{:S(2)}) %collective-permute-start.46) | collective-permute-done | bytes 245792 | tf_op jit(solution)/shard_map/ppermute | solution.py:529
  88.9 5.6 %expand.27 = (bf16[48,2560]{1,0:T(8,128)(2,1)S(1)}, bf16[64,768]{1,0:T(8,128)(2,1)S(1)}, bf16[48,256]{1,0:T(8,128)(2,1)S(1)}, bf16[48,256]{1,0:T(8,128)(2,1)S(1)}, f32[48,128]{1,0:T(8,128)S(1)}) custom-call(bf16[48,2560]{1,0:T(8,128)(2,1)S(1)} %fusion.21.own.refs_3_, bf16[48,2560]{1,0:T(8,128)(2,1)S(1)} %collective-permute-done.47.peer.refs_10_, ...), custom_call_target="tpu_custom_call" | custom-call | tf_op jit(solution)/shard_map/expand/pallas_call | solution.py:297
  96.1 1.6 collective-permute-start.49
  97.7 6.7 %collective-permute-done.49 = bf16[48,2560]{1,0:T(8,128)(2,1)S(1)} collective-permute-done((bf16[48,2560]{1,0:T(8,128)(2,1)S(1)}, bf16[48,2560]{1,0:T(8,128)(2,1)S(1)}, u32[]{:S(2)}, u32[]{:S(2)}) %collective-permute-start.49) | collective-permute-done | bytes 245792 | tf_op jit(solution)/shard_map/ppermute | solution.py:529
  106.2 5.4 %expand.28 = (bf16[48,2560]{1,0:T(8,128)(2,1)S(1)}, bf16[64,768]{1,0:T(8,128)(2,1)S(1)}, bf16[48,256]{1,0:T(8,128)(2,1)S(1)}, bf16[48,256]{1,0:T(8,128)(2,1)S(1)}, f32[48,128]{1,0:T(8,128)S(1)}) custom-call(bf16[48,2560]{1,0:T(8,128)(2,1)S(1)} %get-tuple-element.330.own.refs_4_, bf16[48,2560]{1,0:T(8,128)(2,1)S(1)} %collective-permute-done.50.peer.refs_11_, ...), custom_call_target="tpu_custom_call" | custom-call | tf_op jit(solution)/shard_map/expand/pallas_call | solution.py:297
  113.2 1.6 collective-permute-start.52
  114.8 6.7 %collective-permute-done.52 = bf16[48,2560]{1,0:T(8,128)(2,1)S(1)} collective-permute-done((bf16[48,2560]{1,0:T(8,128)(2,1)S(1)}, bf16[48,2560]{1,0:T(8,128)(2,1)S(1)}, u32[]{:S(2)}, u32[]{:S(2)}) %collective-permute-start.52) | collective-permute-done | bytes 245792 | tf_op jit(solution)/shard_map/ppermute | solution.py:529
  123.2 5.5 %expand.29 = (bf16[48,2560]{1,0:T(8,128)(2,1)S(1)}, bf16[64,768]{1,0:T(8,128)(2,1)S(1)}, bf16[48,256]{1,0:T(8,128)(2,1)S(1)}, bf16[48,256]{1,0:T(8,128)(2,1)S(1)}, f32[48,128]{1,0:T(8,128)S(1)}) custom-call(bf16[48,2560]{1,0:T(8,128)(2,1)S(1)} %fusion.22.own.refs_5_, bf16[48,2560]{1,0:T(8,128)(2,1)S(1)} %collective-permute-done.53.peer.refs_12_, ...), custom_call_target="tpu_custom_call" | custom-call | tf_op jit(solution)/shard_map/expand/pallas_call | solution.py:297
  130.3 1.6 collective-permute-start.55
  131.8 6.7 %collective-permute-done.55 = bf16[48,2560]{1,0:T(8,128)(2,1)S(1)} collective-permute-done((bf16[48,2560]{1,0:T(8,128)(2,1)S(1)}, bf16[48,2560]{1,0:T(8,128)(2,1)S(1)}, u32[]{:S(2)}, u32[]{:S(2)}) %collective-permute-start.55) | collective-permute-done | bytes 245792 | tf_op jit(solution)/shard_map/ppermute | solution.py:529
  140.3 5.7 %expand.30 = (bf16[48,2560]{1,0:T(8,128)(2,1)S(1)}, bf16[64,768]{1,0:T(8,128)(2,1)S(1)}, bf16[48,256]{1,0:T(8,128)(2,1)S(1)}, bf16[48,256]{1,0:T(8,128)(2,1)S(1)}, f32[48,128]{1,0:T(8,128)S(1)}) custom-call(bf16[48,2560]{1,0:T(8,128)(2,1)S(1)} %get-tuple-element.328.own.refs_6_, bf16[48,2560]{1,0:T(8,128)(2,1)S(1)} %collective-permute-done.56.peer.refs_13_, ...), custom_call_target="tpu_custom_call" | custom-call | tf_op jit(solution)/shard_map/expand/pallas_call | solution.py:297
  149.2 6.7 %collective-permute-done.58 = bf16[48,2560]{1,0:T(8,128)(2,1)S(1)} collective-permute-done((bf16[48,2560]{1,0:T(8,128)(2,1)S(1)}, bf16[48,2560]{1,0:T(8,128)(2,1)S(1)}, u32[]{:S(2)}, u32[]{:S(2)}) %collective-permute-start.58) | collective-permute-done | bytes 245792 | tf_op jit(solution)/shard_map/ppermute | solution.py:529
  157.6 5.8 %expand.31 = (bf16[48,2560]{1,0:T(8,128)(2,1)S(1)}, bf16[64,768]{1,0:T(8,128)(2,1)S(1)}, bf16[48,256]{1,0:T(8,128)(2,1)}, bf16[48,256]{1,0:T(8,128)(2,1)}, f32[48,128]{1,0:T(8,128)S(1)}) custom-call(bf16[48,2560]{1,0:T(8,128)(2,1)S(1)} %fusion.23.own.refs_7_, bf16[48,2560]{1,0:T(8,128)(2,1)S(1)} %collective-permute-done.59.peer.refs_14_, ...), custom_call_target="tpu_custom_call" | custom-call | tf_op jit(solution)/shard_map/expand/pallas_call | solution.py:297
  167.2 6.9 %score.6 = (bf16[336,128]{1,0:T(8,128)(2,1)S(1)}, bf16[336,128]{1,0:T(8,128)(2,1)S(1)}, bf16[336,128]{1,0:T(8,128)(2,1)S(1)}, bf16[336,128]{1,0:T(8,128)(2,1)S(1)}, bf16[8,1280,512]{2,1,0:T(8,128)(2,1)S(1)}) custom-call(f32[48,128]{1,0:T(8,128)S(1)} %get-tuple-element.235.notes, bf16[8,1280,512]{2,1,0:T(8,128)(2,1)} %all-gather.2.cloned.1.call-done.refs_0_, ...), custom_call_target="tpu_custom_call" | custom-call | tf_op jit(solution)/shard_map/score/pallas_call | solution.py:387
  176.5 2.0 collective-permute-start.67
  178.6 2.0 score.7
  180.7 2.0 collective-permute-start.64
  188.5 15.3 %all_to_all.9 = f32[8,8,128]{2,1,0:T(8,128)S(1)} all-to-all(f32[8,8,128]{2,1,0:T(8,128)S(1)} %bitcast.22), channel_id=1, replica_groups=mesh['dp'=8,'mp'=4] {'dp'}, dimensions={0} | all-to-all | bytes 65536 | tf_op jit(solution)/shard_map/all_to_all | solution.py:555
  205.4 3.1 %collective-permute-done.70 = f32[8,48]{1,0:T(8,128)S(1)} collective-permute-done((f32[8,48]{1,0:T(8,128)S(1)}, f32[8,48]{1,0:T(8,128)S(1)}, u32[]{:S(2)}, u32[]{:S(2)}) %collective-permute-start.70) | collective-permute-done | bytes 1568 | tf_op jit(solution)/shard_map/ppermute | solution.py:560
  (147 shorter events, 46.5 us)
Async XLA Ops:
  6.5 160.7 %all-gather.2.cloned.1.call-start = ((), (), s32[]{:S(2)}) async-start(), calls=%async_computation.1 | async-start | bytes 11796480 | tf_op jit(solution)/shard_map/all_gather | solution.py:491
  9.4 8.9 %collective-permute-start.31 = (bf16[8,3200]{1,0:T(8,128)(2,1)S(1)}, bf16[8,3200]{1,0:T(8,128)(2,1)S(1)}, u32[]{:S(2)}, u32[]{:S(2)}) collective-permute-start(bf16[8,3200]{1,0:T(8,128)(2,1)S(1)} %get-tuple-element.228), channel_id=1, source_target_pairs={{0,4},{4,0},{8,12},{12,8},{16,20},{20,16},{24,28},{28,24},{1,5},{5... | collective-permute-start | bytes 153608 | tf_op jit(solution)/shard_map/ppermute | solution.py:494
  12.4 9.5 %collective-permute-start.32 = (bf16[8,3200]{1,0:T(8,128)(2,1)S(1)}, bf16[8,3200]{1,0:T(8,128)(2,1)S(1)}, u32[]{:S(2)}, u32[]{:S(2)}) collective-permute-start(bf16[8,3200]{1,0:T(8,128)(2,1)S(1)} %get-tuple-element.229), channel_id=1, source_target_pairs={{0,8},{4,12},{8,0},{12,4},{16,24},{20,28},{24,16},{28,20},{1,9},{5... | collective-permute-start | bytes 153608 | tf_op jit(solution)/shard_map/ppermute | solution.py:494
  14.0 7.9 %collective-permute-start.33 = (bf16[8,3200]{1,0:T(8,128)(2,1)S(1)}, bf16[8,3200]{1,0:T(8,128)(2,1)S(1)}, u32[]{:S(2)}, u32[]{:S(2)}) collective-permute-start(bf16[8,3200]{1,0:T(8,128)(2,1)S(1)} %get-tuple-element.230), channel_id=1, source_target_pairs={{0,12},{4,8},{8,4},{12,0},{16,28},{20,24},{24,20},{28,16},{1,13},{... | collective-permute-start | bytes 153608 | tf_op jit(solution)/shard_map/ppermute | solution.py:494
  14.0 7.9 %collective-permute-start.34 = (bf16[8,3200]{1,0:T(8,128)(2,1)S(1)}, bf16[8,3200]{1,0:T(8,128)(2,1)S(1)}, u32[]{:S(2)}, u32[]{:S(2)}) collective-permute-start(bf16[8,3200]{1,0:T(8,128)(2,1)S(1)} %get-tuple-element.231), channel_id=1, source_target_pairs={{0,16},{4,20},{8,24},{12,28},{16,0},{20,4},{24,8},{28,12},{1,17},{... | collective-permute-start | bytes 153608 | tf_op jit(solution)/shard_map/ppermute | solution.py:494
  17.0 8.1 %collective-permute-start.35 = (bf16[8,3200]{1,0:T(8,128)(2,1)S(1)}, bf16[8,3200]{1,0:T(8,128)(2,1)S(1)}, u32[]{:S(2)}, u32[]{:S(2)}) collective-permute-start(bf16[8,3200]{1,0:T(8,128)(2,1)S(1)} %get-tuple-element.232), channel_id=1, source_target_pairs={{0,20},{4,16},{8,28},{12,24},{16,4},{20,0},{24,12},{28,8},{1,21},{... | collective-permute-start | bytes 153608 | tf_op jit(solution)/shard_map/ppermute | solution.py:494
  18.3 6.8 %collective-permute-start.36 = (bf16[8,3200]{1,0:T(8,128)(2,1)S(1)}, bf16[8,3200]{1,0:T(8,128)(2,1)S(1)}, u32[]{:S(2)}, u32[]{:S(2)}) collective-permute-start(bf16[8,3200]{1,0:T(8,128)(2,1)S(1)} %get-tuple-element.233), channel_id=1, source_target_pairs={{0,24},{4,28},{8,16},{12,20},{16,8},{20,12},{24,0},{28,4},{1,25},{... | collective-permute-start | bytes 153608 | tf_op jit(solution)/shard_map/ppermute | solution.py:494
  21.9 7.7 %collective-permute-start.37 = (bf16[8,3200]{1,0:T(8,128)(2,1)S(1)}, bf16[8,3200]{1,0:T(8,128)(2,1)S(1)}, u32[]{:S(2)}, u32[]{:S(2)}) collective-permute-start(bf16[8,3200]{1,0:T(8,128)(2,1)S(1)} %get-tuple-element.234), channel_id=1, source_target_pairs={{0,28},{4,24},{8,20},{12,16},{16,12},{20,8},{24,4},{28,0},{1,29},{... | collective-permute-start | bytes 153608 | tf_op jit(solution)/shard_map/ppermute | solution.py:494
  30.7 1.6 collective-permute-start.38
  43.2 1.6 collective-permute-start.39
  44.9 8.2 %collective-permute-start.40 = (bf16[48,2560]{1,0:T(8,128)(2,1)S(1)}, bf16[48,2560]{1,0:T(8,128)(2,1)S(1)}, u32[]{:S(2)}, u32[]{:S(2)}) collective-permute-start(bf16[48,2560]{1,0:T(8,128)(2,1)S(1)} %fusion.12), channel_id=1, source_target_pairs={{0,2},{1,3},{2,0},{3,1},{4,6},{5,7},{6,4},{7,5},{8,10},{9,11},{10,... | collective-permute-start | bytes 737288 | tf_op jit(solution)/shard_map/ppermute | solution.py:529
  53.2 1.6 collective-permute-start.41
  60.2 1.6 collective-permute-start.42
  61.9 8.2 %collective-permute-start.43 = (bf16[48,2560]{1,0:T(8,128)(2,1)S(1)}, bf16[48,2560]{1,0:T(8,128)(2,1)S(1)}, u32[]{:S(2)}, u32[]{:S(2)}) collective-permute-start(bf16[48,2560]{1,0:T(8,128)(2,1)S(1)} %fusion.13), channel_id=1, source_target_pairs={{0,2},{1,3},{2,0},{3,1},{4,6},{5,7},{6,4},{7,5},{8,10},{9,11},{10,... | collective-permute-start | bytes 737288 | tf_op jit(solution)/shard_map/ppermute | solution.py:529
  79.0 8.2 %collective-permute-start.46 = (bf16[48,2560]{1,0:T(8,128)(2,1)S(1)}, bf16[48,2560]{1,0:T(8,128)(2,1)S(1)}, u32[]{:S(2)}, u32[]{:S(2)}) collective-permute-start(bf16[48,2560]{1,0:T(8,128)(2,1)S(1)} %fusion.14), channel_id=1, source_target_pairs={{0,2},{1,3},{2,0},{3,1},{4,6},{5,7},{6,4},{7,5},{8,10},{9,11},{10,... | collective-permute-start | bytes 737288 | tf_op jit(solution)/shard_map/ppermute | solution.py:529
  94.5 1.6 collective-permute-start.48
  96.1 8.2 %collective-permute-start.49 = (bf16[48,2560]{1,0:T(8,128)(2,1)S(1)}, bf16[48,2560]{1,0:T(8,128)(2,1)S(1)}, u32[]{:S(2)}, u32[]{:S(2)}) collective-permute-start(bf16[48,2560]{1,0:T(8,128)(2,1)S(1)} %fusion.15), channel_id=1, source_target_pairs={{0,2},{1,3},{2,0},{3,1},{4,6},{5,7},{6,4},{7,5},{8,10},{9,11},{10,... | collective-permute-start | bytes 737288 | tf_op jit(solution)/shard_map/ppermute | solution.py:529
  104.6 1.6 collective-permute-start.50
  113.2 8.2 %collective-permute-start.52 = (bf16[48,2560]{1,0:T(8,128)(2,1)S(1)}, bf16[48,2560]{1,0:T(8,128)(2,1)S(1)}, u32[]{:S(2)}, u32[]{:S(2)}) collective-permute-start(bf16[48,2560]{1,0:T(8,128)(2,1)S(1)} %fusion.16), channel_id=1, source_target_pairs={{0,2},{1,3},{2,0},{3,1},{4,6},{5,7},{6,4},{7,5},{8,10},{9,11},{10,... | collective-permute-start | bytes 737288 | tf_op jit(solution)/shard_map/ppermute | solution.py:529
  130.3 8.2 %collective-permute-start.55 = (bf16[48,2560]{1,0:T(8,128)(2,1)S(1)}, bf16[48,2560]{1,0:T(8,128)(2,1)S(1)}, u32[]{:S(2)}, u32[]{:S(2)}) collective-permute-start(bf16[48,2560]{1,0:T(8,128)(2,1)S(1)} %fusion.17), channel_id=1, source_target_pairs={{0,2},{1,3},{2,0},{3,1},{4,6},{5,7},{6,4},{7,5},{8,10},{9,11},{10,... | collective-permute-start | bytes 737288 | tf_op jit(solution)/shard_map/ppermute | solution.py:529
  146.0 1.6 collective-permute-start.57
  147.6 8.2 %collective-permute-start.58 = (bf16[48,2560]{1,0:T(8,128)(2,1)S(1)}, bf16[48,2560]{1,0:T(8,128)(2,1)S(1)}, u32[]{:S(2)}, u32[]{:S(2)}) collective-permute-start(bf16[48,2560]{1,0:T(8,128)(2,1)S(1)} %fusion.18), channel_id=1, source_target_pairs={{0,2},{1,3},{2,0},{3,1},{4,6},{5,7},{6,4},{7,5},{8,10},{9,11},{10,... | collective-permute-start | bytes 737288 | tf_op jit(solution)/shard_map/ppermute | solution.py:529
  156.0 1.6 collective-permute-start.59
  165.7 8.5 %collective-permute-start.61 = (bf16[48,2560]{1,0:T(8,128)(2,1)}, bf16[48,2560]{1,0:T(8,128)(2,1)}, u32[]{:S(2)}, u32[]{:S(2)}) collective-permute-start(bf16[48,2560]{1,0:T(8,128)(2,1)} %fusion.19), channel_id=1, source_target_pairs={{0,2},{1,3},{2,0},{3,1},{4,6},{5,7},{6,4},{7,5},{8,10},{9,11},{10,... | collective-permute-start | bytes 737288 | tf_op jit(solution)/shard_map/ppermute | solution.py:529
  175.6 3.0 %collective-permute-start.62 = (bf16[48,2560]{1,0:T(8,128)(2,1)S(1)}, bf16[48,2560]{1,0:T(8,128)(2,1)S(1)}, u32[]{:S(2)}, u32[]{:S(2)}) collective-permute-start(bf16[48,2560]{1,0:T(8,128)(2,1)S(1)} %add_convert_fusion.1.refs_1_.own_row), channel_id=1, source_target_pairs={{0,1},{1,0},{2,3},{3,2},{4,5},{5,4},{6,7},{7,6},{8,9},{9,8},{10,11... | collective-permute-start | bytes 737288 | tf_op jit(solution)/shard_map/ppermute | solution.py:538
  176.4 6.3 %collective-permute-start.66 = (bf16[336,128]{1,0:T(8,128)(2,1)S(1)}, bf16[336,128]{1,0:T(8,128)(2,1)S(1)}, u32[]{:S(2)}, u32[]{:S(2)}) collective-permute-start(bf16[336,128]{1,0:T(8,128)(2,1)S(1)} %get-tuple-element.296), channel_id=1, source_target_pairs={{0,1},{1,0},{2,3},{3,2},{4,5},{5,4},{6,7},{7,6},{8,9},{9,8},{10,11... | collective-permute-start | bytes 258056 | tf_op jit(solution)/shard_map/ppermute | solution.py:514
  176.5 6.8 %collective-permute-start.67 = (bf16[336,128]{1,0:T(8,128)(2,1)S(1)}, bf16[336,128]{1,0:T(8,128)(2,1)S(1)}, u32[]{:S(2)}, u32[]{:S(2)}) collective-permute-start(bf16[336,128]{1,0:T(8,128)(2,1)S(1)} %get-tuple-element.297), channel_id=1, source_target_pairs={{0,2},{1,3},{2,0},{3,1},{4,6},{5,7},{6,4},{7,5},{8,10},{9,11},{10,... | collective-permute-start | bytes 258056 | tf_op jit(solution)/shard_map/ppermute | solution.py:514
  178.5 4.8 %collective-permute-start.68 = (bf16[336,128]{1,0:T(8,128)(2,1)S(1)}, bf16[336,128]{1,0:T(8,128)(2,1)S(1)}, u32[]{:S(2)}, u32[]{:S(2)}) collective-permute-start(bf16[336,128]{1,0:T(8,128)(2,1)S(1)} %get-tuple-element.298), channel_id=1, source_target_pairs={{0,3},{1,2},{2,1},{3,0},{4,7},{5,6},{6,5},{7,4},{8,11},{9,10},{10,... | collective-permute-start | bytes 258056 | tf_op jit(solution)/shard_map/ppermute | solution.py:514
  180.6 3.5 %collective-permute-start.63 = (bf16[48,128]{1,0:T(8,128)(2,1)S(1)}, bf16[48,128]{1,0:T(8,128)(2,1)S(1)}, u32[]{:S(2)}, u32[]{:S(2)}) collective-permute-start(bf16[48,128]{1,0:T(8,128)(2,1)S(1)} %get-tuple-element.282), channel_id=1, source_target_pairs={{0,1},{1,0},{2,3},{3,2},{4,5},{5,4},{6,7},{7,6},{8,9},{9,8},{10,11... | collective-permute-start | bytes 36872 | tf_op jit(solution)/shard_map/ppermute | solution.py:514
  180.7 3.7 %collective-permute-start.64 = (bf16[48,128]{1,0:T(8,128)(2,1)S(1)}, bf16[48,128]{1,0:T(8,128)(2,1)S(1)}, u32[]{:S(2)}, u32[]{:S(2)}) collective-permute-start(bf16[48,128]{1,0:T(8,128)(2,1)S(1)} %get-tuple-element.283), channel_id=1, source_target_pairs={{0,2},{1,3},{2,0},{3,1},{4,6},{5,7},{6,4},{7,5},{8,10},{9,11},{10,... | collective-permute-start | bytes 36872 | tf_op jit(solution)/shard_map/ppermute | solution.py:514
  182.7 3.2 %collective-permute-start.65 = (bf16[48,128]{1,0:T(8,128)(2,1)S(1)}, bf16[48,128]{1,0:T(8,128)(2,1)S(1)}, u32[]{:S(2)}, u32[]{:S(2)}) collective-permute-start(bf16[48,128]{1,0:T(8,128)(2,1)S(1)} %get-tuple-element.284), channel_id=1, source_target_pairs={{0,3},{1,2},{2,1},{3,0},{4,7},{5,6},{6,5},{7,4},{8,11},{9,10},{10,... | collective-permute-start | bytes 36872 | tf_op jit(solution)/shard_map/ppermute | solution.py:514
  204.9 3.6 %collective-permute-start.70 = (f32[8,48]{1,0:T(8,128)S(1)}, f32[8,48]{1,0:T(8,128)S(1)}, u32[]{:S(2)}, u32[]{:S(2)}) collective-permute-start(f32[8,48]{1,0:T(8,128)S(1)} %slice_add_fusion), channel_id=1, source_target_pairs={{0,2},{1,3},{2,0},{3,1},{4,6},{5,7},{6,4},{7,5},{8,10},{9,11},{10,... | collective-permute-start | bytes 4616 | tf_op jit(solution)/shard_map/ppermute | solution.py:560
  (35 other events, 216.6 us)
Sparse Core Ops, SparseCore 0:
  9.5 155.9 all-gather.1
where the time goes:
time: 221 us; the launch traced here: 216 us
  waiting for transfers between devices  73.7 us (33%)
  Pallas kernels  72.8 us (33%)
  starting transfers between devices  32.6 us (15%)
  between operations  15.8 us (7%)
  blocking collectives  15.3 us (7%)
  other arithmetic  4.21 us (2%)
    pallas_call x8, Pallas kernels, expand(): pl.pallas_call(functools.partial(step_kernel, step), out_shape=(struct((s...  49.6 us
    ppermute x8, waiting for transfers between devices, run(): others = [lax.ppermute(sent, 'mp', shift(mp, k)) for k in range(2, mp, 2)]  46.7 us
    all_to_all x1, blocking collectives, shards(): table = lax.all_to_all(table, 'dp', split_axis=0, concat_axis=0, tiled=True)  15.3 us
    ppermute x7, starting transfers between devices, shards(): lax.ppermute(blocks[k], 'dp', pairs(groups, k))  12.5 us
    ppermute x8, starting transfers between devices, run(): others = [lax.ppermute(sent, 'mp', shift(mp, k)) for k in range(2, mp, 2)]  12.4 us
    ppermute x9, waiting for transfers between devices, run(): row_peer = lax.ppermute(row_own, 'mp', swap)  12 us
    pallas_call x8, Pallas kernels, project_own(): pl.pallas_call(project_kernel, out_shape=struct((rows, w_out.shape[1] //...  10.3 us
    pallas_call x2, Pallas kernels, score(): pl.pallas_call(functools.partial(score_kernel, steps, load, cuts, mp), ou...  8.91 us
  transfers between devices with their start and end apart: 41, of which 29 were waited for; matrix products, arithmetic and copies ran while one was open for 1% of the time, Pallas kernels for 33%

commit v1 on v0

--- a/solution.py
+++ b/solution.py
@@ -191,6 +191,29 @@
     )(blocks_held, child_parent[None], *blocks)
 
 
+def load_kernel(*refs):
+    count = (len(refs) - 1) // 2
+    copies = [pltpu.make_async_copy(refs[i], refs[count + i], refs[-1].at[i]) for i in range(count)]
+    for copy in copies:
+        copy.start()
+    for copy in copies:
+        copy.wait()
+
+
+def load(*arrays):
+    count = len(arrays)
+    return pl.pallas_call(
+        load_kernel,
+        out_shape=tuple(VMEM(x.shape, x.dtype) for x in arrays),
+        in_specs=[FAR] * count,
+        out_specs=(WHOLE,) * count,
+        scratch_shapes=[pltpu.SemaphoreType.DMA((count,))],
+        compiler_params=pltpu.CompilerParams(vmem_limit_bytes=2 << 20),
+        cost_estimate=pl.CostEstimate(flops=0, bytes_accessed=24 << 20, transcendentals=0),
+        name="load",
+    )(*map(far, arrays))
+
+
 def project(attn, w_out, out, first):
     width = out.shape[1]
 
@@ -209,25 +232,7 @@
     slots = own.shape[0]
     q_cols, kv_cols = w_query.shape[1], w_key.shape[1]
     kv_heads = kv_cols // HD
-    ready = {}
-    if step == 0:
-        part, attn, key_now, value_now, norm, *kept, normed, query, sems = rest
-        moves = [(w_query, kept[0], at, min(at + COLUMNS, q_cols)) for at in range(0, q_cols, COLUMNS)]
-        moves += [(w, v, 0, w.shape[1]) for w, v in zip((w_key, w_value, keys, values, w_out), kept[1:])]
-        for i, (source, target, at, end) in enumerate(moves):
-            copy = pltpu.make_async_copy(source.at[:, at:end], target.at[:, at:end], sems.at[i])
-            copy.start()
-            ready[i] = copy
-        w_query, w_key, w_value, keys, values, w_out = kept
-    else:
-        part, attn, key_now, value_now, norm, normed, query = rest
-    arrivals = iter(ready.values())
-
-    def arrive():
-        for copy in arrivals:
-            copy.wait()
-            break
-
+    part, attn, key_now, value_now, norm, normed, query = rest
     core, _, _ = coordinates()
     first = core == 0
     low = jnp.where(first, own[...], peer[...]).astype(jnp.float32)
@@ -241,14 +246,9 @@
         normed[slots:, :] = jnp.zeros((normed.shape[0] - slots, D), jnp.bfloat16)
     for at in range(0, q_cols, COLUMNS):
         end = min(at + COLUMNS, q_cols)
-        arrive()
         query[:, at:end] = dot(normed[...], w_query[:, at:end])
-    arrive()
     query[:, q_cols : q_cols + kv_cols] = dot(normed[...], w_key[...])
-    arrive()
     query[:, q_cols + kv_cols :] = dot(normed[...], w_value[...])
-    arrive()
-    arrive()
     key_now[...] = query[:slots, q_cols : q_cols + kv_cols].astype(jnp.bfloat16)
     value_now[...] = query[:slots, q_cols + kv_cols :].astype(jnp.bfloat16)
     recent = slots * (step + 1)
@@ -278,7 +278,6 @@
             attn[:slots, at : at + HD] = result[g * slots : (g + 1) * slots]
     if attn.shape[0] > slots:
         attn[slots:, :] = jnp.zeros((attn.shape[0] - slots, q_cols), jnp.bfloat16)
-    arrive()
     project(attn, w_out, part, (1 - core) * half)
 
 
@@ -287,22 +286,15 @@
     kv_cols = w_key.shape[1]
     q_cols = w_query.shape[1]
     padded = -(-slots // ROWS) * ROWS
-    weights = (w_query, w_key, w_value, keys, values, w_out)
-    kept, sems = [], []
-    place = WHOLE
-    if step == 0:
-        kept = [VMEM(w.shape, w.dtype) for w in weights]
-        sems = [pltpu.SemaphoreType.DMA((-(-q_cols // COLUMNS) + 5,))]
-        place = pl.BlockSpec(memory_space=pl.ANY)
     return pl.pallas_call(
         functools.partial(step_kernel, step),
         out_shape=(
             struct((slots, half)), struct((padded, q_cols)), struct((slots, kv_cols)), struct((slots, kv_cols)),
-            struct((slots, 128), jnp.float32), *kept
+            struct((slots, 128), jnp.float32),
         ),
-        in_specs=[WHOLE] * 3 + [place] * 5 + [WHOLE, place] + [WHOLE] * (2 * step),
-        out_specs=[WHOLE] * (5 + len(kept)),
-        scratch_shapes=[VMEM((padded, D), jnp.bfloat16), VMEM((padded, q_cols + 2 * kv_cols), jnp.float32)] + sems,
+        in_specs=[WHOLE] * (10 + 2 * step),
+        out_specs=[WHOLE] * 5,
+        scratch_shapes=[VMEM((padded, D), jnp.bfloat16), VMEM((padded, q_cols + 2 * kv_cols), jnp.float32)],
         compiler_params=pltpu.CompilerParams(vmem_limit_bytes=16 << 20),
         cost_estimate=SMALL,
         name="expand",
@@ -491,18 +483,19 @@
     ups = [lax.all_gather(reward_up[0], "dp", axis=0)]
 
     blocks = dispatch(parents, child_count, child_parent, node_shard, tokens, reward_out, groups, capacity, hidden)
-    blocks = [blocks[0]] + [lax.ppermute(blocks[k], "dp", pairs(groups, k)) for k in range(1, groups)]
-
     keys = parent_keys.reshape(parents * prefix, kv_cols)
     values = parent_values.reshape(parents * prefix, kv_cols)
     raw = (w_query, w_key, w_value, keys, values, w_out)
+    blocks, raw = lax.optimization_barrier((blocks, raw))
+    blocks = [blocks[0]] + [lax.ppermute(blocks[k], "dp", pairs(groups, k)) for k in range(1, groups)]
+    blocks, weights = lax.optimization_barrier((blocks, load(*raw)))
     gain = attn_gain.reshape(1, width)
 
-    def run(offset, blocks, raw, ups, gain, child_parent, parent_blocks):
+    def run(offset, weights, blocks, ups, gain, child_parent, parent_blocks):
         row_own, notes, bias, scale, over = pack(
             offset, rows, hidden, prefix, parent_blocks, child_parent, blocks
         )
-        weights = raw
+        w_query, w_key, w_value, keys, values, w_out = [held(w) for w in weights]
         state = row_own.astype(jnp.float32)
         row_peer = lax.ppermute(row_own, "mp", swap)
         past_keys, past_values, rows_own, rows_peer, norms = [], [], [], [], []
@@ -513,18 +506,15 @@
 
         send = lambda sums: [sums[0]] + [lax.ppermute(sums[k], "mp", pairs(mp, k)) for k in range(1, mp)]
         for step in range(STEPS):
-            w_query, w_key, w_value, keys, values, w_out = weights
-            part, attn, key_now, value_now, norm, *kept = expand(
+            part, attn, key_now, value_now, norm = expand(
                 step, row_own, row_peer, gain, w_query, w_key, w_value, keys, values, bias, w_out,
                 past_keys, past_values,
             )
-            if step == 0:
-                weights = [held(x) for x in kept]
             norms.append(norm)
             past_keys.append(key_now)
             past_values.append(value_now)
             from_peer = lax.ppermute(part, "mp", swap)
-            chip = project_own(rows, attn, weights[-1]) + from_peer.astype(jnp.float32)
+            chip = project_own(rows, attn, w_out) + from_peer.astype(jnp.float32)
             sent = chip.astype(jnp.bfloat16)
             others = [lax.ppermute(sent, "mp", shift(mp, k)) for k in range(2, mp, 2)]
             if step + 1 == STEPS:
@@ -544,13 +534,13 @@
         before = finish(notes, scale, norms[1:], before)
         return place(groups, reward_cap, before, notes, scale, row_own, row_peer, last), over
 
-    operands = (blocks, raw, ups, gain, child_parent, parent_blocks)
-
-    table, over = run(0, *operands)
+    operands = (blocks, ups, gain, child_parent, parent_blocks)
+
+    table, over = run(0, weights, *operands)
     if rows < slots:
-        table, operands = lax.optimization_barrier((table, operands))
-        again = lambda table, operands: table + run(rows, *operands)[0]
-        table = lax.cond(over > 0, again, lambda table, operands: table, table, operands)
+        table, raw, operands = lax.optimization_barrier((table, raw, operands))
+        again = lambda table, raw, operands: table + run(rows, load(*raw), *operands)[0]
+        table = lax.cond(over > 0, again, lambda table, raw, operands: table, table, raw, operands)
 
     table = lax.all_to_all(table, "dp", split_axis=0, concat_axis=0, tiled=True)
     total = jnp.sum(table.reshape(groups, STEPS, -1), 0)[:, : groups * reward_cap]

time: 221 us -> 214 us (0.968)
  waiting for transfers between devices: 73.7 us -> 67.8 us
  blocking collectives: 15.3 us -> 11.2 us
  Pallas kernels: 72.8 us -> 76.1 us
    pallas_call x0 -> x1, Pallas kernels: none -> 7.94 us  [load(): pl.pallas_call(load_kernel, out_shape=tuple((VMEM(x.shape, x.dtype) for x...]
    ppermute x7, waiting for transfers between devices: 7.61 us -> 0.02 us  [shards(): lax.ppermute(blocks[k], 'dp', pairs(groups, k))]
    pallas_call x8, Pallas kernels: 49.6 us -> 45.1 us  [expand(): pl.pallas_call(functools.partial(step_kernel, step), out_shape=(struct((s...]
    all_to_all x1, blocking collectives: 15.3 us -> 11.2 us  [shards(): table = lax.all_to_all(table, 'dp', split_axis=0, concat_axis=0, tiled=True)]
    all_gather x1, waiting for transfers between devices: 0.01 us -> 3.2 us  [shards(): ups = [lax.all_gather(reward_up[0], 'dp', axis=0)]]
  transfers between devices with their start and end apart: 41 -> 41, of which waited for: 29 -> 28; matrix products, arithmetic and copies ran while one was open for 1% -> 1% of each run, Pallas kernels for 33% -> 36%
where the time goes in v1:
time: 214 us; the launch traced here: 210 us
  Pallas kernels  76.1 us (36%)
  waiting for transfers between devices  67.8 us (32%)
  starting transfers between devices  34.7 us (16%)
  between operations  15.5 us (7%)
  blocking collectives  11.2 us (5%)
  other arithmetic  2.36 us (1%)
    ppermute x8, waiting for transfers between devices, run(): others = [lax.ppermute(sent, 'mp', shift(mp, k)) for k in range(2, mp, 2)]  45.2 us
    pallas_call x8, Pallas kernels, expand(): pl.pallas_call(functools.partial(step_kernel, step), out_shape=(struct((s...  45.1 us
    ppermute x8, starting transfers between devices, run(): others = [lax.ppermute(sent, 'mp', shift(mp, k)) for k in range(2, mp, 2)]  14.2 us
    ppermute x7, starting transfers between devices, shards(): lax.ppermute(blocks[k], 'dp', pairs(groups, k))  12.5 us
    ppermute x9, waiting for transfers between devices, run(): row_peer = lax.ppermute(row_own, 'mp', swap)  12 us
    all_to_all x1, blocking collectives, shards(): table = lax.all_to_all(table, 'dp', split_axis=0, concat_axis=0, tiled=True)  11.2 us
    pallas_call x8, Pallas kernels, project_own(): pl.pallas_call(project_kernel, out_shape=struct((rows, w_out.shape[1] //...  10.3 us
    pallas_call x2, Pallas kernels, score(): pl.pallas_call(functools.partial(score_kernel, steps, load, cuts, mp), ou...  8.91 us
  transfers between devices with their start and end apart: 41, of which 28 were waited for; matrix products, arithmetic and copies ran while one was open for 1% of the time, Pallas kernels for 36%

profile of v1, /device:TPU:0, one launch (start us, length us, event | category | flops | bytes accessed | tf_op | source)
XLA Modules:
  0.0 209.7 jit_solution(14963877032873708514)
XLA Ops:
  9.4 3.0 %collective-permute-start.31 = (bf16[8,3200]{1,0:T(8,128)(2,1)S(1)}, bf16[8,3200]{1,0:T(8,128)(2,1)S(1)}, u32[]{:S(2)}, u32[]{:S(2)}) collective-permute-start(bf16[8,3200]{1,0:T(8,128)(2,1)S(1)} %get-tuple-element.264), channel_id=1, source_target_pairs={{0,4},{4,0},{8,12},{12,8},{16,20},{20,16},{24,28},{28,24},{1,5},{5... | collective-permute-start | bytes 153608 | tf_op jit(solution)/shard_map/ppermute | solution.py:490
  14.1 3.0 %collective-permute-start.34 = (bf16[8,3200]{1,0:T(8,128)(2,1)S(1)}, bf16[8,3200]{1,0:T(8,128)(2,1)S(1)}, u32[]{:S(2)}, u32[]{:S(2)}) collective-permute-start(bf16[8,3200]{1,0:T(8,128)(2,1)S(1)} %get-tuple-element.267), channel_id=1, source_target_pairs={{0,16},{4,20},{8,24},{12,28},{16,0},{20,4},{24,8},{28,12},{1,17},{... | collective-permute-start | bytes 153608 | tf_op jit(solution)/shard_map/ppermute | solution.py:490
  18.3 3.6 %collective-permute-start.36 = (bf16[8,3200]{1,0:T(8,128)(2,1)S(1)}, bf16[8,3200]{1,0:T(8,128)(2,1)S(1)}, u32[]{:S(2)}, u32[]{:S(2)}) collective-permute-start(bf16[8,3200]{1,0:T(8,128)(2,1)S(1)} %get-tuple-element.269), channel_id=1, source_target_pairs={{0,24},{4,28},{8,16},{12,20},{16,8},{20,12},{24,0},{28,4},{1,25},{... | collective-permute-start | bytes 153608 | tf_op jit(solution)/shard_map/ppermute | solution.py:490
  21.9 7.9 %load.3 = (bf16[5120,768]{1,0:T(8,128)(2,1)S(1)}, bf16[5120,256]{1,0:T(8,128)(2,1)S(1)}, bf16[5120,256]{1,0:T(8,128)(2,1)S(1)}, bf16[2048,256]{1,0:T(8,128)(2,1)...) custom-call(bf16[5120,768]{1,0:T(8,128)(2,1)} %refs_0_, bf16[5120,256]{1,0:T(8,128)(2,1)} %refs_1_, ...), custom_call_target="tpu_custom_call" | custom-call | bytes 25165824 | tf_op jit(solution)/shard_map/load/pallas_call | solution.py:205
  32.5 6.0 %expand.24 = (bf16[48,2560]{1,0:T(8,128)(2,1)S(1)}, bf16[64,768]{1,0:T(8,128)(2,1)S(1)}, bf16[48,256]{1,0:T(8,128)(2,1)S(1)}, bf16[48,256]{1,0:T(8,128)(2,1)S(1)}, f32[48,128]{1,0:T(8,128)}) custom-call(bf16[48,2560]{1,0:T(8,128)(2,1)S(1)} %get-tuple-element.292.own, bf16[48,2560]{1,0:T(8,128)(2,1)S(1)} %collective-permute-done.38.peer, ...), custom_call_target="tpu_custom_call" | custom-call | tf_op jit(solution)/shard_map/expand/pallas_call | solution.py:289
  40.1 1.8 collective-permute-start.40
  41.9 6.5 %collective-permute-done.40 = bf16[48,2560]{1,0:T(8,128)(2,1)S(1)} collective-permute-done((bf16[48,2560]{1,0:T(8,128)(2,1)S(1)}, bf16[48,2560]{1,0:T(8,128)(2,1)S(1)}, u32[]{:S(2)}, u32[]{:S(2)}) %collective-permute-start.40) | collective-permute-done | bytes 245792 | tf_op jit(solution)/shard_map/ppermute | solution.py:519
  50.1 5.4 %expand.25 = (bf16[48,2560]{1,0:T(8,128)(2,1)S(1)}, bf16[64,768]{1,0:T(8,128)(2,1)S(1)}, bf16[48,256]{1,0:T(8,128)(2,1)S(1)}, bf16[48,256]{1,0:T(8,128)(2,1)S(1)}, f32[48,128]{1,0:T(8,128)S(1)}) custom-call(bf16[48,2560]{1,0:T(8,128)(2,1)S(1)} %fusion.20.own.refs_1_, bf16[48,2560]{1,0:T(8,128)(2,1)S(1)} %collective-permute-done.41.peer.refs_8_, ...), custom_call_target="tpu_custom_call" | custom-call | tf_op jit(solution)/shard_map/expand/pallas_call | solution.py:289
  57.1 1.8 collective-permute-start.43
  58.9 6.5 %collective-permute-done.43 = bf16[48,2560]{1,0:T(8,128)(2,1)S(1)} collective-permute-done((bf16[48,2560]{1,0:T(8,128)(2,1)S(1)}, bf16[48,2560]{1,0:T(8,128)(2,1)S(1)}, u32[]{:S(2)}, u32[]{:S(2)}) %collective-permute-start.43) | collective-permute-done | bytes 245792 | tf_op jit(solution)/shard_map/ppermute | solution.py:519
  67.2 5.4 %expand.26 = (bf16[48,2560]{1,0:T(8,128)(2,1)S(1)}, bf16[64,768]{1,0:T(8,128)(2,1)S(1)}, bf16[48,256]{1,0:T(8,128)(2,1)S(1)}, bf16[48,256]{1,0:T(8,128)(2,1)S(1)}, f32[48,128]{1,0:T(8,128)S(1)}) custom-call(bf16[48,2560]{1,0:T(8,128)(2,1)S(1)} %get-tuple-element.388.own.refs_2_, bf16[48,2560]{1,0:T(8,128)(2,1)S(1)} %collective-permute-done.44.peer.refs_9_, ...), custom_call_target="tpu_custom_call" | custom-call | tf_op jit(solution)/shard_map/expand/pallas_call | solution.py:289
  74.2 1.8 collective-permute-start.46
  76.0 6.5 %collective-permute-done.46 = bf16[48,2560]{1,0:T(8,128)(2,1)S(1)} collective-permute-done((bf16[48,2560]{1,0:T(8,128)(2,1)S(1)}, bf16[48,2560]{1,0:T(8,128)(2,1)S(1)}, u32[]{:S(2)}, u32[]{:S(2)}) %collective-permute-start.46) | collective-permute-done | bytes 245792 | tf_op jit(solution)/shard_map/ppermute | solution.py:519
  84.2 5.9 %expand.27 = (bf16[48,2560]{1,0:T(8,128)(2,1)S(1)}, bf16[64,768]{1,0:T(8,128)(2,1)S(1)}, bf16[48,256]{1,0:T(8,128)(2,1)S(1)}, bf16[48,256]{1,0:T(8,128)(2,1)S(1)}, f32[48,128]{1,0:T(8,128)S(1)}) custom-call(bf16[48,2560]{1,0:T(8,128)(2,1)S(1)} %fusion.21.own.refs_3_, bf16[48,2560]{1,0:T(8,128)(2,1)S(1)} %collective-permute-done.47.peer.refs_10_, ...), custom_call_target="tpu_custom_call" | custom-call | tf_op jit(solution)/shard_map/expand/pallas_call | solution.py:289
  91.7 1.8 collective-permute-start.49
  93.5 6.5 %collective-permute-done.49 = bf16[48,2560]{1,0:T(8,128)(2,1)S(1)} collective-permute-done((bf16[48,2560]{1,0:T(8,128)(2,1)S(1)}, bf16[48,2560]{1,0:T(8,128)(2,1)S(1)}, u32[]{:S(2)}, u32[]{:S(2)}) %collective-permute-start.49) | collective-permute-done | bytes 245792 | tf_op jit(solution)/shard_map/ppermute | solution.py:519
  101.8 5.4 %expand.28 = (bf16[48,2560]{1,0:T(8,128)(2,1)S(1)}, bf16[64,768]{1,0:T(8,128)(2,1)S(1)}, bf16[48,256]{1,0:T(8,128)(2,1)S(1)}, bf16[48,256]{1,0:T(8,128)(2,1)S(1)}, f32[48,128]{1,0:T(8,128)S(1)}) custom-call(bf16[48,2560]{1,0:T(8,128)(2,1)S(1)} %get-tuple-element.386.own.refs_4_, bf16[48,2560]{1,0:T(8,128)(2,1)S(1)} %collective-permute-done.50.peer.refs_11_, ...), custom_call_target="tpu_custom_call" | custom-call | tf_op jit(solution)/shard_map/expand/pallas_call | solution.py:289
  108.8 1.8 collective-permute-start.52
  110.6 6.5 %collective-permute-done.52 = bf16[48,2560]{1,0:T(8,128)(2,1)S(1)} collective-permute-done((bf16[48,2560]{1,0:T(8,128)(2,1)S(1)}, bf16[48,2560]{1,0:T(8,128)(2,1)S(1)}, u32[]{:S(2)}, u32[]{:S(2)}) %collective-permute-start.52) | collective-permute-done | bytes 245792 | tf_op jit(solution)/shard_map/ppermute | solution.py:519
  118.8 5.5 %expand.29 = (bf16[48,2560]{1,0:T(8,128)(2,1)S(1)}, bf16[64,768]{1,0:T(8,128)(2,1)S(1)}, bf16[48,256]{1,0:T(8,128)(2,1)S(1)}, bf16[48,256]{1,0:T(8,128)(2,1)S(1)}, f32[48,128]{1,0:T(8,128)S(1)}) custom-call(bf16[48,2560]{1,0:T(8,128)(2,1)S(1)} %fusion.22.own.refs_5_, bf16[48,2560]{1,0:T(8,128)(2,1)S(1)} %collective-permute-done.53.peer.refs_12_, ...), custom_call_target="tpu_custom_call" | custom-call | tf_op jit(solution)/shard_map/expand/pallas_call | solution.py:289
  125.9 1.8 collective-permute-start.55
  127.7 6.5 %collective-permute-done.55 = bf16[48,2560]{1,0:T(8,128)(2,1)S(1)} collective-permute-done((bf16[48,2560]{1,0:T(8,128)(2,1)S(1)}, bf16[48,2560]{1,0:T(8,128)(2,1)S(1)}, u32[]{:S(2)}, u32[]{:S(2)}) %collective-permute-start.55) | collective-permute-done | bytes 245792 | tf_op jit(solution)/shard_map/ppermute | solution.py:519
  135.9 5.6 %expand.30 = (bf16[48,2560]{1,0:T(8,128)(2,1)S(1)}, bf16[64,768]{1,0:T(8,128)(2,1)S(1)}, bf16[48,256]{1,0:T(8,128)(2,1)S(1)}, bf16[48,256]{1,0:T(8,128)(2,1)S(1)}, f32[48,128]{1,0:T(8,128)S(1)}) custom-call(bf16[48,2560]{1,0:T(8,128)(2,1)S(1)} %get-tuple-element.384.own.refs_6_, bf16[48,2560]{1,0:T(8,128)(2,1)S(1)} %collective-permute-done.56.peer.refs_13_, ...), custom_call_target="tpu_custom_call" | custom-call | tf_op jit(solution)/shard_map/expand/pallas_call | solution.py:289
  145.0 6.5 %collective-permute-done.58 = bf16[48,2560]{1,0:T(8,128)(2,1)S(1)} collective-permute-done((bf16[48,2560]{1,0:T(8,128)(2,1)S(1)}, bf16[48,2560]{1,0:T(8,128)(2,1)S(1)}, u32[]{:S(2)}, u32[]{:S(2)}) %collective-permute-start.58) | collective-permute-done | bytes 245792 | tf_op jit(solution)/shard_map/ppermute | solution.py:519
  153.2 5.8 %expand.31 = (bf16[48,2560]{1,0:T(8,128)(2,1)S(1)}, bf16[64,768]{1,0:T(8,128)(2,1)S(1)}, bf16[48,256]{1,0:T(8,128)(2,1)}, bf16[48,256]{1,0:T(8,128)(2,1)}, f32[48,128]{1,0:T(8,128)S(1)}) custom-call(bf16[48,2560]{1,0:T(8,128)(2,1)S(1)} %fusion.23.own.refs_7_, bf16[48,2560]{1,0:T(8,128)(2,1)S(1)} %collective-permute-done.59.peer.refs_14_, ...), custom_call_target="tpu_custom_call" | custom-call | tf_op jit(solution)/shard_map/expand/pallas_call | solution.py:289
  162.4 3.2 %all-gather.2.cloned.1.call-done.refs_0_ = bf16[8,1280,512]{2,1,0:T(8,128)(2,1)} async-done(((bf16[1,1280,512]{2,1,0:T(8,128)(2,1)}), bf16[8,1280,512]{2,1,0:T(8,128)(2,1)}) %all-gather.2.cloned.1.call-update) | async-done | bytes 10485776 | tf_op jit(solution)/shard_map/all_gather | solution.py:483
  165.6 6.9 %score.6 = (bf16[336,128]{1,0:T(8,128)(2,1)S(1)}, bf16[336,128]{1,0:T(8,128)(2,1)S(1)}, bf16[336,128]{1,0:T(8,128)(2,1)S(1)}, bf16[336,128]{1,0:T(8,128)(2,1)S(1)}, bf16[8,1280,512]{2,1,0:T(8,128)(2,1)S(1)}) custom-call(f32[48,128]{1,0:T(8,128)S(1)} %get-tuple-element.291.notes, bf16[8,1280,512]{2,1,0:T(8,128)(2,1)} %all-gather.2.cloned.1.call-done.refs_0_, ...), custom_call_target="tpu_custom_call" | custom-call | tf_op jit(solution)/shard_map/score/pallas_call | solution.py:379
  173.3 2.7 %collective-permute-start.67 = (bf16[336,128]{1,0:T(8,128)(2,1)S(1)}, bf16[336,128]{1,0:T(8,128)(2,1)S(1)}, u32[]{:S(2)}, u32[]{:S(2)}) collective-permute-start(bf16[336,128]{1,0:T(8,128)(2,1)S(1)} %get-tuple-element.353), channel_id=1, source_target_pairs={{0,2},{1,3},{2,0},{3,1},{4,6},{5,7},{6,4},{7,5},{8,10},{9,11},{10,... | collective-permute-start | bytes 258056 | tf_op jit(solution)/shard_map/ppermute | solution.py:507
  176.0 2.0 score.7
  178.2 2.0 collective-permute-start.64
  186.0 11.2 %all_to_all.9 = f32[8,8,128]{2,1,0:T(8,128)S(1)} all-to-all(f32[8,8,128]{2,1,0:T(8,128)S(1)} %bitcast.22), channel_id=1, replica_groups=mesh['dp'=8,'mp'=4] {'dp'}, dimensions={0} | all-to-all | bytes 65536 | tf_op jit(solution)/shard_map/all_to_all | solution.py:545
  198.9 3.1 %collective-permute-done.70 = f32[8,48]{1,0:T(8,128)S(1)} collective-permute-done((f32[8,48]{1,0:T(8,128)S(1)}, f32[8,48]{1,0:T(8,128)S(1)}, u32[]{:S(2)}, u32[]{:S(2)}) %collective-permute-start.70) | collective-permute-done | bytes 1568 | tf_op jit(solution)/shard_map/ppermute | solution.py:550
  (130 shorter events, 44.7 us)
Async XLA Ops:
  6.5 159.0 %all-gather.2.cloned.1.call-start = ((), (), s32[]{:S(2)}) async-start(), calls=%async_computation.1 | async-start | bytes 11796480 | tf_op jit(solution)/shard_map/all_gather | solution.py:483
  9.4 8.9 %collective-permute-start.31 = (bf16[8,3200]{1,0:T(8,128)(2,1)S(1)}, bf16[8,3200]{1,0:T(8,128)(2,1)S(1)}, u32[]{:S(2)}, u32[]{:S(2)}) collective-permute-start(bf16[8,3200]{1,0:T(8,128)(2,1)S(1)} %get-tuple-element.264), channel_id=1, source_target_pairs={{0,4},{4,0},{8,12},{12,8},{16,20},{20,16},{24,28},{28,24},{1,5},{5... | collective-permute-start | bytes 153608 | tf_op jit(solution)/shard_map/ppermute | solution.py:490
  12.5 9.5 %collective-permute-start.32 = (bf16[8,3200]{1,0:T(8,128)(2,1)S(1)}, bf16[8,3200]{1,0:T(8,128)(2,1)S(1)}, u32[]{:S(2)}, u32[]{:S(2)}) collective-permute-start(bf16[8,3200]{1,0:T(8,128)(2,1)S(1)} %get-tuple-element.265), channel_id=1, source_target_pairs={{0,8},{4,12},{8,0},{12,4},{16,24},{20,28},{24,16},{28,20},{1,9},{5... | collective-permute-start | bytes 153608 | tf_op jit(solution)/shard_map/ppermute | solution.py:490
  14.0 15.9 %collective-permute-start.33 = (bf16[8,3200]{1,0:T(8,128)(2,1)S(1)}, bf16[8,3200]{1,0:T(8,128)(2,1)S(1)}, u32[]{:S(2)}, u32[]{:S(2)}) collective-permute-start(bf16[8,3200]{1,0:T(8,128)(2,1)S(1)} %get-tuple-element.266), channel_id=1, source_target_pairs={{0,12},{4,8},{8,4},{12,0},{16,28},{20,24},{24,20},{28,16},{1,13},{... | collective-permute-start | bytes 153608 | tf_op jit(solution)/shard_map/ppermute | solution.py:490
  14.1 15.9 %collective-permute-start.34 = (bf16[8,3200]{1,0:T(8,128)(2,1)S(1)}, bf16[8,3200]{1,0:T(8,128)(2,1)S(1)}, u32[]{:S(2)}, u32[]{:S(2)}) collective-permute-start(bf16[8,3200]{1,0:T(8,128)(2,1)S(1)} %get-tuple-element.267), channel_id=1, source_target_pairs={{0,16},{4,20},{8,24},{12,28},{16,0},{20,4},{24,8},{28,12},{1,17},{... | collective-permute-start | bytes 153608 | tf_op jit(solution)/shard_map/ppermute | solution.py:490
  17.0 12.9 %collective-permute-start.35 = (bf16[8,3200]{1,0:T(8,128)(2,1)S(1)}, bf16[8,3200]{1,0:T(8,128)(2,1)S(1)}, u32[]{:S(2)}, u32[]{:S(2)}) collective-permute-start(bf16[8,3200]{1,0:T(8,128)(2,1)S(1)} %get-tuple-element.268), channel_id=1, source_target_pairs={{0,20},{4,16},{8,28},{12,24},{16,4},{20,0},{24,12},{28,8},{1,21},{... | collective-permute-start | bytes 153608 | tf_op jit(solution)/shard_map/ppermute | solution.py:490
  18.3 11.6 %collective-permute-start.36 = (bf16[8,3200]{1,0:T(8,128)(2,1)S(1)}, bf16[8,3200]{1,0:T(8,128)(2,1)S(1)}, u32[]{:S(2)}, u32[]{:S(2)}) collective-permute-start(bf16[8,3200]{1,0:T(8,128)(2,1)S(1)} %get-tuple-element.269), channel_id=1, source_target_pairs={{0,24},{4,28},{8,16},{12,20},{16,8},{20,12},{24,0},{28,4},{1,25},{... | collective-permute-start | bytes 153608 | tf_op jit(solution)/shard_map/ppermute | solution.py:490
  21.9 8.0 %collective-permute-start.37 = (bf16[8,3200]{1,0:T(8,128)(2,1)S(1)}, bf16[8,3200]{1,0:T(8,128)(2,1)S(1)}, u32[]{:S(2)}, u32[]{:S(2)}) collective-permute-start(bf16[8,3200]{1,0:T(8,128)(2,1)S(1)} %get-tuple-element.270), channel_id=1, source_target_pairs={{0,28},{4,24},{8,20},{12,16},{16,12},{20,8},{24,4},{28,0},{1,29},{... | collective-permute-start | bytes 153608 | tf_op jit(solution)/shard_map/ppermute | solution.py:490
  30.9 1.6 collective-permute-start.38
  40.1 8.2 %collective-permute-start.40 = (bf16[48,2560]{1,0:T(8,128)(2,1)S(1)}, bf16[48,2560]{1,0:T(8,128)(2,1)S(1)}, u32[]{:S(2)}, u32[]{:S(2)}) collective-permute-start(bf16[48,2560]{1,0:T(8,128)(2,1)S(1)} %fusion.12), channel_id=1, source_target_pairs={{0,2},{1,3},{2,0},{3,1},{4,6},{5,7},{6,4},{7,5},{8,10},{9,11},{10,... | collective-permute-start | bytes 737288 | tf_op jit(solution)/shard_map/ppermute | solution.py:519
  48.5 1.6 collective-permute-start.41
  55.5 1.6 collective-permute-start.42
  57.1 8.2 %collective-permute-start.43 = (bf16[48,2560]{1,0:T(8,128)(2,1)S(1)}, bf16[48,2560]{1,0:T(8,128)(2,1)S(1)}, u32[]{:S(2)}, u32[]{:S(2)}) collective-permute-start(bf16[48,2560]{1,0:T(8,128)(2,1)S(1)} %fusion.13), channel_id=1, source_target_pairs={{0,2},{1,3},{2,0},{3,1},{4,6},{5,7},{6,4},{7,5},{8,10},{9,11},{10,... | collective-permute-start | bytes 737288 | tf_op jit(solution)/shard_map/ppermute | solution.py:519
  65.6 1.6 collective-permute-start.44
  72.6 1.6 collective-permute-start.45
  74.2 8.2 %collective-permute-start.46 = (bf16[48,2560]{1,0:T(8,128)(2,1)S(1)}, bf16[48,2560]{1,0:T(8,128)(2,1)S(1)}, u32[]{:S(2)}, u32[]{:S(2)}) collective-permute-start(bf16[48,2560]{1,0:T(8,128)(2,1)S(1)} %fusion.14), channel_id=1, source_target_pairs={{0,2},{1,3},{2,0},{3,1},{4,6},{5,7},{6,4},{7,5},{8,10},{9,11},{10,... | collective-permute-start | bytes 737288 | tf_op jit(solution)/shard_map/ppermute | solution.py:519
  82.6 1.6 collective-permute-start.47
  90.1 1.6 collective-permute-start.48
  91.7 8.2 %collective-permute-start.49 = (bf16[48,2560]{1,0:T(8,128)(2,1)S(1)}, bf16[48,2560]{1,0:T(8,128)(2,1)S(1)}, u32[]{:S(2)}, u32[]{:S(2)}) collective-permute-start(bf16[48,2560]{1,0:T(8,128)(2,1)S(1)} %fusion.15), channel_id=1, source_target_pairs={{0,2},{1,3},{2,0},{3,1},{4,6},{5,7},{6,4},{7,5},{8,10},{9,11},{10,... | collective-permute-start | bytes 737288 | tf_op jit(solution)/shard_map/ppermute | solution.py:519
  100.2 1.6 collective-permute-start.50
  108.8 8.2 %collective-permute-start.52 = (bf16[48,2560]{1,0:T(8,128)(2,1)S(1)}, bf16[48,2560]{1,0:T(8,128)(2,1)S(1)}, u32[]{:S(2)}, u32[]{:S(2)}) collective-permute-start(bf16[48,2560]{1,0:T(8,128)(2,1)S(1)} %fusion.16), channel_id=1, source_target_pairs={{0,2},{1,3},{2,0},{3,1},{4,6},{5,7},{6,4},{7,5},{8,10},{9,11},{10,... | collective-permute-start | bytes 737288 | tf_op jit(solution)/shard_map/ppermute | solution.py:519
  125.9 8.2 %collective-permute-start.55 = (bf16[48,2560]{1,0:T(8,128)(2,1)S(1)}, bf16[48,2560]{1,0:T(8,128)(2,1)S(1)}, u32[]{:S(2)}, u32[]{:S(2)}) collective-permute-start(bf16[48,2560]{1,0:T(8,128)(2,1)S(1)} %fusion.17), channel_id=1, source_target_pairs={{0,2},{1,3},{2,0},{3,1},{4,6},{5,7},{6,4},{7,5},{8,10},{9,11},{10,... | collective-permute-start | bytes 737288 | tf_op jit(solution)/shard_map/ppermute | solution.py:519
  143.2 8.2 %collective-permute-start.58 = (bf16[48,2560]{1,0:T(8,128)(2,1)S(1)}, bf16[48,2560]{1,0:T(8,128)(2,1)S(1)}, u32[]{:S(2)}, u32[]{:S(2)}) collective-permute-start(bf16[48,2560]{1,0:T(8,128)(2,1)S(1)} %fusion.18), channel_id=1, source_target_pairs={{0,2},{1,3},{2,0},{3,1},{4,6},{5,7},{6,4},{7,5},{8,10},{9,11},{10,... | collective-permute-start | bytes 737288 | tf_op jit(solution)/shard_map/ppermute | solution.py:519
  160.6 11.9 %collective-permute-start.61 = (bf16[48,2560]{1,0:T(8,128)(2,1)S(1)}, bf16[48,2560]{1,0:T(8,128)(2,1)S(1)}, u32[]{:S(2)}, u32[]{:S(2)}) collective-permute-start(bf16[48,2560]{1,0:T(8,128)(2,1)S(1)} %fusion.19), channel_id=1, source_target_pairs={{0,2},{1,3},{2,0},{3,1},{4,6},{5,7},{6,4},{7,5},{8,10},{9,11},{10,... | collective-permute-start | bytes 737288 | tf_op jit(solution)/shard_map/ppermute | solution.py:519
  172.7 3.3 %collective-permute-start.62 = (bf16[48,2560]{1,0:T(8,128)(2,1)S(1)}, bf16[48,2560]{1,0:T(8,128)(2,1)S(1)}, u32[]{:S(2)}, u32[]{:S(2)}) collective-permute-start(bf16[48,2560]{1,0:T(8,128)(2,1)S(1)} %add_convert_fusion.1.refs_1_.own_row), channel_id=1, source_target_pairs={{0,1},{1,0},{2,3},{3,2},{4,5},{5,4},{6,7},{7,6},{8,9},{9,8},{10,11... | collective-permute-start | bytes 737288 | tf_op jit(solution)/shard_map/ppermute | solution.py:528
  172.9 7.3 %collective-permute-start.66 = (bf16[336,128]{1,0:T(8,128)(2,1)S(1)}, bf16[336,128]{1,0:T(8,128)(2,1)S(1)}, u32[]{:S(2)}, u32[]{:S(2)}) collective-permute-start(bf16[336,128]{1,0:T(8,128)(2,1)S(1)} %get-tuple-element.352), channel_id=1, source_target_pairs={{0,1},{1,0},{2,3},{3,2},{4,5},{5,4},{6,7},{7,6},{8,9},{9,8},{10,11... | collective-permute-start | bytes 258056 | tf_op jit(solution)/shard_map/ppermute | solution.py:507
  173.3 7.4 %collective-permute-start.67 = (bf16[336,128]{1,0:T(8,128)(2,1)S(1)}, bf16[336,128]{1,0:T(8,128)(2,1)S(1)}, u32[]{:S(2)}, u32[]{:S(2)}) collective-permute-start(bf16[336,128]{1,0:T(8,128)(2,1)S(1)} %get-tuple-element.353), channel_id=1, source_target_pairs={{0,2},{1,3},{2,0},{3,1},{4,6},{5,7},{6,4},{7,5},{8,10},{9,11},{10,... | collective-permute-start | bytes 258056 | tf_op jit(solution)/shard_map/ppermute | solution.py:507
  176.0 4.8 %collective-permute-start.68 = (bf16[336,128]{1,0:T(8,128)(2,1)S(1)}, bf16[336,128]{1,0:T(8,128)(2,1)S(1)}, u32[]{:S(2)}, u32[]{:S(2)}) collective-permute-start(bf16[336,128]{1,0:T(8,128)(2,1)S(1)} %get-tuple-element.354), channel_id=1, source_target_pairs={{0,3},{1,2},{2,1},{3,0},{4,7},{5,6},{6,5},{7,4},{8,11},{9,10},{10,... | collective-permute-start | bytes 258056 | tf_op jit(solution)/shard_map/ppermute | solution.py:507
  178.1 3.5 %collective-permute-start.63 = (bf16[48,128]{1,0:T(8,128)(2,1)S(1)}, bf16[48,128]{1,0:T(8,128)(2,1)S(1)}, u32[]{:S(2)}, u32[]{:S(2)}) collective-permute-start(bf16[48,128]{1,0:T(8,128)(2,1)S(1)} %get-tuple-element.338), channel_id=1, source_target_pairs={{0,1},{1,0},{2,3},{3,2},{4,5},{5,4},{6,7},{7,6},{8,9},{9,8},{10,11... | collective-permute-start | bytes 36872 | tf_op jit(solution)/shard_map/ppermute | solution.py:507
  178.2 3.7 %collective-permute-start.64 = (bf16[48,128]{1,0:T(8,128)(2,1)S(1)}, bf16[48,128]{1,0:T(8,128)(2,1)S(1)}, u32[]{:S(2)}, u32[]{:S(2)}) collective-permute-start(bf16[48,128]{1,0:T(8,128)(2,1)S(1)} %get-tuple-element.339), channel_id=1, source_target_pairs={{0,2},{1,3},{2,0},{3,1},{4,6},{5,7},{6,4},{7,5},{8,10},{9,11},{10,... | collective-permute-start | bytes 36872 | tf_op jit(solution)/shard_map/ppermute | solution.py:507
  180.2 3.2 %collective-permute-start.65 = (bf16[48,128]{1,0:T(8,128)(2,1)S(1)}, bf16[48,128]{1,0:T(8,128)(2,1)S(1)}, u32[]{:S(2)}, u32[]{:S(2)}) collective-permute-start(bf16[48,128]{1,0:T(8,128)(2,1)S(1)} %get-tuple-element.340), channel_id=1, source_target_pairs={{0,3},{1,2},{2,1},{3,0},{4,7},{5,6},{6,5},{7,4},{8,11},{9,10},{10,... | collective-permute-start | bytes 36872 | tf_op jit(solution)/shard_map/ppermute | solution.py:507
  198.4 3.6 %collective-permute-start.70 = (f32[8,48]{1,0:T(8,128)S(1)}, f32[8,48]{1,0:T(8,128)S(1)}, u32[]{:S(2)}, u32[]{:S(2)}) collective-permute-start(f32[8,48]{1,0:T(8,128)S(1)} %slice_add_fusion), channel_id=1, source_target_pairs={{0,2},{1,3},{2,0},{3,1},{4,6},{5,7},{6,4},{7,5},{8,10},{9,11},{10,... | collective-permute-start | bytes 4616 | tf_op jit(solution)/shard_map/ppermute | solution.py:550
  (26 other events, 167.2 us)
Sparse Core Ops, SparseCore 0:
  9.5 155.9 all-gather.1

commit v2 on v1

--- a/solution.py
+++ b/solution.py
@@ -21,7 +21,7 @@
 EXPONENT = HD ** (-0.5) * math.log2(math.e)
 VMEM = pltpu.VMEM
 NOTES = 128
-LIVE, RANK, SHARD, PARENT, SOURCE = range(5)
+LIVE, RANK, SHARD, PARENT, SOURCE, COUNT = range(6)
 
 
 def dot(a, b):
@@ -44,6 +44,12 @@
 FAR = pl.BlockSpec(memory_space=pltpu.HBM)
 SMALL = pl.CostEstimate(flops=0, bytes_accessed=0, transcendentals=0)
 SCALARS = pl.BlockSpec(memory_space=pltpu.SMEM)
+
+
+def paired_sum(parts):
+    while len(parts) > 1:
+        parts = [a + b for a, b in zip(parts[::2], parts[1::2])]
+    return parts[0]
 
 
 def coordinates():
@@ -91,7 +97,7 @@
         notes = jnp.where(lane == at, value, notes)
 
     width = blocks[0].shape[1] - half - NOTES
-    hidden = (width - 128) // 3
+    hidden = width // 3
     rest = jnp.zeros((1, hidden), float32)
     for m in range(reward_out.shape[1] // hidden):
         rest = rest + jnp.where(me == m, reward_out[:, m * hidden : (m + 1) * hidden], 0.0)
@@ -99,13 +105,15 @@
     for _ in range(3):
         parts.append(rest.astype(bfloat16).astype(float32))
         rest = rest - parts[-1]
-    parts.append(jnp.full((1, 128), 1, int32).astype(float32) * count[0].astype(float32))
     shared = jnp.broadcast_to(jnp.concatenate(parts, 1), (capacity, width))
 
     rows = lax.broadcasted_iota(int32, (groups * capacity, children), 0)
     put = (rows == slot).astype(float32).astype(bfloat16)
     token_rows = dot(put, tokens[...])
     note_rows = dot(put, notes.astype(float32).astype(bfloat16))
+    row = lax.broadcasted_iota(int32, note_rows.shape, 0)
+    lane = lax.broadcasted_iota(int32, note_rows.shape, 1)
+    note_rows = jnp.where((lax.rem(row, capacity) == 0) & (lane == COUNT), count[0].astype(float32), note_rows)
     for k, block in enumerate(blocks):
         at = slice(k * capacity, (k + 1) * capacity)
         block[...] = jnp.concatenate([token_rows[at], note_rows[at], shared], 1).astype(bfloat16)
@@ -116,7 +124,7 @@
     tables = (child_parent[None], node_shard[None])
     return pl.pallas_call(
         functools.partial(dispatch_kernel, parents, groups),
-        out_shape=(struct((capacity, half + NOTES + 3 * hidden + 128)),) * groups,
+        out_shape=(struct((capacity, half + NOTES + 3 * hidden)),) * groups,
         in_specs=[SCALARS] + [FAR] * 4,
         out_specs=(WHOLE,) * groups,
         scratch_shapes=[VMEM(x.shape, x.dtype) for x in tables]
@@ -158,9 +166,10 @@
     at, child = lax.div(child, children), lax.rem(child, children)
     count = jnp.zeros(parent_row.shape, jnp.float32)
     for k in range(groups):
-        head = arrived[k * capacity : k * capacity + 1, base:]
+        first_row = arrived[k * capacity : k * capacity + 1]
+        head = first_row[:, base:]
         scale[pl.ds(own ^ k, 1), :] = head[:, :hidden] + head[:, hidden : 2 * hidden] + head[:, 2 * hidden : 3 * hidden]
-        count = jnp.where(at == (own ^ k), head[:, 3 * hidden : 3 * hidden + 1], count)
+        count = jnp.where(at == (own ^ k), first_row[:, half + COUNT : half + COUNT + 1], count)
     source = lax.div(parent_row[...], parents)
     going = child < count.astype(jnp.int32)
     most = jnp.zeros((1, 1), jnp.float32)
@@ -321,7 +330,7 @@
 def score_kernel(steps, load, cuts, mp, notes, *refs):
     take = lambda count: [refs.pop(0) for _ in range(count)]
     refs = list(refs)
-    ups, own_rows, peer_rows, blocks = take(cuts), take(steps), take(steps), take(mp)
+    ups, own_rows, peer_rows, blocks = take(cuts), take(steps), take(steps), take(mp if load else 1)
     kept = take(cuts * load)
     flat, total, *sems = refs
     groups, depth, hidden = ups[0].shape
@@ -361,6 +370,9 @@
             z = sum(dot(flat[:, i * depth : (i + 1) * depth], ups[i][r, :, at:end]) for i in range(cuts))
             here = jnp.where(shard == r, z, 0.0)
             total[:, at:end] = here if r == 0 else total[:, at:end] + here
+    if not load:
+        blocks[0][...] = total[...].astype(jnp.bfloat16)
+        return
     width = hidden // mp
     for j, block in enumerate(blocks):
         for m in range(mp):
@@ -374,13 +386,13 @@
     steps, cuts = len(own_rows), len(ups)
     groups, depth, hidden = ups[0].shape
     count = steps * own_rows[0].shape[0]
-    block = struct((count, hidden // mp))
+    blocks = (struct((count, hidden // mp)),) * mp if load else (struct((count, hidden)),)
     place = FAR if load else WHOLE
     return pl.pallas_call(
         functools.partial(score_kernel, steps, load, cuts, mp),
-        out_shape=(block,) * mp + tuple(VMEM(up.shape, up.dtype) for up in ups) * load,
+        out_shape=blocks + tuple(VMEM(up.shape, up.dtype) for up in ups) * load,
         in_specs=[WHOLE] + [place] * (cuts + 2 * steps),
-        out_specs=(WHOLE,) * (mp + cuts * load),
+        out_specs=(WHOLE,) * (len(blocks) + cuts * load),
         scratch_shapes=[VMEM((count, depth * cuts), jnp.bfloat16), VMEM((count, hidden), jnp.float32)]
         + [pltpu.SemaphoreType.DMA((steps,)), pltpu.SemaphoreType.DMA((groups, cuts))] * load,
         compiler_params=pltpu.CompilerParams(vmem_limit_bytes=16 << 20),
@@ -397,7 +409,7 @@
         gain = gain + jnp.where(shard == r, scale[r : r + 1, :], 0.0)
     values = []
     for t, factor in enumerate(factors):
-        z = sum(part[t * rows : (t + 1) * rows, :].astype(jnp.float32) for part in parts) * factor
+        z = paired_sum([part[t * rows : (t + 1) * rows, :].astype(jnp.float32) for part in parts]) * factor
         values.append(jnp.sum(z * jax.nn.sigmoid(z) * gain, -1, keepdims=True))
     return values
 
@@ -423,13 +435,16 @@
     )(notes, scale, *norms, *parts)
 
 
-def place_kernel(groups, cap, before, notes, scale, own_row, peer_row, *refs):
-    parts, table = refs[:-1], refs[-1]
+def place_kernel(groups, cap, mp, notes, own_row, peer_row, *refs):
+    befores, scales, parts, table = refs[:mp], refs[mp : 2 * mp], refs[2 * mp : 3 * mp], refs[3 * mp]
     rows = notes.shape[0]
+    _, _, me = coordinates()
+    before = paired_sum([x[...] for x in befores])
     values = [before[:, t : t + 1] for t in range(STEPS - 1)]
+    scale = [sum(jnp.where((me ^ j) == m, scales[j][...], 0.0) for j in range(mp)) for m in range(mp)]
     low, high = own_row[...].astype(jnp.float32), peer_row[...].astype(jnp.float32)
     squares = jnp.sum(low * low, -1, keepdims=True) + jnp.sum(high * high, -1, keepdims=True)
-    values += scores_of(notes, scale, parts, [lax.rsqrt(squares / D + 1e-06)])
+    values += scores_of(notes, jnp.concatenate(scale, 1), parts, [lax.rsqrt(squares / D + 1e-06)])
     number = lambda lane: notes[:, lane : lane + 1].astype(jnp.int32)
     shard, at = number(SHARD), number(SOURCE) * cap + number(RANK)
     live = notes[:, LIVE : LIVE + 1] > 0.5
@@ -440,16 +455,17 @@
             table[r * STEPS + t : r * STEPS + t + 1, :] = jnp.sum(jnp.where(spots, value, 0.0), 0, keepdims=True)
 
 
-def place(groups, cap, before, notes, scale, own_row, peer_row, parts):
-    return pl.pallas_call(
-        functools.partial(place_kernel, groups, cap),
+def place(groups, cap, notes, own_row, peer_row, befores, scales, parts):
+    mp = len(parts)
+    return pl.pallas_call(
+        functools.partial(place_kernel, groups, cap, mp),
         out_shape=struct((groups * STEPS, -(-groups * cap // 128) * 128), jnp.float32),
-        in_specs=[WHOLE] * (5 + len(parts)),
+        in_specs=[WHOLE] * (3 + 3 * mp),
         out_specs=WHOLE,
         compiler_params=pltpu.CompilerParams(vmem_limit_bytes=12 << 20),
         cost_estimate=SMALL,
         name="place",
-    )(before, notes, scale, own_row, peer_row, *parts)
+    )(notes, own_row, peer_row, *befores, *scales, *parts)
 
 
 def shards(
@@ -478,7 +494,6 @@
     hidden = reward_out.shape[1] // mp
     pairs = lambda count, k: [(i, i ^ k) for i in range(count)]
     swap = pairs(mp, 1)
-    shift = lambda count, k: [(i, (i + k) % count) for i in range(count)]
 
     ups = [lax.all_gather(reward_up[0], "dp", axis=0)]
 
@@ -487,7 +502,10 @@
     values = parent_values.reshape(parents * prefix, kv_cols)
     raw = (w_query, w_key, w_value, keys, values, w_out)
     blocks, raw = lax.optimization_barrier((blocks, raw))
-    blocks = [blocks[0]] + [lax.ppermute(blocks[k], "dp", pairs(groups, k)) for k in range(1, groups)]
+    arrived = {0: blocks[0]}
+    for k in sorted(range(1, groups), key=lambda k: -(k ^ (k & 1))):
+        arrived[k] = lax.ppermute(blocks[k], "dp", pairs(groups, k))
+    blocks = [arrived[k] for k in range(groups)]
     blocks, weights = lax.optimization_barrier((blocks, load(*raw)))
     gain = attn_gain.reshape(1, width)
 
@@ -502,9 +520,11 @@
 
         def products(first, last, ups, load):
             sums = score(mp, notes, ups, rows_own[first:last], rows_peer[first:last], load)
-            return sums[:mp], [held(up) for up in sums[mp:]]
+            count = mp if load else 1
+            return list(sums[:count]), [held(up) for up in sums[count:]]
 
         send = lambda sums: [sums[0]] + [lax.ppermute(sums[k], "mp", pairs(mp, k)) for k in range(1, mp)]
+        scales = send([scale] * mp)
         for step in range(STEPS):
             part, attn, key_now, value_now, norm = expand(
                 step, row_own, row_peer, gain, w_query, w_key, w_value, keys, values, bias, w_out,
@@ -516,23 +536,23 @@
             from_peer = lax.ppermute(part, "mp", swap)
             chip = project_own(rows, attn, w_out) + from_peer.astype(jnp.float32)
             sent = chip.astype(jnp.bfloat16)
-            others = [lax.ppermute(sent, "mp", shift(mp, k)) for k in range(2, mp, 2)]
+            others = [sent] + [lax.ppermute(sent, "mp", pairs(mp, k)) for k in range(2, mp, 2)]
+            if step == 0:
+                others, scales = lax.optimization_barrier((others, scales))
             if step + 1 == STEPS:
                 _, ups = lax.optimization_barrier((sent, ups))
                 before, ups = products(0, step, ups, True)
                 others, before = lax.optimization_barrier((others, before))
-            for other in others:
-                chip = chip + other.astype(jnp.float32)
-            state = state + chip
+            state = state + paired_sum([other.astype(jnp.float32) for other in others])
             row_own = state.astype(jnp.bfloat16)
             row_peer = lax.ppermute(row_own, "mp", swap)
             rows_own.append(row_own)
             rows_peer.append(row_peer)
         before = send(before)
         last, _ = products(step, STEPS, ups, False)
-        last, over = lax.optimization_barrier((send(last), over[0, 0]))
-        before = finish(notes, scale, norms[1:], before)
-        return place(groups, reward_cap, before, notes, scale, row_own, row_peer, last), over
+        last, over = lax.optimization_barrier((send(last * mp), over[0, 0]))
+        before = send([finish(notes, scale, norms[1:], before)] * mp)
+        return place(groups, reward_cap, notes, row_own, row_peer, before, scales, last), over
 
     operands = (blocks, ups, gain, child_parent, parent_blocks)
 
@@ -543,12 +563,7 @@
         table = lax.cond(over > 0, again, lambda table, raw, operands: table, table, raw, operands)
 
     table = lax.all_to_all(table, "dp", split_axis=0, concat_axis=0, tiled=True)
-    total = jnp.sum(table.reshape(groups, STEPS, -1), 0)[:, : groups * reward_cap]
-    total = total + lax.ppermute(total, "mp", swap)
-    result = total
-    for k in range(2, mp, 2):
-        result = result + lax.ppermute(total, "mp", shift(mp, k))
-    return result
+    return jnp.sum(table.reshape(groups, STEPS, -1), 0)[:, : groups * reward_cap]
 
 
 def solution(mesh):

time: 214 us -> 210 us (0.981)
  waiting for transfers between devices: 67.8 us -> 62.8 us
  starting transfers between devices: 34.7 us -> 38 us
    ppermute x17 -> x15, waiting for transfers between devices: 49.5 us -> 38.9 us  [the longest x8 38.9 us: run(): lax.ppermute(sent, 'mp', pairs(mp, k))]
    ppermute x6 -> x12, waiting for transfers between devices: 1.78 us -> 7.47 us  [run(): lax.ppermute(sums[k], 'mp', pairs(mp, k))]
    ppermute x6 -> x12, starting transfers between devices: 5.22 us -> 8.87 us  [run(): lax.ppermute(sums[k], 'mp', pairs(mp, k))]
    ppermute x17 -> x15, starting transfers between devices: 27.2 us -> 26.7 us  [the longest x8 14.2 us: run(): lax.ppermute(sent, 'mp', pairs(mp, k))]
  transfers between devices with their start and end apart: 41 -> 45, of which waited for: 28 -> 26; matrix products, arithmetic and copies ran while one was open for 1% -> 1% of each run, Pallas kernels for 36% -> 37%
where the time goes in v2:
time: 210 us; the launch traced here: 206 us
  Pallas kernels  76 us (36%)
  waiting for transfers between devices  62.8 us (30%)
  starting transfers between devices  38 us (18%)
  between operations  15.5 us (7%)
  blocking collectives  10.4 us (5%)
    pallas_call x8, Pallas kernels, expand(): pl.pallas_call(functools.partial(step_kernel, step), out_shape=(struct((s...  44.3 us
    ppermute x8, waiting for transfers between devices, run(): lax.ppermute(sent, 'mp', pairs(mp, k))  38.9 us
    ppermute x8, starting transfers between devices, run(): lax.ppermute(sent, 'mp', pairs(mp, k))  14.2 us
    ppermute x7, starting transfers between devices, shards(): arrived[k] = lax.ppermute(blocks[k], 'dp', pairs(groups, k))  12.5 us
    ppermute x9, waiting for transfers between devices, run(): row_peer = lax.ppermute(row_own, 'mp', swap)  11.8 us
    pallas_call x8, Pallas kernels, project_own(): pl.pallas_call(project_kernel, out_shape=struct((rows, w_out.shape[1] //...  10.7 us
    all_to_all x1, blocking collectives, shards(): table = lax.all_to_all(table, 'dp', split_axis=0, concat_axis=0, tiled=True)  10.4 us
    pallas_call x2, Pallas kernels, score(): pl.pallas_call(functools.partial(score_kernel, steps, load, cuts, mp), ou...  9.24 us
  transfers between devices with their start and end apart: 45, of which 26 were waited for; matrix products, arithmetic and copies ran while one was open for 1% of the time, Pallas kernels for 37%

profile of v2, /device:TPU:0, one launch (start us, length us, event | category | flops | bytes accessed | tf_op | source)
XLA Modules:
  0.0 206.5 jit_solution(15273942975166689418)
XLA Ops:
  9.4 3.0 %collective-permute-start.37 = (bf16[8,3072]{1,0:T(8,128)(2,1)S(1)}, bf16[8,3072]{1,0:T(8,128)(2,1)S(1)}, u32[]{:S(2)}, u32[]{:S(2)}) collective-permute-start(bf16[8,3072]{1,0:T(8,128)(2,1)S(1)} %get-tuple-element.270), channel_id=1, source_target_pairs={{0,4},{4,0},{8,12},{12,8},{16,20},{20,16},{24,28},{28,24},{1,5},{5... | collective-permute-start | bytes 147464 | tf_op jit(solution)/shard_map/ppermute | solution.py:507
  14.1 3.0 %collective-permute-start.40 = (bf16[8,3072]{1,0:T(8,128)(2,1)S(1)}, bf16[8,3072]{1,0:T(8,128)(2,1)S(1)}, u32[]{:S(2)}, u32[]{:S(2)}) collective-permute-start(bf16[8,3072]{1,0:T(8,128)(2,1)S(1)} %get-tuple-element.273), channel_id=1, source_target_pairs={{0,16},{4,20},{8,24},{12,28},{16,0},{20,4},{24,8},{28,12},{1,17},{... | collective-permute-start | bytes 147464 | tf_op jit(solution)/shard_map/ppermute | solution.py:507
  18.3 3.6 %collective-permute-start.42 = (bf16[8,3072]{1,0:T(8,128)(2,1)S(1)}, bf16[8,3072]{1,0:T(8,128)(2,1)S(1)}, u32[]{:S(2)}, u32[]{:S(2)}) collective-permute-start(bf16[8,3072]{1,0:T(8,128)(2,1)S(1)} %get-tuple-element.275), channel_id=1, source_target_pairs={{0,24},{4,28},{8,16},{12,20},{16,8},{20,12},{24,0},{28,4},{1,25},{... | collective-permute-start | bytes 147464 | tf_op jit(solution)/shard_map/ppermute | solution.py:507
  21.9 7.9 %load.3 = (bf16[5120,768]{1,0:T(8,128)(2,1)S(1)}, bf16[5120,256]{1,0:T(8,128)(2,1)S(1)}, bf16[5120,256]{1,0:T(8,128)(2,1)S(1)}, bf16[2048,256]{1,0:T(8,128)(2,1)...) custom-call(bf16[5120,768]{1,0:T(8,128)(2,1)} %refs_0_, bf16[5120,256]{1,0:T(8,128)(2,1)} %refs_1_, ...), custom_call_target="tpu_custom_call" | custom-call | bytes 25165824 | tf_op jit(solution)/shard_map/load/pallas_call | solution.py:214
  32.5 6.3 %expand.24 = (bf16[48,2560]{1,0:T(8,128)(2,1)S(1)}, bf16[64,768]{1,0:T(8,128)(2,1)S(1)}, bf16[48,256]{1,0:T(8,128)(2,1)S(1)}, bf16[48,256]{1,0:T(8,128)(2,1)S(1)}, f32[48,128]{1,0:T(8,128)}) custom-call(bf16[48,2560]{1,0:T(8,128)(2,1)S(1)} %get-tuple-element.298.own, bf16[48,2560]{1,0:T(8,128)(2,1)S(1)} %collective-permute-done.44.peer, ...), custom_call_target="tpu_custom_call" | custom-call | tf_op jit(solution)/shard_map/expand/pallas_call | solution.py:298
  40.4 1.8 collective-permute-start.46
  44.0 4.1 %collective-permute-done.49.refs_7_ = f32[8,128]{1,0:T(8,128)S(1)} collective-permute-done((f32[8,128]{1,0:T(8,128)S(1)}, f32[8,128]{1,0:T(8,128)S(1)}, u32[]{:S(2)}, u32[]{:S(2)}) %collective-permute-start.49) | collective-permute-done | bytes 4128 | tf_op jit(solution)/shard_map/ppermute | solution.py:526
  50.5 5.3 %expand.25 = (bf16[48,2560]{1,0:T(8,128)(2,1)S(1)}, bf16[64,768]{1,0:T(8,128)(2,1)S(1)}, bf16[48,256]{1,0:T(8,128)(2,1)S(1)}, bf16[48,256]{1,0:T(8,128)(2,1)S(1)}, f32[48,128]{1,0:T(8,128)S(1)}) custom-call(bf16[48,2560]{1,0:T(8,128)(2,1)S(1)} %fusion.4.own.refs_1_, bf16[48,2560]{1,0:T(8,128)(2,1)S(1)} %collective-permute-done.50.peer.refs_8_, ...), custom_call_target="tpu_custom_call" | custom-call | tf_op jit(solution)/shard_map/expand/pallas_call | solution.py:298
  57.5 1.8 collective-permute-start.52
  59.2 6.5 %collective-permute-done.52 = bf16[48,2560]{1,0:T(8,128)(2,1)S(1)} collective-permute-done((bf16[48,2560]{1,0:T(8,128)(2,1)S(1)}, bf16[48,2560]{1,0:T(8,128)(2,1)S(1)}, u32[]{:S(2)}, u32[]{:S(2)}) %collective-permute-start.52) | collective-permute-done | bytes 245792 | tf_op jit(solution)/shard_map/ppermute | solution.py:539
  67.5 5.4 %expand.26 = (bf16[48,2560]{1,0:T(8,128)(2,1)S(1)}, bf16[64,768]{1,0:T(8,128)(2,1)S(1)}, bf16[48,256]{1,0:T(8,128)(2,1)S(1)}, bf16[48,256]{1,0:T(8,128)(2,1)S(1)}, f32[48,128]{1,0:T(8,128)S(1)}) custom-call(bf16[48,2560]{1,0:T(8,128)(2,1)S(1)} %get-tuple-element.397.own.refs_2_, bf16[48,2560]{1,0:T(8,128)(2,1)S(1)} %collective-permute-done.53.peer.refs_9_, ...), custom_call_target="tpu_custom_call" | custom-call | tf_op jit(solution)/shard_map/expand/pallas_call | solution.py:298
  74.6 1.8 collective-permute-start.55
  76.4 6.5 %collective-permute-done.55 = bf16[48,2560]{1,0:T(8,128)(2,1)S(1)} collective-permute-done((bf16[48,2560]{1,0:T(8,128)(2,1)S(1)}, bf16[48,2560]{1,0:T(8,128)(2,1)S(1)}, u32[]{:S(2)}, u32[]{:S(2)}) %collective-permute-start.55) | collective-permute-done | bytes 245792 | tf_op jit(solution)/shard_map/ppermute | solution.py:539
  84.6 5.4 %expand.27 = (bf16[48,2560]{1,0:T(8,128)(2,1)S(1)}, bf16[64,768]{1,0:T(8,128)(2,1)S(1)}, bf16[48,256]{1,0:T(8,128)(2,1)S(1)}, bf16[48,256]{1,0:T(8,128)(2,1)S(1)}, f32[48,128]{1,0:T(8,128)S(1)}) custom-call(bf16[48,2560]{1,0:T(8,128)(2,1)S(1)} %fusion.5.own.refs_3_, bf16[48,2560]{1,0:T(8,128)(2,1)S(1)} %collective-permute-done.56.peer.refs_10_, ...), custom_call_target="tpu_custom_call" | custom-call | tf_op jit(solution)/shard_map/expand/pallas_call | solution.py:298
  93.4 6.5 %collective-permute-done.58 = bf16[48,2560]{1,0:T(8,128)(2,1)S(1)} collective-permute-done((bf16[48,2560]{1,0:T(8,128)(2,1)S(1)}, bf16[48,2560]{1,0:T(8,128)(2,1)S(1)}, u32[]{:S(2)}, u32[]{:S(2)}) %collective-permute-start.58) | collective-permute-done | bytes 245792 | tf_op jit(solution)/shard_map/ppermute | solution.py:539
  101.6 5.4 %expand.28 = (bf16[48,2560]{1,0:T(8,128)(2,1)S(1)}, bf16[64,768]{1,0:T(8,128)(2,1)S(1)}, bf16[48,256]{1,0:T(8,128)(2,1)S(1)}, bf16[48,256]{1,0:T(8,128)(2,1)S(1)}, f32[48,128]{1,0:T(8,128)S(1)}) custom-call(bf16[48,2560]{1,0:T(8,128)(2,1)S(1)} %get-tuple-element.395.own.refs_4_, bf16[48,2560]{1,0:T(8,128)(2,1)S(1)} %collective-permute-done.59.peer.refs_11_, ...), custom_call_target="tpu_custom_call" | custom-call | tf_op jit(solution)/shard_map/expand/pallas_call | solution.py:298
  108.6 1.8 collective-permute-start.61
  110.3 6.5 %collective-permute-done.61 = bf16[48,2560]{1,0:T(8,128)(2,1)S(1)} collective-permute-done((bf16[48,2560]{1,0:T(8,128)(2,1)S(1)}, bf16[48,2560]{1,0:T(8,128)(2,1)S(1)}, u32[]{:S(2)}, u32[]{:S(2)}) %collective-permute-start.61) | collective-permute-done | bytes 245792 | tf_op jit(solution)/shard_map/ppermute | solution.py:539
  118.5 5.4 %expand.29 = (bf16[48,2560]{1,0:T(8,128)(2,1)S(1)}, bf16[64,768]{1,0:T(8,128)(2,1)S(1)}, bf16[48,256]{1,0:T(8,128)(2,1)S(1)}, bf16[48,256]{1,0:T(8,128)(2,1)S(1)}, f32[48,128]{1,0:T(8,128)S(1)}) custom-call(bf16[48,2560]{1,0:T(8,128)(2,1)S(1)} %fusion.6.own.refs_5_, bf16[48,2560]{1,0:T(8,128)(2,1)S(1)} %collective-permute-done.62.peer.refs_12_, ...), custom_call_target="tpu_custom_call" | custom-call | tf_op jit(solution)/shard_map/expand/pallas_call | solution.py:298
  125.7 1.8 collective-permute-start.64
  127.5 6.5 %collective-permute-done.64 = bf16[48,2560]{1,0:T(8,128)(2,1)S(1)} collective-permute-done((bf16[48,2560]{1,0:T(8,128)(2,1)S(1)}, bf16[48,2560]{1,0:T(8,128)(2,1)S(1)}, u32[]{:S(2)}, u32[]{:S(2)}) %collective-permute-start.64) | collective-permute-done | bytes 245792 | tf_op jit(solution)/shard_map/ppermute | solution.py:539
  135.8 5.4 %expand.30 = (bf16[48,2560]{1,0:T(8,128)(2,1)S(1)}, bf16[64,768]{1,0:T(8,128)(2,1)S(1)}, bf16[48,256]{1,0:T(8,128)(2,1)S(1)}, bf16[48,256]{1,0:T(8,128)(2,1)S(1)}, f32[48,128]{1,0:T(8,128)S(1)}) custom-call(bf16[48,2560]{1,0:T(8,128)(2,1)S(1)} %get-tuple-element.393.own.refs_6_, bf16[48,2560]{1,0:T(8,128)(2,1)S(1)} %collective-permute-done.65.peer.refs_13_, ...), custom_call_target="tpu_custom_call" | custom-call | tf_op jit(solution)/shard_map/expand/pallas_call | solution.py:298
  142.8 1.8 collective-permute-start.67
  144.6 6.5 %collective-permute-done.67 = bf16[48,2560]{1,0:T(8,128)(2,1)S(1)} collective-permute-done((bf16[48,2560]{1,0:T(8,128)(2,1)S(1)}, bf16[48,2560]{1,0:T(8,128)(2,1)S(1)}, u32[]{:S(2)}, u32[]{:S(2)}) %collective-permute-start.67) | collective-permute-done | bytes 245792 | tf_op jit(solution)/shard_map/ppermute | solution.py:539
  152.7 5.8 %expand.31 = (bf16[48,2560]{1,0:T(8,128)(2,1)S(1)}, bf16[64,768]{1,0:T(8,128)(2,1)S(1)}, bf16[48,256]{1,0:T(8,128)(2,1)}, bf16[48,256]{1,0:T(8,128)(2,1)}, f32[48,128]{1,0:T(8,128)S(1)}) custom-call(bf16[48,2560]{1,0:T(8,128)(2,1)S(1)} %fusion.7.own.refs_7_, bf16[48,2560]{1,0:T(8,128)(2,1)S(1)} %collective-permute-done.68.peer.refs_14_, ...), custom_call_target="tpu_custom_call" | custom-call | tf_op jit(solution)/shard_map/expand/pallas_call | solution.py:298
  160.1 1.8 collective-permute-start.70
  161.9 3.4 %all-gather.2.cloned.1.call-done.refs_0_ = bf16[8,1280,512]{2,1,0:T(8,128)(2,1)} async-done(((bf16[1,1280,512]{2,1,0:T(8,128)(2,1)}), bf16[8,1280,512]{2,1,0:T(8,128)(2,1)}) %all-gather.2.cloned.1.call-update) | async-done | bytes 10485776 | tf_op jit(solution)/shard_map/all_gather | solution.py:498
  165.3 6.9 %score.6 = (bf16[336,128]{1,0:T(8,128)(2,1)S(1)}, bf16[336,128]{1,0:T(8,128)(2,1)S(1)}, bf16[336,128]{1,0:T(8,128)(2,1)S(1)}, bf16[336,128]{1,0:T(8,128)(2,1)S(1)}, bf16[8,1280,512]{2,1,0:T(8,128)(2,1)S(1)}) custom-call(f32[48,128]{1,0:T(8,128)S(1)} %get-tuple-element.297.notes, bf16[8,1280,512]{2,1,0:T(8,128)(2,1)} %all-gather.2.cloned.1.call-done.refs_0_, ...), custom_call_target="tpu_custom_call" | custom-call | tf_op jit(solution)/shard_map/score/pallas_call | solution.py:391
  172.9 2.7 %collective-permute-start.76 = (bf16[336,128]{1,0:T(8,128)(2,1)S(1)}, bf16[336,128]{1,0:T(8,128)(2,1)S(1)}, u32[]{:S(2)}, u32[]{:S(2)}) collective-permute-start(bf16[336,128]{1,0:T(8,128)(2,1)S(1)} %get-tuple-element.358), channel_id=1, source_target_pairs={{0,2},{1,3},{2,0},{3,1},{4,6},{5,7},{6,4},{7,5},{8,10},{9,11},{10,... | collective-permute-start | bytes 258056 | tf_op jit(solution)/shard_map/ppermute | solution.py:526
  175.7 2.3 %score.7.refs_8_ = bf16[48,512]{1,0:T(8,128)(2,1)S(1)} custom-call(f32[48,128]{1,0:T(8,128)S(1)} %get-tuple-element.297.notes, bf16[8,1280,512]{2,1,0:T(8,128)(2,1)S(1)} %get-tuple-element.340.refs_0_, bf16[48,2560]{1,0:T(8,128)(2,1)S(1)} %add_convert_fusion.9.refs_1_.own_row, bf16[48,2560]{1,0:T(8,128)(2,1)S(1)} %collective-permute-done.71.refs_2_.peer_row), custom_call_target="tpu_custom_call" | custom-call | tf_op jit(solution)/shard_map/score/pallas_call | solution.py:391
  184.5 2.1 %collective-permute-done.79.refs_2_ = f32[48,128]{1,0:T(8,128)S(1)} collective-permute-done((f32[48,128]{1,0:T(8,128)S(1)}, f32[48,128]{1,0:T(8,128)S(1)}, u32[]{:S(2)}, u32[]{:S(2)}) %collective-permute-start.79) | collective-permute-done | bytes 24608 | tf_op jit(solution)/shard_map/ppermute | solution.py:526
  188.4 10.4 %all_to_all.9 = f32[8,8,128]{2,1,0:T(8,128)S(1)} all-to-all(f32[8,8,128]{2,1,0:T(8,128)S(1)} %bitcast.22), channel_id=1, replica_groups=mesh['dp'=8,'mp'=4] {'dp'}, dimensions={0} | all-to-all | bytes 65536 | tf_op jit(solution)/shard_map/all_to_all | solution.py:565
  (136 shorter events, 45.9 us)
Async XLA Ops:
  6.5 158.7 %all-gather.2.cloned.1.call-start = ((), (), s32[]{:S(2)}) async-start(), calls=%async_computation.1 | async-start | bytes 11796480 | tf_op jit(solution)/shard_map/all_gather | solution.py:498
  9.4 8.9 %collective-permute-start.37 = (bf16[8,3072]{1,0:T(8,128)(2,1)S(1)}, bf16[8,3072]{1,0:T(8,128)(2,1)S(1)}, u32[]{:S(2)}, u32[]{:S(2)}) collective-permute-start(bf16[8,3072]{1,0:T(8,128)(2,1)S(1)} %get-tuple-element.270), channel_id=1, source_target_pairs={{0,4},{4,0},{8,12},{12,8},{16,20},{20,16},{24,28},{28,24},{1,5},{5... | collective-permute-start | bytes 147464 | tf_op jit(solution)/shard_map/ppermute | solution.py:507
  12.5 9.5 %collective-permute-start.38 = (bf16[8,3072]{1,0:T(8,128)(2,1)S(1)}, bf16[8,3072]{1,0:T(8,128)(2,1)S(1)}, u32[]{:S(2)}, u32[]{:S(2)}) collective-permute-start(bf16[8,3072]{1,0:T(8,128)(2,1)S(1)} %get-tuple-element.271), channel_id=1, source_target_pairs={{0,8},{4,12},{8,0},{12,4},{16,24},{20,28},{24,16},{28,20},{1,9},{5... | collective-permute-start | bytes 147464 | tf_op jit(solution)/shard_map/ppermute | solution.py:507
  14.1 15.8 %collective-permute-start.39 = (bf16[8,3072]{1,0:T(8,128)(2,1)S(1)}, bf16[8,3072]{1,0:T(8,128)(2,1)S(1)}, u32[]{:S(2)}, u32[]{:S(2)}) collective-permute-start(bf16[8,3072]{1,0:T(8,128)(2,1)S(1)} %get-tuple-element.272), channel_id=1, source_target_pairs={{0,12},{4,8},{8,4},{12,0},{16,28},{20,24},{24,20},{28,16},{1,13},{... | collective-permute-start | bytes 147464 | tf_op jit(solution)/shard_map/ppermute | solution.py:507
  14.1 15.9 %collective-permute-start.40 = (bf16[8,3072]{1,0:T(8,128)(2,1)S(1)}, bf16[8,3072]{1,0:T(8,128)(2,1)S(1)}, u32[]{:S(2)}, u32[]{:S(2)}) collective-permute-start(bf16[8,3072]{1,0:T(8,128)(2,1)S(1)} %get-tuple-element.273), channel_id=1, source_target_pairs={{0,16},{4,20},{8,24},{12,28},{16,0},{20,4},{24,8},{28,12},{1,17},{... | collective-permute-start | bytes 147464 | tf_op jit(solution)/shard_map/ppermute | solution.py:507
  17.0 12.9 %collective-permute-start.41 = (bf16[8,3072]{1,0:T(8,128)(2,1)S(1)}, bf16[8,3072]{1,0:T(8,128)(2,1)S(1)}, u32[]{:S(2)}, u32[]{:S(2)}) collective-permute-start(bf16[8,3072]{1,0:T(8,128)(2,1)S(1)} %get-tuple-element.274), channel_id=1, source_target_pairs={{0,20},{4,16},{8,28},{12,24},{16,4},{20,0},{24,12},{28,8},{1,21},{... | collective-permute-start | bytes 147464 | tf_op jit(solution)/shard_map/ppermute | solution.py:507
  18.3 11.6 %collective-permute-start.42 = (bf16[8,3072]{1,0:T(8,128)(2,1)S(1)}, bf16[8,3072]{1,0:T(8,128)(2,1)S(1)}, u32[]{:S(2)}, u32[]{:S(2)}) collective-permute-start(bf16[8,3072]{1,0:T(8,128)(2,1)S(1)} %get-tuple-element.275), channel_id=1, source_target_pairs={{0,24},{4,28},{8,16},{12,20},{16,8},{20,12},{24,0},{28,4},{1,25},{... | collective-permute-start | bytes 147464 | tf_op jit(solution)/shard_map/ppermute | solution.py:507
  21.9 8.0 %collective-permute-start.43 = (bf16[8,3072]{1,0:T(8,128)(2,1)S(1)}, bf16[8,3072]{1,0:T(8,128)(2,1)S(1)}, u32[]{:S(2)}, u32[]{:S(2)}) collective-permute-start(bf16[8,3072]{1,0:T(8,128)(2,1)S(1)} %get-tuple-element.276), channel_id=1, source_target_pairs={{0,28},{4,24},{8,20},{12,16},{16,12},{20,8},{24,4},{28,0},{1,29},{... | collective-permute-start | bytes 147464 | tf_op jit(solution)/shard_map/ppermute | solution.py:507
  30.9 1.6 collective-permute-start.44
  40.4 8.4 %collective-permute-start.46 = (bf16[48,2560]{1,0:T(8,128)(2,1)S(1)}, bf16[48,2560]{1,0:T(8,128)(2,1)S(1)}, u32[]{:S(2)}, u32[]{:S(2)}) collective-permute-start(bf16[48,2560]{1,0:T(8,128)(2,1)S(1)} %add_convert_fusion.17), channel_id=1, source_target_pairs={{0,2},{1,3},{2,0},{3,1},{4,6},{5,7},{6,4},{7,5},{8,10},{9,11},{10,... | collective-permute-start | bytes 737288 | tf_op jit(solution)/shard_map/ppermute | solution.py:539
  42.2 5.9 %collective-permute-start.49 = (f32[8,128]{1,0:T(8,128)S(1)}, f32[8,128]{1,0:T(8,128)S(1)}, u32[]{:S(2)}, u32[]{:S(2)}) collective-permute-start(f32[8,128]{1,0:T(8,128)S(1)} %get-tuple-element.360.scale.refs_4_), channel_id=1, source_target_pairs={{0,3},{1,2},{2,1},{3,0},{4,7},{5,6},{6,5},{7,4},{8,11},{9,10},{10,... | collective-permute-start | bytes 12296 | tf_op jit(solution)/shard_map/ppermute | solution.py:526
  42.2 6.6 %collective-permute-start.48 = (f32[8,128]{1,0:T(8,128)S(1)}, f32[8,128]{1,0:T(8,128)S(1)}, u32[]{:S(2)}, u32[]{:S(2)}) collective-permute-start(f32[8,128]{1,0:T(8,128)S(1)} %get-tuple-element.360.scale.refs_4_), channel_id=1, source_target_pairs={{0,2},{1,3},{2,0},{3,1},{4,6},{5,7},{6,4},{7,5},{8,10},{9,11},{10,... | collective-permute-start | bytes 12296 | tf_op jit(solution)/shard_map/ppermute | solution.py:526
  43.8 5.0 %collective-permute-start.47 = (f32[8,128]{1,0:T(8,128)S(1)}, f32[8,128]{1,0:T(8,128)S(1)}, u32[]{:S(2)}, u32[]{:S(2)}) collective-permute-start(f32[8,128]{1,0:T(8,128)S(1)} %get-tuple-element.360.scale.refs_4_), channel_id=1, source_target_pairs={{0,1},{1,0},{2,3},{3,2},{4,5},{5,4},{6,7},{7,6},{8,9},{9,8},{10,11... | collective-permute-start | bytes 12296 | tf_op jit(solution)/shard_map/ppermute | solution.py:526
  57.5 8.2 %collective-permute-start.52 = (bf16[48,2560]{1,0:T(8,128)(2,1)S(1)}, bf16[48,2560]{1,0:T(8,128)(2,1)S(1)}, u32[]{:S(2)}, u32[]{:S(2)}) collective-permute-start(bf16[48,2560]{1,0:T(8,128)(2,1)S(1)} %add_convert_fusion.16), channel_id=1, source_target_pairs={{0,2},{1,3},{2,0},{3,1},{4,6},{5,7},{6,4},{7,5},{8,10},{9,11},{10,... | collective-permute-start | bytes 737288 | tf_op jit(solution)/shard_map/ppermute | solution.py:539
  72.8 1.7 collective-permute-start.54
  74.6 8.3 %collective-permute-start.55 = (bf16[48,2560]{1,0:T(8,128)(2,1)S(1)}, bf16[48,2560]{1,0:T(8,128)(2,1)S(1)}, u32[]{:S(2)}, u32[]{:S(2)}) collective-permute-start(bf16[48,2560]{1,0:T(8,128)(2,1)S(1)} %add_convert_fusion.15), channel_id=1, source_target_pairs={{0,2},{1,3},{2,0},{3,1},{4,6},{5,7},{6,4},{7,5},{8,10},{9,11},{10,... | collective-permute-start | bytes 737288 | tf_op jit(solution)/shard_map/ppermute | solution.py:539
  91.6 8.2 %collective-permute-start.58 = (bf16[48,2560]{1,0:T(8,128)(2,1)S(1)}, bf16[48,2560]{1,0:T(8,128)(2,1)S(1)}, u32[]{:S(2)}, u32[]{:S(2)}) collective-permute-start(bf16[48,2560]{1,0:T(8,128)(2,1)S(1)} %add_convert_fusion.14), channel_id=1, source_target_pairs={{0,2},{1,3},{2,0},{3,1},{4,6},{5,7},{6,4},{7,5},{8,10},{9,11},{10,... | collective-permute-start | bytes 737288 | tf_op jit(solution)/shard_map/ppermute | solution.py:539
  108.6 8.2 %collective-permute-start.61 = (bf16[48,2560]{1,0:T(8,128)(2,1)S(1)}, bf16[48,2560]{1,0:T(8,128)(2,1)S(1)}, u32[]{:S(2)}, u32[]{:S(2)}) collective-permute-start(bf16[48,2560]{1,0:T(8,128)(2,1)S(1)} %add_convert_fusion.13), channel_id=1, source_target_pairs={{0,2},{1,3},{2,0},{3,1},{4,6},{5,7},{6,4},{7,5},{8,10},{9,11},{10,... | collective-permute-start | bytes 737288 | tf_op jit(solution)/shard_map/ppermute | solution.py:539
  123.9 1.7 collective-permute-start.63
  125.7 8.3 %collective-permute-start.64 = (bf16[48,2560]{1,0:T(8,128)(2,1)S(1)}, bf16[48,2560]{1,0:T(8,128)(2,1)S(1)}, u32[]{:S(2)}, u32[]{:S(2)}) collective-permute-start(bf16[48,2560]{1,0:T(8,128)(2,1)S(1)} %add_convert_fusion.12), channel_id=1, source_target_pairs={{0,2},{1,3},{2,0},{3,1},{4,6},{5,7},{6,4},{7,5},{8,10},{9,11},{10,... | collective-permute-start | bytes 737288 | tf_op jit(solution)/shard_map/ppermute | solution.py:539
  142.8 8.2 %collective-permute-start.67 = (bf16[48,2560]{1,0:T(8,128)(2,1)S(1)}, bf16[48,2560]{1,0:T(8,128)(2,1)S(1)}, u32[]{:S(2)}, u32[]{:S(2)}) collective-permute-start(bf16[48,2560]{1,0:T(8,128)(2,1)S(1)} %add_convert_fusion.11), channel_id=1, source_target_pairs={{0,2},{1,3},{2,0},{3,1},{4,6},{5,7},{6,4},{7,5},{8,10},{9,11},{10,... | collective-permute-start | bytes 737288 | tf_op jit(solution)/shard_map/ppermute | solution.py:539
  160.1 12.0 %collective-permute-start.70 = (bf16[48,2560]{1,0:T(8,128)(2,1)S(1)}, bf16[48,2560]{1,0:T(8,128)(2,1)S(1)}, u32[]{:S(2)}, u32[]{:S(2)}) collective-permute-start(bf16[48,2560]{1,0:T(8,128)(2,1)S(1)} %add_convert_fusion.10), channel_id=1, source_target_pairs={{0,2},{1,3},{2,0},{3,1},{4,6},{5,7},{6,4},{7,5},{8,10},{9,11},{10,... | collective-permute-start | bytes 737288 | tf_op jit(solution)/shard_map/ppermute | solution.py:539
  172.3 3.3 %collective-permute-start.71 = (bf16[48,2560]{1,0:T(8,128)(2,1)S(1)}, bf16[48,2560]{1,0:T(8,128)(2,1)S(1)}, u32[]{:S(2)}, u32[]{:S(2)}) collective-permute-start(bf16[48,2560]{1,0:T(8,128)(2,1)S(1)} %add_convert_fusion.9.refs_1_.own_row), channel_id=1, source_target_pairs={{0,1},{1,0},{2,3},{3,2},{4,5},{5,4},{6,7},{7,6},{8,9},{9,8},{10,11... | collective-permute-start | bytes 737288 | tf_op jit(solution)/shard_map/ppermute | solution.py:548
  172.5 7.3 %collective-permute-start.75 = (bf16[336,128]{1,0:T(8,128)(2,1)S(1)}, bf16[336,128]{1,0:T(8,128)(2,1)S(1)}, u32[]{:S(2)}, u32[]{:S(2)}) collective-permute-start(bf16[336,128]{1,0:T(8,128)(2,1)S(1)} %get-tuple-element.357), channel_id=1, source_target_pairs={{0,1},{1,0},{2,3},{3,2},{4,5},{5,4},{6,7},{7,6},{8,9},{9,8},{10,11... | collective-permute-start | bytes 258056 | tf_op jit(solution)/shard_map/ppermute | solution.py:526
  172.9 7.1 %collective-permute-start.76 = (bf16[336,128]{1,0:T(8,128)(2,1)S(1)}, bf16[336,128]{1,0:T(8,128)(2,1)S(1)}, u32[]{:S(2)}, u32[]{:S(2)}) collective-permute-start(bf16[336,128]{1,0:T(8,128)(2,1)S(1)} %get-tuple-element.358), channel_id=1, source_target_pairs={{0,2},{1,3},{2,0},{3,1},{4,6},{5,7},{6,4},{7,5},{8,10},{9,11},{10,... | collective-permute-start | bytes 258056 | tf_op jit(solution)/shard_map/ppermute | solution.py:526
  175.6 4.8 %collective-permute-start.77 = (bf16[336,128]{1,0:T(8,128)(2,1)S(1)}, bf16[336,128]{1,0:T(8,128)(2,1)S(1)}, u32[]{:S(2)}, u32[]{:S(2)}) collective-permute-start(bf16[336,128]{1,0:T(8,128)(2,1)S(1)} %get-tuple-element.359), channel_id=1, source_target_pairs={{0,3},{1,2},{2,1},{3,0},{4,7},{5,6},{6,5},{7,4},{8,11},{9,10},{10,... | collective-permute-start | bytes 258056 | tf_op jit(solution)/shard_map/ppermute | solution.py:526
  178.0 5.0 %collective-permute-start.74 = (bf16[48,512]{1,0:T(8,128)(2,1)S(1)}, bf16[48,512]{1,0:T(8,128)(2,1)S(1)}, u32[]{:S(2)}, u32[]{:S(2)}) collective-permute-start(bf16[48,512]{1,0:T(8,128)(2,1)S(1)} %score.7.refs_8_), channel_id=1, source_target_pairs={{0,3},{1,2},{2,1},{3,0},{4,7},{5,6},{6,5},{7,4},{8,11},{9,10},{10,... | collective-permute-start | bytes 147464 | tf_op jit(solution)/shard_map/ppermute | solution.py:526
  179.7 4.1 %collective-permute-start.73 = (bf16[48,512]{1,0:T(8,128)(2,1)S(1)}, bf16[48,512]{1,0:T(8,128)(2,1)S(1)}, u32[]{:S(2)}, u32[]{:S(2)}) collective-permute-start(bf16[48,512]{1,0:T(8,128)(2,1)S(1)} %score.7.refs_8_), channel_id=1, source_target_pairs={{0,2},{1,3},{2,0},{3,1},{4,6},{5,7},{6,4},{7,5},{8,10},{9,11},{10,... | collective-permute-start | bytes 147464 | tf_op jit(solution)/shard_map/ppermute | solution.py:526
  179.9 3.9 %collective-permute-start.72 = (bf16[48,512]{1,0:T(8,128)(2,1)S(1)}, bf16[48,512]{1,0:T(8,128)(2,1)S(1)}, u32[]{:S(2)}, u32[]{:S(2)}) collective-permute-start(bf16[48,512]{1,0:T(8,128)(2,1)S(1)} %score.7.refs_8_), channel_id=1, source_target_pairs={{0,1},{1,0},{2,3},{3,2},{4,5},{5,4},{6,7},{7,6},{8,9},{9,8},{10,11... | collective-permute-start | bytes 147464 | tf_op jit(solution)/shard_map/ppermute | solution.py:526
  181.2 3.3 %collective-permute-start.80 = (f32[48,128]{1,0:T(8,128)S(1)}, f32[48,128]{1,0:T(8,128)S(1)}, u32[]{:S(2)}, u32[]{:S(2)}) collective-permute-start(f32[48,128]{1,0:T(8,128)S(1)} %finish.3.refs_0_), channel_id=1, source_target_pairs={{0,3},{1,2},{2,1},{3,0},{4,7},{5,6},{6,5},{7,4},{8,11},{9,10},{10,... | collective-permute-start | bytes 73736 | tf_op jit(solution)/shard_map/ppermute | solution.py:526
  182.8 3.8 %collective-permute-start.79 = (f32[48,128]{1,0:T(8,128)S(1)}, f32[48,128]{1,0:T(8,128)S(1)}, u32[]{:S(2)}, u32[]{:S(2)}) collective-permute-start(f32[48,128]{1,0:T(8,128)S(1)} %finish.3.refs_0_), channel_id=1, source_target_pairs={{0,2},{1,3},{2,0},{3,1},{4,6},{5,7},{6,4},{7,5},{8,10},{9,11},{10,... | collective-permute-start | bytes 73736 | tf_op jit(solution)/shard_map/ppermute | solution.py:526
  183.0 3.6 %collective-permute-start.78 = (f32[48,128]{1,0:T(8,128)S(1)}, f32[48,128]{1,0:T(8,128)S(1)}, u32[]{:S(2)}, u32[]{:S(2)}) collective-permute-start(f32[48,128]{1,0:T(8,128)S(1)} %finish.3.refs_0_), channel_id=1, source_target_pairs={{0,1},{1,0},{2,3},{3,2},{4,5},{5,4},{6,7},{7,6},{8,9},{9,8},{10,11... | collective-permute-start | bytes 73736 | tf_op jit(solution)/shard_map/ppermute | solution.py:526
  (30 other events, 171.9 us)
Sparse Core Ops, SparseCore 0:
  9.5 155.6 all-gather.1

commit v3 on v2

--- a/solution.py
+++ b/solution.py
@@ -136,8 +136,13 @@
     )(child_count, *map(far, (*tables, tokens, reward_out)))
 
 
+def crossing_first(groups):
+    return sorted(range(groups), key=lambda k: -(k ^ (k & 1)))
+
+
 def pack_kernel(offset, hidden, prefix, blocks_held, parent_row, *rest):
     blocks, (row, notes, bias, scale, over) = rest[:-5], rest[-5:]
+    blocks = [block for _, block in sorted(zip(crossing_first(len(blocks)), blocks), key=lambda pair: pair[0])]
     _, own, _ = coordinates()
     groups, capacity = len(blocks), blocks[0].shape[0]
     rows, half = row.shape
@@ -197,7 +202,7 @@
         compiler_params=pltpu.CompilerParams(vmem_limit_bytes=12 << 20),
         cost_estimate=SMALL,
         name="pack",
-    )(blocks_held, child_parent[None], *blocks)
+    )(blocks_held, child_parent[None], *[blocks[k] for k in crossing_first(groups)])
 
 
 def load_kernel(*refs):
@@ -234,7 +239,43 @@
         )[: out.shape[0]].astype(out.dtype)
 
 
-def step_kernel(step, own, peer, gain, w_query, w_key, w_value, keys, values, bias, w_out, *rest):
+def products_of(row, first, half, gain, weights, normed):
+    at = pl.ds(pl.multiple_of(first, half), half)
+    slots = row.shape[0]
+    normed[:slots, :] = (row[...].astype(jnp.float32) * gain[:, at]).astype(jnp.bfloat16)
+    if normed.shape[0] > slots:
+        normed[slots:, :] = jnp.zeros((normed.shape[0] - slots, half), jnp.bfloat16)
+    column = 0
+    for w in weights:
+        for start in range(0, w.shape[1], COLUMNS):
+            end = min(start + COLUMNS, w.shape[1])
+            yield slice(column + start, column + end), dot(normed[...], w[at, start:end])[:slots]
+        column += w.shape[1]
+
+
+def begin_kernel(own, gain, w_query, w_key, w_value, out, normed):
+    core, _, _ = coordinates()
+    half = own.shape[1]
+    for columns, value in products_of(own, core * half, half, gain, (w_query, w_key, w_value), normed):
+        out[:, columns] = value
+
+
+def begin(own, gain, w_query, w_key, w_value):
+    slots, half = own.shape
+    padded = -(-slots // ROWS) * ROWS
+    return pl.pallas_call(
+        begin_kernel,
+        out_shape=struct((slots, w_query.shape[1] + 2 * w_key.shape[1]), jnp.float32),
+        in_specs=[WHOLE] * 5,
+        out_specs=WHOLE,
+        scratch_shapes=[VMEM((padded, half), jnp.bfloat16)],
+        compiler_params=pltpu.CompilerParams(vmem_limit_bytes=8 << 20),
+        cost_estimate=SMALL,
+        name="begin",
+    )(own, gain, w_query, w_key, w_value)
+
+
+def step_kernel(step, own, peer, begun, gain, w_query, w_key, w_value, keys, values, bias, w_out, *rest):
     past_keys, past_values = rest[:step], rest[step : 2 * step]
     rest = rest[2 * step :]
     half = own.shape[1]
@@ -243,21 +284,12 @@
     kv_heads = kv_cols // HD
     part, attn, key_now, value_now, norm, normed, query = rest
     core, _, _ = coordinates()
-    first = core == 0
-    low = jnp.where(first, own[...], peer[...]).astype(jnp.float32)
-    high = jnp.where(first, peer[...], own[...]).astype(jnp.float32)
-    squares = jnp.sum(low * low, -1, keepdims=True) + jnp.sum(high * high, -1, keepdims=True)
+    here, there = own[...].astype(jnp.float32), peer[...].astype(jnp.float32)
+    squares = jnp.sum(here * here, -1, keepdims=True) + jnp.sum(there * there, -1, keepdims=True)
     factor = lax.rsqrt(squares / D + 1e-06)
     norm[...] = jnp.broadcast_to(factor, norm.shape)
-    normed[:slots, :half] = (low * factor * gain[:, :half]).astype(jnp.bfloat16)
-    normed[:slots, half:] = (high * factor * gain[:, half:]).astype(jnp.bfloat16)
-    if normed.shape[0] > slots:
-        normed[slots:, :] = jnp.zeros((normed.shape[0] - slots, D), jnp.bfloat16)
-    for at in range(0, q_cols, COLUMNS):
-        end = min(at + COLUMNS, q_cols)
-        query[:, at:end] = dot(normed[...], w_query[:, at:end])
-    query[:, q_cols : q_cols + kv_cols] = dot(normed[...], w_key[...])
-    query[:, q_cols + kv_cols :] = dot(normed[...], w_value[...])
+    for columns, value in products_of(peer, (1 - core) * half, half, gain, (w_query, w_key, w_value), normed):
+        query[:, columns] = (begun[:, columns] + value) * factor
     key_now[...] = query[:slots, q_cols : q_cols + kv_cols].astype(jnp.bfloat16)
     value_now[...] = query[:slots, q_cols + kv_cols :].astype(jnp.bfloat16)
     recent = slots * (step + 1)
@@ -290,7 +322,7 @@
     project(attn, w_out, part, (1 - core) * half)
 
 
-def expand(step, own, peer, gain, w_query, w_key, w_value, keys, values, bias, w_out, past_keys, past_values):
+def expand(step, own, peer, begun, gain, w_query, w_key, w_value, keys, values, bias, w_out, past_keys, past_values):
     slots, half = own.shape
     kv_cols = w_key.shape[1]
     q_cols = w_query.shape[1]
@@ -301,13 +333,13 @@
             struct((slots, half)), struct((padded, q_cols)), struct((slots, kv_cols)), struct((slots, kv_cols)),
             struct((slots, 128), jnp.float32),
         ),
-        in_specs=[WHOLE] * (10 + 2 * step),
+        in_specs=[WHOLE] * (11 + 2 * step),
         out_specs=[WHOLE] * 5,
-        scratch_shapes=[VMEM((padded, D), jnp.bfloat16), VMEM((padded, q_cols + 2 * kv_cols), jnp.float32)],
+        scratch_shapes=[VMEM((padded, half), jnp.bfloat16), VMEM((slots, q_cols + 2 * kv_cols), jnp.float32)],
         compiler_params=pltpu.CompilerParams(vmem_limit_bytes=16 << 20),
         cost_estimate=SMALL,
         name="expand",
-    )(own, peer, gain, w_query, w_key, w_value, keys, values, bias, w_out, *past_keys, *past_values)
+    )(own, peer, begun, gain, w_query, w_key, w_value, keys, values, bias, w_out, *past_keys, *past_values)
 
 
 def project_kernel(attn, w_out, part):
@@ -327,21 +359,22 @@
     )(attn, w_out)
 
 
-def score_kernel(steps, load, cuts, mp, notes, *refs):
+def score_kernel(steps, load, groups, mp, notes, *refs):
     take = lambda count: [refs.pop(0) for _ in range(count)]
     refs = list(refs)
-    ups, own_rows, peer_rows, blocks = take(cuts), take(steps), take(steps), take(mp if load else 1)
-    kept = take(cuts * load)
+    ups, own_rows, peer_rows, blocks = take(1 + groups if load else 2), take(steps), take(steps), take(mp if load else 1)
+    kept = take(2 * load)
     flat, total, *sems = refs
-    groups, depth, hidden = ups[0].shape
+    _, cut, hidden = ups[0].shape
+    depth = flat.shape[1]
     rows = own_rows[0].shape[0]
-    core, _, me = coordinates()
+    core, own, me = coordinates()
     for t in range(steps):
         target = flat.at[t * rows : (t + 1) * rows]
         for m in range(mp):
-            at = m % (mp // 2) * depth * cuts
+            at = m % (mp // 2) * depth
             for c in range(2):
-                source = (own_rows if m // (mp // 2) == c else peer_rows)[t].at[:, at : at + depth * cuts]
+                source = (own_rows if m // (mp // 2) == c else peer_rows)[t].at[:, at : at + depth]
 
                 @pl.when((me == m) & (core == c))
                 def _():
@@ -350,24 +383,23 @@
                     else:
                         target[...] = source[...]
 
-    copies = {}
     if load:
         for r in range(groups):
-            for i in range(cuts):
-                copies[r, i] = pltpu.make_async_copy(ups[i].at[r], kept[i].at[r], sems[1].at[r, i])
-                copies[r, i].start()
+            pltpu.make_async_copy(ups[0].at[r], kept[0].at[r], sems[1].at[r]).start()
+        for k in range(groups):
+            pltpu.make_async_copy(ups[1 + k], kept[1].at[own ^ k], sems[2].at[own ^ k]).start()
         ups = kept
         for t in range(steps):
             target = flat.at[t * rows : (t + 1) * rows]
             pltpu.make_async_copy(target, target, sems[0].at[t]).wait()
     shard = jnp.concatenate([notes[:, SHARD : SHARD + 1].astype(jnp.int32)] * steps, 0)
     for r in range(groups):
-        for i in range(cuts):
-            if load:
-                copies[r, i].wait()
+        if load:
+            for i, up in enumerate(ups):
+                pltpu.make_async_copy(up.at[r], up.at[r], sems[1 + i].at[r]).wait()
         for at in range(0, hidden, COLUMNS):
             end = min(at + COLUMNS, hidden)
-            z = sum(dot(flat[:, i * depth : (i + 1) * depth], ups[i][r, :, at:end]) for i in range(cuts))
+            z = dot(flat[:, :cut], ups[0][r, :, at:end]) + dot(flat[:, cut:], ups[1][r, :, at:end])
             here = jnp.where(shard == r, z, 0.0)
             total[:, at:end] = here if r == 0 else total[:, at:end] + here
     if not load:
@@ -383,18 +415,20 @@
 
 
 def score(mp, notes, ups, own_rows, peer_rows, load):
-    steps, cuts = len(own_rows), len(ups)
-    groups, depth, hidden = ups[0].shape
+    steps = len(own_rows)
+    groups, cut, hidden = ups[0].shape
+    rest = ups[1].shape[-2]
     count = steps * own_rows[0].shape[0]
     blocks = (struct((count, hidden // mp)),) * mp if load else (struct((count, hidden)),)
+    kept = (VMEM((groups, cut, hidden), jnp.bfloat16), VMEM((groups, rest, hidden), jnp.bfloat16)) * load
     place = FAR if load else WHOLE
-    return pl.pallas_call(
-        functools.partial(score_kernel, steps, load, cuts, mp),
-        out_shape=blocks + tuple(VMEM(up.shape, up.dtype) for up in ups) * load,
-        in_specs=[WHOLE] + [place] * (cuts + 2 * steps),
-        out_specs=(WHOLE,) * (len(blocks) + cuts * load),
-        scratch_shapes=[VMEM((count, depth * cuts), jnp.bfloat16), VMEM((count, hidden), jnp.float32)]
-        + [pltpu.SemaphoreType.DMA((steps,)), pltpu.SemaphoreType.DMA((groups, cuts))] * load,
+    sems = [pltpu.SemaphoreType.DMA((steps,))] + [pltpu.SemaphoreType.DMA((groups,))] * 2
+    return pl.pallas_call(
+        functools.partial(score_kernel, steps, load, groups, mp),
+        out_shape=blocks + kept,
+        in_specs=[WHOLE] + [place] * (len(ups) + 2 * steps),
+        out_specs=(WHOLE,) * (len(blocks) + len(kept)),
+        scratch_shapes=[VMEM((count, cut + rest), jnp.bfloat16), VMEM((count, hidden), jnp.float32)] + sems * load,
         compiler_params=pltpu.CompilerParams(vmem_limit_bytes=16 << 20),
         cost_estimate=SMALL,
         name="score",
@@ -495,21 +529,21 @@
     pairs = lambda count, k: [(i, i ^ k) for i in range(count)]
     swap = pairs(mp, 1)
 
-    ups = [lax.all_gather(reward_up[0], "dp", axis=0)]
+    cut = reward_up.shape[1] * 4 // 5
+    rest = reward_up[0, cut:]
+    ups = [lax.all_gather(reward_up[0, :cut], "dp", axis=0)]
 
     blocks = dispatch(parents, child_count, child_parent, node_shard, tokens, reward_out, groups, capacity, hidden)
     keys = parent_keys.reshape(parents * prefix, kv_cols)
     values = parent_values.reshape(parents * prefix, kv_cols)
     raw = (w_query, w_key, w_value, keys, values, w_out)
     blocks, raw = lax.optimization_barrier((blocks, raw))
-    arrived = {0: blocks[0]}
-    for k in sorted(range(1, groups), key=lambda k: -(k ^ (k & 1))):
-        arrived[k] = lax.ppermute(blocks[k], "dp", pairs(groups, k))
-    blocks = [arrived[k] for k in range(groups)]
+    blocks = [blocks[0]] + [lax.ppermute(blocks[k], "dp", pairs(groups, k)) for k in range(1, groups)]
     blocks, weights = lax.optimization_barrier((blocks, load(*raw)))
     gain = attn_gain.reshape(1, width)
 
-    def run(offset, weights, blocks, ups, gain, child_parent, parent_blocks):
+    def run(offset, weights, blocks, ups, rests, gain, child_parent, parent_blocks):
+        rests = list(rests)
         row_own, notes, bias, scale, over = pack(
             offset, rows, hidden, prefix, parent_blocks, child_parent, blocks
         )
@@ -527,7 +561,7 @@
         scales = send([scale] * mp)
         for step in range(STEPS):
             part, attn, key_now, value_now, norm = expand(
-                step, row_own, row_peer, gain, w_query, w_key, w_value, keys, values, bias, w_out,
+                step, row_own, row_peer, begin(row_own, gain, w_query, w_key, w_value), gain, w_query, w_key, w_value, keys, values, bias, w_out,
                 past_keys, past_values,
             )
             norms.append(norm)
@@ -537,11 +571,16 @@
             chip = project_own(rows, attn, w_out) + from_peer.astype(jnp.float32)
             sent = chip.astype(jnp.bfloat16)
             others = [sent] + [lax.ppermute(sent, "mp", pairs(mp, k)) for k in range(2, mp, 2)]
+            if len(rests) < groups:
+                more = range(len(rests), min(groups, len(rests) - (1 - groups) // (STEPS - 1)))
+                more = [lax.ppermute(rests[0], "dp", pairs(groups, k)) for k in more]
+                others, more = lax.optimization_barrier((others, more))
+                rests += more
             if step == 0:
                 others, scales = lax.optimization_barrier((others, scales))
             if step + 1 == STEPS:
                 _, ups = lax.optimization_barrier((sent, ups))
-                before, ups = products(0, step, ups, True)
+                before, ups = products(0, step, [*ups, *rests], True)
                 others, before = lax.optimization_barrier((others, before))
             state = state + paired_sum([other.astype(jnp.float32) for other in others])
             row_own = state.astype(jnp.bfloat16)
@@ -552,11 +591,11 @@
         last, _ = products(step, STEPS, ups, False)
         last, over = lax.optimization_barrier((send(last * mp), over[0, 0]))
         before = send([finish(notes, scale, norms[1:], before)] * mp)
-        return place(groups, reward_cap, notes, row_own, row_peer, before, scales, last), over
-
-    operands = (blocks, ups, gain, child_parent, parent_blocks)
-
-    table, over = run(0, weights, *operands)
+        return place(groups, reward_cap, notes, row_own, row_peer, before, scales, last), over, rests
+
+    others = (gain, child_parent, parent_blocks)
+    table, over, rests = run(0, weights, blocks, ups, [rest], *others)
+    operands = (blocks, ups, rests, *others)
     if rows < slots:
         table, raw, operands = lax.optimization_barrier((table, raw, operands))
         again = lambda table, raw, operands: table + run(rows, load(*raw), *operands)[0]

time: 210 us -> 295 us (1.40)
  waiting for transfers between devices: 62.8 us -> 109 us
  local copies, waits for them, and re-layouts: 0.59 us -> 24.3 us
  starting transfers between devices: 38 us -> 47.4 us
  blocking collectives: 10.4 us -> 14.5 us
  other arithmetic: 1.99 us -> 5.14 us
    ppermute x7 -> x14, waiting for transfers between devices: 0.02 us -> 100 us  [the longest x7 100 us: run(): more = [lax.ppermute(rests[0], 'dp', pairs(groups, k)) for k in more]]
    ppermute x8, waiting for transfers between devices: 38.9 us -> 4.44 us  [run(): lax.ppermute(sent, 'mp', pairs(mp, k))]
    unnamed x34 -> x150, local copies, waits for them, and re-layouts: 0.07 us -> 21.4 us
    pallas_call x8, Pallas kernels: 44.3 us -> 33.2 us  [expand(): pl.pallas_call(functools.partial(step_kernel, step), out_shape=(struct((s...]
    ppermute x9, waiting for transfers between devices: 11.8 us -> 1.46 us  [run(): row_peer = lax.ppermute(row_own, 'mp', swap)]
    ppermute x7 -> x14, starting transfers between devices: 12.5 us -> 22.7 us  [the longest x7 12.5 us: shards(): lax.ppermute(blocks[k], 'dp', pairs(groups, k))]
    pallas_call x2 -> x10, Pallas kernels: 9.24 us -> 18.9 us  [the longest x8 9.99 us: begin(): pl.pallas_call(begin_kernel, out_shape=struct((slots, w_query.shape[1] +...]
    ppermute x12, waiting for transfers between devices: 7.47 us -> 2.2 us  [run(): lax.ppermute(sums[k], 'mp', pairs(mp, k))]
  transfers between devices with their start and end apart: 45 -> 52, of which waited for: 26 -> 18; matrix products, arithmetic and copies ran while one was open for 1% -> 3% of each run, Pallas kernels for 37% -> 23%
where the time goes in v3:
time: 295 us; the launch traced here: 291 us
  waiting for transfers between devices  109 us (37%)
  Pallas kernels  74 us (25%)
  starting transfers between devices  47.4 us (16%)
  local copies, waits for them, and re-layouts  24.3 us (8%)
  between operations  15.9 us (5%)
  blocking collectives  14.5 us (5%)
  other arithmetic  5.14 us (2%)
    ppermute x7, waiting for transfers between devices, run(): more = [lax.ppermute(rests[0], 'dp', pairs(groups, k)) for k in more]  100 us
    pallas_call x8, Pallas kernels, expand(): pl.pallas_call(functools.partial(step_kernel, step), out_shape=(struct((s...  33.2 us
    unnamed x150, local copies, waits for them, and re-layouts  21.4 us
    all_to_all x1, blocking collectives, shards(): table = lax.all_to_all(table, 'dp', split_axis=0, concat_axis=0, tiled=True)  14.5 us
    ppermute x8, starting transfers between devices, run(): lax.ppermute(sent, 'mp', pairs(mp, k))  13 us
    ppermute x7, starting transfers between devices, shards(): lax.ppermute(blocks[k], 'dp', pairs(groups, k))  12.5 us
    pallas_call x8, Pallas kernels, project_own(): pl.pallas_call(project_kernel, out_shape=struct((rows, w_out.shape[1] //...  10.3 us
    ppermute x7, starting transfers between devices, run(): more = [lax.ppermute(rests[0], 'dp', pairs(groups, k)) for k in more]  10.2 us
  transfers between devices with their start and end apart: 52, of which 18 were waited for; matrix products, arithmetic and copies ran while one was open for 3% of the time, Pallas kernels for 23%

profile of v3, /device:TPU:0, one launch (start us, length us, event | category | flops | bytes accessed | tf_op | source)
XLA Modules:
  0.0 291.2 jit_solution(12375037520470231681)
XLA Ops:
  8.7 3.0 %collective-permute-start.37 = (bf16[8,3072]{1,0:T(8,128)(2,1)S(1)}, bf16[8,3072]{1,0:T(8,128)(2,1)S(1)}, u32[]{:S(2)}, u32[]{:S(2)}) collective-permute-start(bf16[8,3072]{1,0:T(8,128)(2,1)S(1)} %get-tuple-element.325), channel_id=1, source_target_pairs={{0,4},{4,0},{8,12},{12,8},{16,20},{20,16},{24,28},{28,24},{1,5},{5... | collective-permute-start | bytes 147464 | tf_op jit(solution)/shard_map/ppermute | solution.py:541
  13.3 3.0 %collective-permute-start.40 = (bf16[8,3072]{1,0:T(8,128)(2,1)S(1)}, bf16[8,3072]{1,0:T(8,128)(2,1)S(1)}, u32[]{:S(2)}, u32[]{:S(2)}) collective-permute-start(bf16[8,3072]{1,0:T(8,128)(2,1)S(1)} %get-tuple-element.328), channel_id=1, source_target_pairs={{0,16},{4,20},{8,24},{12,28},{16,0},{20,4},{24,8},{28,12},{1,17},{... | collective-permute-start | bytes 147464 | tf_op jit(solution)/shard_map/ppermute | solution.py:541
  17.6 3.6 %collective-permute-start.42 = (bf16[8,3072]{1,0:T(8,128)(2,1)S(1)}, bf16[8,3072]{1,0:T(8,128)(2,1)S(1)}, u32[]{:S(2)}, u32[]{:S(2)}) collective-permute-start(bf16[8,3072]{1,0:T(8,128)(2,1)S(1)} %get-tuple-element.330), channel_id=1, source_target_pairs={{0,24},{4,28},{8,16},{12,20},{16,8},{20,12},{24,0},{28,4},{1,25},{... | collective-permute-start | bytes 147464 | tf_op jit(solution)/shard_map/ppermute | solution.py:541
  21.2 7.6 %load.3 = (bf16[5120,768]{1,0:T(8,128)(2,1)S(1)}, bf16[5120,256]{1,0:T(8,128)(2,1)S(1)}, bf16[5120,256]{1,0:T(8,128)(2,1)S(1)}, bf16[2048,256]{1,0:T(8,128)(2,1)...) custom-call(bf16[5120,768]{1,0:T(8,128)(2,1)} %refs_0_, bf16[5120,256]{1,0:T(8,128)(2,1)} %refs_1_, ...), custom_call_target="tpu_custom_call" | custom-call | bytes 25165824 | tf_op jit(solution)/shard_map/load/pallas_call | solution.py:219
  31.6 4.6 %expand.24 = (bf16[48,2560]{1,0:T(8,128)(2,1)S(1)}, bf16[64,768]{1,0:T(8,128)(2,1)S(1)}, bf16[48,256]{1,0:T(8,128)(2,1)S(1)}, bf16[48,256]{1,0:T(8,128)(2,1)S(1)}, f32[48,128]{1,0:T(8,128)}) custom-call(bf16[48,2560]{1,0:T(8,128)(2,1)S(1)} %get-tuple-element.353.own, bf16[48,2560]{1,0:T(8,128)(2,1)S(1)} %collective-permute-done.44.peer, ...), custom_call_target="tpu_custom_call" | custom-call | tf_op jit(solution)/shard_map/expand/pallas_call | solution.py:330
  36.2 3.2 %copy-done.1 = bf16[5120,768]{1,0:T(8,128)(2,1)} copy-done((bf16[5120,768]{1,0:T(8,128)(2,1)}, bf16[5120,768]{1,0:T(8,128)(2,1)S(1)}, u32[]{:S(2)}) %copy-start.1) | copy-done | bytes 7864344
  49.1 3.2 %collective-permute-done.46 = bf16[48,2560]{1,0:T(8,128)(2,1)} collective-permute-done((bf16[48,2560]{1,0:T(8,128)(2,1)}, bf16[48,2560]{1,0:T(8,128)(2,1)}, u32[]{:S(2)}, u32[]{:S(2)}) %collective-permute-start.46) | collective-permute-done | bytes 245792 | tf_op jit(solution)/shard_map/ppermute | solution.py:573
  55.7 4.5 %copy-done.2 = bf16[5120,768]{1,0:T(8,128)(2,1)S(1)} copy-done((bf16[5120,768]{1,0:T(8,128)(2,1)S(1)}, bf16[5120,768]{1,0:T(8,128)(2,1)}, u32[]{:S(2)}) %copy-start.2) | copy-done | bytes 7864344
  64.4 3.3 %copy-done.3 = bf16[5120,768]{1,0:T(8,128)(2,1)S(1)} copy-done((bf16[5120,768]{1,0:T(8,128)(2,1)S(1)}, bf16[5120,768]{1,0:T(8,128)(2,1)}, u32[]{:S(2)}) %copy-start.3) | copy-done | bytes 7864344
  67.6 3.9 %expand.25 = (bf16[48,2560]{1,0:T(8,128)(2,1)S(1)}, bf16[64,768]{1,0:T(8,128)(2,1)S(1)}, bf16[48,256]{1,0:T(8,128)(2,1)S(1)}, bf16[48,256]{1,0:T(8,128)(2,1)S(1)}, f32[48,128]{1,0:T(8,128)S(1)}) custom-call(bf16[48,2560]{1,0:T(8,128)(2,1)S(1)} %fusion.4.own.refs_9_, bf16[48,2560]{1,0:T(8,128)(2,1)S(1)} %collective-permute-done.51.peer.refs_16_, ...), custom_call_target="tpu_custom_call" | custom-call | tf_op jit(solution)/shard_map/expand/pallas_call | solution.py:330
  75.1 21.2 %collective-permute-done.54.refs_3_ = bf16[256,512]{1,0:T(8,128)(2,1)S(1)} collective-permute-done((bf16[256,512]{1,0:T(8,128)(2,1)}, bf16[256,512]{1,0:T(8,128)(2,1)S(1)}, u32[]{:S(2)}, u32[]{:S(2)}) %collective-permute-start.54) | collective-permute-done | bytes 262176 | tf_op jit(solution)/shard_map/ppermute | solution.py:576
  99.9 3.9 %expand.26 = (bf16[48,2560]{1,0:T(8,128)(2,1)S(1)}, bf16[64,768]{1,0:T(8,128)(2,1)S(1)}, bf16[48,256]{1,0:T(8,128)(2,1)S(1)}, bf16[48,256]{1,0:T(8,128)(2,1)S(1)}, f32[48,128]{1,0:T(8,128)S(1)}) custom-call(bf16[48,2560]{1,0:T(8,128)(2,1)S(1)} %get-tuple-element.482.own.refs_10_, bf16[48,2560]{1,0:T(8,128)(2,1)S(1)} %collective-permute-done.55.peer.refs_17_, ...), custom_call_target="tpu_custom_call" | custom-call | tf_op jit(solution)/shard_map/expand/pallas_call | solution.py:330
  107.9 26.0 %collective-permute-done.58.refs_4_ = bf16[256,512]{1,0:T(8,128)(2,1)S(1)} collective-permute-done((bf16[256,512]{1,0:T(8,128)(2,1)}, bf16[256,512]{1,0:T(8,128)(2,1)S(1)}, u32[]{:S(2)}, u32[]{:S(2)}) %collective-permute-start.58) | collective-permute-done | bytes 262176 | tf_op jit(solution)/shard_map/ppermute | solution.py:576
  136.1 4.4 %expand.27 = (bf16[48,2560]{1,0:T(8,128)(2,1)S(1)}, bf16[64,768]{1,0:T(8,128)(2,1)S(1)}, bf16[48,256]{1,0:T(8,128)(2,1)S(1)}, bf16[48,256]{1,0:T(8,128)(2,1)S(1)}, f32[48,128]{1,0:T(8,128)S(1)}) custom-call(bf16[48,2560]{1,0:T(8,128)(2,1)S(1)} %fusion.5.own.refs_11_, bf16[48,2560]{1,0:T(8,128)(2,1)S(1)} %collective-permute-done.59.peer.refs_18_, ...), custom_call_target="tpu_custom_call" | custom-call | tf_op jit(solution)/shard_map/expand/pallas_call | solution.py:330
  141.4 2.7 collective-permute-start.62
  146.8 22.4 %collective-permute-done.62.refs_5_ = bf16[256,512]{1,0:T(8,128)(2,1)S(1)} collective-permute-done((bf16[256,512]{1,0:T(8,128)(2,1)}, bf16[256,512]{1,0:T(8,128)(2,1)S(1)}, u32[]{:S(2)}, u32[]{:S(2)}) %collective-permute-start.62) | collective-permute-done | bytes 262176 | tf_op jit(solution)/shard_map/ppermute | solution.py:576
  171.4 3.9 %expand.28 = (bf16[48,2560]{1,0:T(8,128)(2,1)S(1)}, bf16[64,768]{1,0:T(8,128)(2,1)S(1)}, bf16[48,256]{1,0:T(8,128)(2,1)S(1)}, bf16[48,256]{1,0:T(8,128)(2,1)S(1)}, f32[48,128]{1,0:T(8,128)S(1)}) custom-call(bf16[48,2560]{1,0:T(8,128)(2,1)S(1)} %get-tuple-element.480.own.refs_12_, bf16[48,2560]{1,0:T(8,128)(2,1)S(1)} %collective-permute-done.63.peer.refs_19_, ...), custom_call_target="tpu_custom_call" | custom-call | tf_op jit(solution)/shard_map/expand/pallas_call | solution.py:330
  177.7 1.9 collective-permute-start.65
  179.6 19.9 %collective-permute-done.66.refs_6_ = bf16[256,512]{1,0:T(8,128)(2,1)S(1)} collective-permute-done((bf16[256,512]{1,0:T(8,128)(2,1)}, bf16[256,512]{1,0:T(8,128)(2,1)S(1)}, u32[]{:S(2)}, u32[]{:S(2)}) %collective-permute-start.66) | collective-permute-done | bytes 262176 | tf_op jit(solution)/shard_map/ppermute | solution.py:576
  201.8 4.0 %expand.29 = (bf16[48,2560]{1,0:T(8,128)(2,1)S(1)}, bf16[64,768]{1,0:T(8,128)(2,1)S(1)}, bf16[48,256]{1,0:T(8,128)(2,1)S(1)}, bf16[48,256]{1,0:T(8,128)(2,1)S(1)}, f32[48,128]{1,0:T(8,128)S(1)}) custom-call(bf16[48,2560]{1,0:T(8,128)(2,1)S(1)} %fusion.6.own.refs_13_, bf16[48,2560]{1,0:T(8,128)(2,1)S(1)} %collective-permute-done.67.peer.refs_20_, ...), custom_call_target="tpu_custom_call" | custom-call | tf_op jit(solution)/shard_map/expand/pallas_call | solution.py:330
  206.1 3.0 %collective-permute-start.70 = (bf16[256,512]{1,0:T(8,128)(2,1)}, bf16[256,512]{1,0:T(8,128)(2,1)S(1)}, u32[]{:S(2)}, u32[]{:S(2)}) collective-permute-start(bf16[256,512]{1,0:T(8,128)(2,1)} %slice_bitcast_fusion.refs_1_), channel_id=1, source_target_pairs={{0,24},{4,28},{8,16},{12,20},{16,8},{20,12},{24,0},{28,4},{1,25},{... | collective-permute-start | bytes 786440 | tf_op jit(solution)/shard_map/ppermute | solution.py:576
  212.2 4.4 %collective-permute-done.70.refs_7_ = bf16[256,512]{1,0:T(8,128)(2,1)S(1)} collective-permute-done((bf16[256,512]{1,0:T(8,128)(2,1)}, bf16[256,512]{1,0:T(8,128)(2,1)S(1)}, u32[]{:S(2)}, u32[]{:S(2)}) %collective-permute-start.70) | collective-permute-done | bytes 262176 | tf_op jit(solution)/shard_map/ppermute | solution.py:576
  220.2 4.2 %expand.30 = (bf16[48,2560]{1,0:T(8,128)(2,1)S(1)}, bf16[64,768]{1,0:T(8,128)(2,1)S(1)}, bf16[48,256]{1,0:T(8,128)(2,1)S(1)}, bf16[48,256]{1,0:T(8,128)(2,1)S(1)}, f32[48,128]{1,0:T(8,128)S(1)}) custom-call(bf16[48,2560]{1,0:T(8,128)(2,1)S(1)} %get-tuple-element.478.own.refs_14_, bf16[48,2560]{1,0:T(8,128)(2,1)S(1)} %collective-permute-done.71.peer.refs_21_, ...), custom_call_target="tpu_custom_call" | custom-call | tf_op jit(solution)/shard_map/expand/pallas_call | solution.py:330
  224.7 2.4 collective-permute-start.74
  228.5 1.8 collective-permute-start.73
  230.3 5.9 %collective-permute-done.74.refs_8_ = bf16[256,512]{1,0:T(8,128)(2,1)S(1)} collective-permute-done((bf16[256,512]{1,0:T(8,128)(2,1)}, bf16[256,512]{1,0:T(8,128)(2,1)S(1)}, u32[]{:S(2)}, u32[]{:S(2)}) %collective-permute-start.74) | collective-permute-done | bytes 262176 | tf_op jit(solution)/shard_map/ppermute | solution.py:576
  238.4 4.4 %expand.31 = (bf16[48,2560]{1,0:T(8,128)(2,1)S(1)}, bf16[64,768]{1,0:T(8,128)(2,1)S(1)}, bf16[48,256]{1,0:T(8,128)(2,1)}, bf16[48,256]{1,0:T(8,128)(2,1)}, f32[48,128]{1,0:T(8,128)S(1)}) custom-call(bf16[48,2560]{1,0:T(8,128)(2,1)S(1)} %fusion.7.own.refs_15_, bf16[48,2560]{1,0:T(8,128)(2,1)S(1)} %collective-permute-done.75.peer.refs_22_, ...), custom_call_target="tpu_custom_call" | custom-call | tf_op jit(solution)/shard_map/expand/pallas_call | solution.py:330
  246.2 7.0 %score.6 = (bf16[336,128]{1,0:T(8,128)(2,1)S(1)}, bf16[336,128]{1,0:T(8,128)(2,1)S(1)}, bf16[336,128]{1,0:T(8,128)(2,1)S(1)}, bf16[336,128]{1,0:T(8,128)(2,1)S(1...) custom-call(f32[48,128]{1,0:T(8,128)S(1)} %copy-done.41, ...), custom_call_target="tpu_custom_call" | custom-call | tf_op jit(solution)/shard_map/score/pallas_call | solution.py:426
  254.3 1.8 collective-permute-start.83
  256.3 2.0 score.7.refs_8_
  258.2 1.7 collective-permute-start.81
  269.0 14.5 %all_to_all.9 = f32[8,8,128]{2,1,0:T(8,128)S(1)} all-to-all(f32[8,8,128]{2,1,0:T(8,128)S(1)} %bitcast.34), channel_id=1, replica_groups=mesh['dp'=8,'mp'=4] {'dp'}, dimensions={0} | all-to-all | bytes 65536 | tf_op jit(solution)/shard_map/all_to_all | solution.py:604
  (277 shorter events, 72.1 us)
Async XLA Ops:
  6.5 239.7 %all-gather.2.cloned.1.call-start = ((), (), s32[]{:S(2)}) async-start(), calls=%async_computation.1 | async-start | bytes 9437184 | tf_op jit(solution)/shard_map/all_gather | solution.py:534
  8.7 8.9 %collective-permute-start.37 = (bf16[8,3072]{1,0:T(8,128)(2,1)S(1)}, bf16[8,3072]{1,0:T(8,128)(2,1)S(1)}, u32[]{:S(2)}, u32[]{:S(2)}) collective-permute-start(bf16[8,3072]{1,0:T(8,128)(2,1)S(1)} %get-tuple-element.325), channel_id=1, source_target_pairs={{0,4},{4,0},{8,12},{12,8},{16,20},{20,16},{24,28},{28,24},{1,5},{5... | collective-permute-start | bytes 147464 | tf_op jit(solution)/shard_map/ppermute | solution.py:541
  11.8 9.5 %collective-permute-start.38 = (bf16[8,3072]{1,0:T(8,128)(2,1)S(1)}, bf16[8,3072]{1,0:T(8,128)(2,1)S(1)}, u32[]{:S(2)}, u32[]{:S(2)}) collective-permute-start(bf16[8,3072]{1,0:T(8,128)(2,1)S(1)} %get-tuple-element.326), channel_id=1, source_target_pairs={{0,8},{4,12},{8,0},{12,4},{16,24},{20,28},{24,16},{28,20},{1,9},{5... | collective-permute-start | bytes 147464 | tf_op jit(solution)/shard_map/ppermute | solution.py:541
  13.3 15.6 %collective-permute-start.39 = (bf16[8,3072]{1,0:T(8,128)(2,1)S(1)}, bf16[8,3072]{1,0:T(8,128)(2,1)S(1)}, u32[]{:S(2)}, u32[]{:S(2)}) collective-permute-start(bf16[8,3072]{1,0:T(8,128)(2,1)S(1)} %get-tuple-element.327), channel_id=1, source_target_pairs={{0,12},{4,8},{8,4},{12,0},{16,28},{20,24},{24,20},{28,16},{1,13},{... | collective-permute-start | bytes 147464 | tf_op jit(solution)/shard_map/ppermute | solution.py:541
  13.3 15.6 %collective-permute-start.40 = (bf16[8,3072]{1,0:T(8,128)(2,1)S(1)}, bf16[8,3072]{1,0:T(8,128)(2,1)S(1)}, u32[]{:S(2)}, u32[]{:S(2)}) collective-permute-start(bf16[8,3072]{1,0:T(8,128)(2,1)S(1)} %get-tuple-element.328), channel_id=1, source_target_pairs={{0,16},{4,20},{8,24},{12,28},{16,0},{20,4},{24,8},{28,12},{1,17},{... | collective-permute-start | bytes 147464 | tf_op jit(solution)/shard_map/ppermute | solution.py:541
  16.3 12.6 %collective-permute-start.41 = (bf16[8,3072]{1,0:T(8,128)(2,1)S(1)}, bf16[8,3072]{1,0:T(8,128)(2,1)S(1)}, u32[]{:S(2)}, u32[]{:S(2)}) collective-permute-start(bf16[8,3072]{1,0:T(8,128)(2,1)S(1)} %get-tuple-element.329), channel_id=1, source_target_pairs={{0,20},{4,16},{8,28},{12,24},{16,4},{20,0},{24,12},{28,8},{1,21},{... | collective-permute-start | bytes 147464 | tf_op jit(solution)/shard_map/ppermute | solution.py:541
  17.6 11.3 %collective-permute-start.42 = (bf16[8,3072]{1,0:T(8,128)(2,1)S(1)}, bf16[8,3072]{1,0:T(8,128)(2,1)S(1)}, u32[]{:S(2)}, u32[]{:S(2)}) collective-permute-start(bf16[8,3072]{1,0:T(8,128)(2,1)S(1)} %get-tuple-element.330), channel_id=1, source_target_pairs={{0,24},{4,28},{8,16},{12,20},{16,8},{20,12},{24,0},{28,4},{1,25},{... | collective-permute-start | bytes 147464 | tf_op jit(solution)/shard_map/ppermute | solution.py:541
  21.2 7.7 %collective-permute-start.43 = (bf16[8,3072]{1,0:T(8,128)(2,1)S(1)}, bf16[8,3072]{1,0:T(8,128)(2,1)S(1)}, u32[]{:S(2)}, u32[]{:S(2)}) collective-permute-start(bf16[8,3072]{1,0:T(8,128)(2,1)S(1)} %get-tuple-element.331), channel_id=1, source_target_pairs={{0,28},{4,24},{8,20},{12,16},{16,12},{20,8},{24,4},{28,0},{1,29},{... | collective-permute-start | bytes 147464 | tf_op jit(solution)/shard_map/ppermute | solution.py:541
  40.4 8.7 %collective-permute-start.47 = (bf16[256,512]{1,0:T(8,128)(2,1)}, bf16[256,512]{1,0:T(8,128)(2,1)}, u32[]{:S(2)}, u32[]{:S(2)}) collective-permute-start(bf16[256,512]{1,0:T(8,128)(2,1)} %slice_bitcast_fusion.refs_1_), channel_id=1, source_target_pairs={{0,4},{4,0},{8,12},{12,8},{16,20},{20,16},{24,28},{28,24},{1,5},{5... | collective-permute-start | bytes 786440 | tf_op jit(solution)/shard_map/ppermute | solution.py:576
  44.1 8.2 %collective-permute-start.46 = (bf16[48,2560]{1,0:T(8,128)(2,1)}, bf16[48,2560]{1,0:T(8,128)(2,1)}, u32[]{:S(2)}, u32[]{:S(2)}) collective-permute-start(bf16[48,2560]{1,0:T(8,128)(2,1)} %add_convert_fusion.17), channel_id=1, source_target_pairs={{0,2},{1,3},{2,0},{3,1},{4,6},{5,7},{6,4},{7,5},{8,10},{9,11},{10,... | collective-permute-start | bytes 737288 | tf_op jit(solution)/shard_map/ppermute | solution.py:573
  45.6 6.7 %collective-permute-start.50 = (f32[8,128]{1,0:T(8,128)S(1)}, f32[8,128]{1,0:T(8,128)S(1)}, u32[]{:S(2)}, u32[]{:S(2)}) collective-permute-start(f32[8,128]{1,0:T(8,128)S(1)} %get-tuple-element.437.scale.refs_4_), channel_id=1, source_target_pairs={{0,3},{1,2},{2,1},{3,0},{4,7},{5,6},{6,5},{7,4},{8,11},{9,10},{10,... | collective-permute-start | bytes 12296 | tf_op jit(solution)/shard_map/ppermute | solution.py:560
  45.6 7.3 %collective-permute-start.49 = (f32[8,128]{1,0:T(8,128)S(1)}, f32[8,128]{1,0:T(8,128)S(1)}, u32[]{:S(2)}, u32[]{:S(2)}) collective-permute-start(f32[8,128]{1,0:T(8,128)S(1)} %get-tuple-element.437.scale.refs_4_), channel_id=1, source_target_pairs={{0,2},{1,3},{2,0},{3,1},{4,6},{5,7},{6,4},{7,5},{8,10},{9,11},{10,... | collective-permute-start | bytes 12296 | tf_op jit(solution)/shard_map/ppermute | solution.py:560
  46.9 6.6 %collective-permute-start.48 = (f32[8,128]{1,0:T(8,128)S(1)}, f32[8,128]{1,0:T(8,128)S(1)}, u32[]{:S(2)}, u32[]{:S(2)}) collective-permute-start(f32[8,128]{1,0:T(8,128)S(1)} %get-tuple-element.437.scale.refs_4_), channel_id=1, source_target_pairs={{0,1},{1,0},{2,3},{3,2},{4,5},{5,4},{6,7},{7,6},{8,9},{9,8},{10,11... | collective-permute-start | bytes 12296 | tf_op jit(solution)/shard_map/ppermute | solution.py:560
  55.5 7.7 %collective-permute-start.51 = (bf16[48,2560]{1,0:T(8,128)(2,1)S(1)}, bf16[48,2560]{1,0:T(8,128)(2,1)S(1)}, u32[]{:S(2)}, u32[]{:S(2)}) collective-permute-start(bf16[48,2560]{1,0:T(8,128)(2,1)S(1)} %fusion.4.own.refs_9_), channel_id=1, source_target_pairs={{0,1},{1,0},{2,3},{3,2},{4,5},{5,4},{6,7},{7,6},{8,9},{9,8},{10,11... | collective-permute-start | bytes 737288 | tf_op jit(solution)/shard_map/ppermute | solution.py:587
  72.1 24.2 %collective-permute-start.54 = (bf16[256,512]{1,0:T(8,128)(2,1)}, bf16[256,512]{1,0:T(8,128)(2,1)S(1)}, u32[]{:S(2)}, u32[]{:S(2)}) collective-permute-start(bf16[256,512]{1,0:T(8,128)(2,1)} %slice_bitcast_fusion.refs_1_), channel_id=1, source_target_pairs={{0,8},{4,12},{8,0},{12,4},{16,24},{20,28},{24,16},{28,20},{1,9},{5... | collective-permute-start | bytes 786440 | tf_op jit(solution)/shard_map/ppermute | solution.py:576
  73.5 23.5 %collective-permute-start.53 = (bf16[48,2560]{1,0:T(8,128)(2,1)S(1)}, bf16[48,2560]{1,0:T(8,128)(2,1)S(1)}, u32[]{:S(2)}, u32[]{:S(2)}) collective-permute-start(bf16[48,2560]{1,0:T(8,128)(2,1)S(1)} %add_convert_fusion.16), channel_id=1, source_target_pairs={{0,2},{1,3},{2,0},{3,1},{4,6},{5,7},{6,4},{7,5},{8,10},{9,11},{10,... | collective-permute-start | bytes 737288 | tf_op jit(solution)/shard_map/ppermute | solution.py:573
  104.7 29.2 %collective-permute-start.58 = (bf16[256,512]{1,0:T(8,128)(2,1)}, bf16[256,512]{1,0:T(8,128)(2,1)S(1)}, u32[]{:S(2)}, u32[]{:S(2)}) collective-permute-start(bf16[256,512]{1,0:T(8,128)(2,1)} %slice_bitcast_fusion.refs_1_), channel_id=1, source_target_pairs={{0,12},{4,8},{8,4},{12,0},{16,28},{20,24},{24,20},{28,16},{1,13},{... | collective-permute-start | bytes 786440 | tf_op jit(solution)/shard_map/ppermute | solution.py:576
  106.3 27.5 %collective-permute-start.57 = (bf16[48,2560]{1,0:T(8,128)(2,1)S(1)}, bf16[48,2560]{1,0:T(8,128)(2,1)S(1)}, u32[]{:S(2)}, u32[]{:S(2)}) collective-permute-start(bf16[48,2560]{1,0:T(8,128)(2,1)S(1)} %add_convert_fusion.15), channel_id=1, source_target_pairs={{0,2},{1,3},{2,0},{3,1},{4,6},{5,7},{6,4},{7,5},{8,10},{9,11},{10,... | collective-permute-start | bytes 737288 | tf_op jit(solution)/shard_map/ppermute | solution.py:573
  141.4 27.8 %collective-permute-start.62 = (bf16[256,512]{1,0:T(8,128)(2,1)}, bf16[256,512]{1,0:T(8,128)(2,1)S(1)}, u32[]{:S(2)}, u32[]{:S(2)}) collective-permute-start(bf16[256,512]{1,0:T(8,128)(2,1)} %slice_bitcast_fusion.refs_1_), channel_id=1, source_target_pairs={{0,16},{4,20},{8,24},{12,28},{16,0},{20,4},{24,8},{28,12},{1,17},{... | collective-permute-start | bytes 786440 | tf_op jit(solution)/shard_map/ppermute | solution.py:576
  145.5 23.7 %collective-permute-start.61 = (bf16[48,2560]{1,0:T(8,128)(2,1)S(1)}, bf16[48,2560]{1,0:T(8,128)(2,1)S(1)}, u32[]{:S(2)}, u32[]{:S(2)}) collective-permute-start(bf16[48,2560]{1,0:T(8,128)(2,1)S(1)} %add_convert_fusion.14), channel_id=1, source_target_pairs={{0,2},{1,3},{2,0},{3,1},{4,6},{5,7},{6,4},{7,5},{8,10},{9,11},{10,... | collective-permute-start | bytes 737288 | tf_op jit(solution)/shard_map/ppermute | solution.py:573
  176.3 23.2 %collective-permute-start.66 = (bf16[256,512]{1,0:T(8,128)(2,1)}, bf16[256,512]{1,0:T(8,128)(2,1)S(1)}, u32[]{:S(2)}, u32[]{:S(2)}) collective-permute-start(bf16[256,512]{1,0:T(8,128)(2,1)} %slice_bitcast_fusion.refs_1_), channel_id=1, source_target_pairs={{0,20},{4,16},{8,28},{12,24},{16,4},{20,0},{24,12},{28,8},{1,21},{... | collective-permute-start | bytes 786440 | tf_op jit(solution)/shard_map/ppermute | solution.py:576
  177.7 21.8 %collective-permute-start.65 = (bf16[48,2560]{1,0:T(8,128)(2,1)S(1)}, bf16[48,2560]{1,0:T(8,128)(2,1)S(1)}, u32[]{:S(2)}, u32[]{:S(2)}) collective-permute-start(bf16[48,2560]{1,0:T(8,128)(2,1)S(1)} %add_convert_fusion.13), channel_id=1, source_target_pairs={{0,2},{1,3},{2,0},{3,1},{4,6},{5,7},{6,4},{7,5},{8,10},{9,11},{10,... | collective-permute-start | bytes 737288 | tf_op jit(solution)/shard_map/ppermute | solution.py:573
  206.1 10.5 %collective-permute-start.70 = (bf16[256,512]{1,0:T(8,128)(2,1)}, bf16[256,512]{1,0:T(8,128)(2,1)S(1)}, u32[]{:S(2)}, u32[]{:S(2)}) collective-permute-start(bf16[256,512]{1,0:T(8,128)(2,1)} %slice_bitcast_fusion.refs_1_), channel_id=1, source_target_pairs={{0,24},{4,28},{8,16},{12,20},{16,8},{20,12},{24,0},{28,4},{1,25},{... | collective-permute-start | bytes 786440 | tf_op jit(solution)/shard_map/ppermute | solution.py:576
  210.5 7.9 %collective-permute-start.69 = (bf16[48,2560]{1,0:T(8,128)(2,1)S(1)}, bf16[48,2560]{1,0:T(8,128)(2,1)S(1)}, u32[]{:S(2)}, u32[]{:S(2)}) collective-permute-start(bf16[48,2560]{1,0:T(8,128)(2,1)S(1)} %add_convert_fusion.12), channel_id=1, source_target_pairs={{0,2},{1,3},{2,0},{3,1},{4,6},{5,7},{6,4},{7,5},{8,10},{9,11},{10,... | collective-permute-start | bytes 737288 | tf_op jit(solution)/shard_map/ppermute | solution.py:573
  224.7 11.4 %collective-permute-start.74 = (bf16[256,512]{1,0:T(8,128)(2,1)}, bf16[256,512]{1,0:T(8,128)(2,1)S(1)}, u32[]{:S(2)}, u32[]{:S(2)}) collective-permute-start(bf16[256,512]{1,0:T(8,128)(2,1)} %slice_bitcast_fusion.refs_1_), channel_id=1, source_target_pairs={{0,28},{4,24},{8,20},{12,16},{16,12},{20,8},{24,4},{28,0},{1,29},{... | collective-permute-start | bytes 786440 | tf_op jit(solution)/shard_map/ppermute | solution.py:576
  228.5 7.8 %collective-permute-start.73 = (bf16[48,2560]{1,0:T(8,128)(2,1)S(1)}, bf16[48,2560]{1,0:T(8,128)(2,1)S(1)}, u32[]{:S(2)}, u32[]{:S(2)}) collective-permute-start(bf16[48,2560]{1,0:T(8,128)(2,1)S(1)} %add_convert_fusion.11), channel_id=1, source_target_pairs={{0,2},{1,3},{2,0},{3,1},{4,6},{5,7},{6,4},{7,5},{8,10},{9,11},{10,... | collective-permute-start | bytes 737288 | tf_op jit(solution)/shard_map/ppermute | solution.py:573
  244.5 8.7 %collective-permute-start.77 = (bf16[48,2560]{1,0:T(8,128)(2,1)S(1)}, bf16[48,2560]{1,0:T(8,128)(2,1)S(1)}, u32[]{:S(2)}, u32[]{:S(2)}) collective-permute-start(bf16[48,2560]{1,0:T(8,128)(2,1)S(1)} %add_convert_fusion.10), channel_id=1, source_target_pairs={{0,2},{1,3},{2,0},{3,1},{4,6},{5,7},{6,4},{7,5},{8,10},{9,11},{10,... | collective-permute-start | bytes 737288 | tf_op jit(solution)/shard_map/ppermute | solution.py:573
  254.2 6.0 %collective-permute-start.82 = (bf16[336,128]{1,0:T(8,128)(2,1)S(1)}, bf16[336,128]{1,0:T(8,128)(2,1)S(1)}, u32[]{:S(2)}, u32[]{:S(2)}) collective-permute-start(bf16[336,128]{1,0:T(8,128)(2,1)S(1)} %get-tuple-element.434), channel_id=1, source_target_pairs={{0,1},{1,0},{2,3},{3,2},{4,5},{5,4},{6,7},{7,6},{8,9},{9,8},{10,11... | collective-permute-start | bytes 258056 | tf_op jit(solution)/shard_map/ppermute | solution.py:560
  254.3 5.9 %collective-permute-start.83 = (bf16[336,128]{1,0:T(8,128)(2,1)S(1)}, bf16[336,128]{1,0:T(8,128)(2,1)S(1)}, u32[]{:S(2)}, u32[]{:S(2)}) collective-permute-start(bf16[336,128]{1,0:T(8,128)(2,1)S(1)} %get-tuple-element.435), channel_id=1, source_target_pairs={{0,2},{1,3},{2,0},{3,1},{4,6},{5,7},{6,4},{7,5},{8,10},{9,11},{10,... | collective-permute-start | bytes 258056 | tf_op jit(solution)/shard_map/ppermute | solution.py:560
  256.1 4.8 %collective-permute-start.84 = (bf16[336,128]{1,0:T(8,128)(2,1)S(1)}, bf16[336,128]{1,0:T(8,128)(2,1)S(1)}, u32[]{:S(2)}, u32[]{:S(2)}) collective-permute-start(bf16[336,128]{1,0:T(8,128)(2,1)S(1)} %get-tuple-element.436), channel_id=1, source_target_pairs={{0,3},{1,2},{2,1},{3,0},{4,7},{5,6},{6,5},{7,4},{8,11},{9,10},{10,... | collective-permute-start | bytes 258056 | tf_op jit(solution)/shard_map/ppermute | solution.py:560
  258.2 5.3 %collective-permute-start.81 = (bf16[48,512]{1,0:T(8,128)(2,1)S(1)}, bf16[48,512]{1,0:T(8,128)(2,1)S(1)}, u32[]{:S(2)}, u32[]{:S(2)}) collective-permute-start(bf16[48,512]{1,0:T(8,128)(2,1)S(1)} %score.7.refs_8_), channel_id=1, source_target_pairs={{0,3},{1,2},{2,1},{3,0},{4,7},{5,6},{6,5},{7,4},{8,11},{9,10},{10,... | collective-permute-start | bytes 147464 | tf_op jit(solution)/shard_map/ppermute | solution.py:560
  260.0 4.9 %collective-permute-start.80 = (bf16[48,512]{1,0:T(8,128)(2,1)S(1)}, bf16[48,512]{1,0:T(8,128)(2,1)S(1)}, u32[]{:S(2)}, u32[]{:S(2)}) collective-permute-start(bf16[48,512]{1,0:T(8,128)(2,1)S(1)} %score.7.refs_8_), channel_id=1, source_target_pairs={{0,2},{1,3},{2,0},{3,1},{4,6},{5,7},{6,4},{7,5},{8,10},{9,11},{10,... | collective-permute-start | bytes 147464 | tf_op jit(solution)/shard_map/ppermute | solution.py:560
  (95 other events, 459.8 us)
Sparse Core Ops, SparseCore 0:
  48.7 149.2 all-gather.1

commit v4 on v3

--- a/solution.py
+++ b/solution.py
@@ -50,6 +50,10 @@
     while len(parts) > 1:
         parts = [a + b for a, b in zip(parts[::2], parts[1::2])]
     return parts[0]
+
+
+def ring_order(groups):
+    return list(range(0, groups, 2)) + list(range(groups - 1, 0, -2))
 
 
 def coordinates():
@@ -359,16 +363,14 @@
     )(attn, w_out)
 
 
-def score_kernel(steps, load, groups, mp, notes, *refs):
+def score_kernel(steps, load, mp, notes, up, *refs):
     take = lambda count: [refs.pop(0) for _ in range(count)]
     refs = list(refs)
-    ups, own_rows, peer_rows, blocks = take(1 + groups if load else 2), take(steps), take(steps), take(mp if load else 1)
-    kept = take(2 * load)
+    own_rows, peer_rows, blocks, kept = take(steps), take(steps), take(mp if load else 1), take(1 * load)
     flat, total, *sems = refs
-    _, cut, hidden = ups[0].shape
-    depth = flat.shape[1]
+    groups, depth, hidden = up.shape
     rows = own_rows[0].shape[0]
-    core, own, me = coordinates()
+    core, _, me = coordinates()
     for t in range(steps):
         target = flat.at[t * rows : (t + 1) * rows]
         for m in range(mp):
@@ -384,23 +386,19 @@
                         target[...] = source[...]
 
     if load:
-        for r in range(groups):
-            pltpu.make_async_copy(ups[0].at[r], kept[0].at[r], sems[1].at[r]).start()
-        for k in range(groups):
-            pltpu.make_async_copy(ups[1 + k], kept[1].at[own ^ k], sems[2].at[own ^ k]).start()
-        ups = kept
+        for i, r in enumerate(ring_order(groups)):
+            pltpu.make_async_copy(up.at[i], kept[0].at[r], sems[1].at[r]).start()
+        up = kept[0]
         for t in range(steps):
             target = flat.at[t * rows : (t + 1) * rows]
             pltpu.make_async_copy(target, target, sems[0].at[t]).wait()
     shard = jnp.concatenate([notes[:, SHARD : SHARD + 1].astype(jnp.int32)] * steps, 0)
     for r in range(groups):
         if load:
-            for i, up in enumerate(ups):
-                pltpu.make_async_copy(up.at[r], up.at[r], sems[1 + i].at[r]).wait()
+            pltpu.make_async_copy(up.at[r], up.at[r], sems[1].at[r]).wait()
         for at in range(0, hidden, COLUMNS):
             end = min(at + COLUMNS, hidden)
-            z = dot(flat[:, :cut], ups[0][r, :, at:end]) + dot(flat[:, cut:], ups[1][r, :, at:end])
-            here = jnp.where(shard == r, z, 0.0)
+            here = jnp.where(shard == r, dot(flat[...], up[r, :, at:end]), 0.0)
             total[:, at:end] = here if r == 0 else total[:, at:end] + here
     if not load:
         blocks[0][...] = total[...].astype(jnp.bfloat16)
@@ -414,25 +412,24 @@
                 block[...] = total[:, m * width : (m + 1) * width].astype(jnp.bfloat16)
 
 
-def score(mp, notes, ups, own_rows, peer_rows, load):
+def score(mp, notes, up, own_rows, peer_rows, load):
     steps = len(own_rows)
-    groups, cut, hidden = ups[0].shape
-    rest = ups[1].shape[-2]
+    groups, depth, hidden = up.shape
     count = steps * own_rows[0].shape[0]
     blocks = (struct((count, hidden // mp)),) * mp if load else (struct((count, hidden)),)
-    kept = (VMEM((groups, cut, hidden), jnp.bfloat16), VMEM((groups, rest, hidden), jnp.bfloat16)) * load
+    kept = (VMEM(up.shape, up.dtype),) * load
     place = FAR if load else WHOLE
-    sems = [pltpu.SemaphoreType.DMA((steps,))] + [pltpu.SemaphoreType.DMA((groups,))] * 2
-    return pl.pallas_call(
-        functools.partial(score_kernel, steps, load, groups, mp),
+    sems = [pltpu.SemaphoreType.DMA((steps,)), pltpu.SemaphoreType.DMA((groups,))]
+    return pl.pallas_call(
+        functools.partial(score_kernel, steps, load, mp),
         out_shape=blocks + kept,
-        in_specs=[WHOLE] + [place] * (len(ups) + 2 * steps),
+        in_specs=[WHOLE] + [place] * (1 + 2 * steps),
         out_specs=(WHOLE,) * (len(blocks) + len(kept)),
-        scratch_shapes=[VMEM((count, cut + rest), jnp.bfloat16), VMEM((count, hidden), jnp.float32)] + sems * load,
+        scratch_shapes=[VMEM((count, depth), jnp.bfloat16), VMEM((count, hidden), jnp.float32)] + sems * load,
         compiler_params=pltpu.CompilerParams(vmem_limit_bytes=16 << 20),
         cost_estimate=SMALL,
         name="score",
-    )(notes, *(map(far, (*ups, *own_rows, *peer_rows)) if load else (*ups, *own_rows, *peer_rows)))
+    )(notes, *(map(far, (up, *own_rows, *peer_rows)) if load else (up, *own_rows, *peer_rows)))
 
 
 def scores_of(notes, scale, parts, factors):
@@ -529,9 +526,7 @@
     pairs = lambda count, k: [(i, i ^ k) for i in range(count)]
     swap = pairs(mp, 1)
 
-    cut = reward_up.shape[1] * 4 // 5
-    rest = reward_up[0, cut:]
-    ups = [lax.all_gather(reward_up[0, :cut], "dp", axis=0)]
+    up = lax.all_gather(reward_up[0], "dp", axis=0, axis_index_groups=[ring_order(groups)])
 
     blocks = dispatch(parents, child_count, child_parent, node_shard, tokens, reward_out, groups, capacity, hidden)
     keys = parent_keys.reshape(parents * prefix, kv_cols)
@@ -542,8 +537,7 @@
     blocks, weights = lax.optimization_barrier((blocks, load(*raw)))
     gain = attn_gain.reshape(1, width)
 
-    def run(offset, weights, blocks, ups, rests, gain, child_parent, parent_blocks):
-        rests = list(rests)
+    def run(offset, weights, blocks, up, gain, child_parent, parent_blocks):
         row_own, notes, bias, scale, over = pack(
             offset, rows, hidden, prefix, parent_blocks, child_parent, blocks
         )
@@ -552,10 +546,10 @@
         row_peer = lax.ppermute(row_own, "mp", swap)
         past_keys, past_values, rows_own, rows_peer, norms = [], [], [], [], []
 
-        def products(first, last, ups, load):
-            sums = score(mp, notes, ups, rows_own[first:last], rows_peer[first:last], load)
+        def products(first, last, up, load):
+            sums = score(mp, notes, up, rows_own[first:last], rows_peer[first:last], load)
             count = mp if load else 1
-            return list(sums[:count]), [held(up) for up in sums[count:]]
+            return list(sums[:count]), held(sums[-1]) if load else None
 
         send = lambda sums: [sums[0]] + [lax.ppermute(sums[k], "mp", pairs(mp, k)) for k in range(1, mp)]
         scales = send([scale] * mp)
@@ -571,16 +565,11 @@
             chip = project_own(rows, attn, w_out) + from_peer.astype(jnp.float32)
             sent = chip.astype(jnp.bfloat16)
             others = [sent] + [lax.ppermute(sent, "mp", pairs(mp, k)) for k in range(2, mp, 2)]
-            if len(rests) < groups:
-                more = range(len(rests), min(groups, len(rests) - (1 - groups) // (STEPS - 1)))
-                more = [lax.ppermute(rests[0], "dp", pairs(groups, k)) for k in more]
-                others, more = lax.optimization_barrier((others, more))
-                rests += more
             if step == 0:
                 others, scales = lax.optimization_barrier((others, scales))
             if step + 1 == STEPS:
-                _, ups = lax.optimization_barrier((sent, ups))
-                before, ups = products(0, step, [*ups, *rests], True)
+                _, up = lax.optimization_barrier((sent, up))
+                before, up = products(0, step, up, True)
                 others, before = lax.optimization_barrier((others, before))
             state = state + paired_sum([other.astype(jnp.float32) for other in others])
             row_own = state.astype(jnp.bfloat16)
@@ -588,14 +577,13 @@
             rows_own.append(row_own)
             rows_peer.append(row_peer)
         before = send(before)
-        last, _ = products(step, STEPS, ups, False)
+        last, _ = products(step, STEPS, up, False)
         last, over = lax.optimization_barrier((send(last * mp), over[0, 0]))
         before = send([finish(notes, scale, norms[1:], before)] * mp)
-        return place(groups, reward_cap, notes, row_own, row_peer, before, scales, last), over, rests
-
-    others = (gain, child_parent, parent_blocks)
-    table, over, rests = run(0, weights, blocks, ups, [rest], *others)
-    operands = (blocks, ups, rests, *others)
+        return place(groups, reward_cap, notes, row_own, row_peer, before, scales, last), over
+
+    operands = (blocks, up, gain, child_parent, parent_blocks)
+    table, over = run(0, weights, *operands)
     if rows < slots:
         table, raw, operands = lax.optimization_barrier((table, raw, operands))
         again = lambda table, raw, operands: table + run(rows, load(*raw), *operands)[0]

time: 295 us -> 197 us (0.67)
  waiting for transfers between devices: 109 us -> 47.3 us
  local copies, waits for them, and re-layouts: 24.3 us -> 0.59 us
  starting transfers between devices: 47.4 us -> 38 us
  other arithmetic: 5.14 us -> 1.88 us
    ppermute x7 -> x0, waiting for transfers between devices: 100 us -> none  [run(): more = [lax.ppermute(rests[0], 'dp', pairs(groups, k)) for k in more]]
    ppermute x8, waiting for transfers between devices: 4.44 us -> 38.7 us  [run(): lax.ppermute(sent, 'mp', pairs(mp, k))]
    unnamed x150 -> x34, local copies, waits for them, and re-layouts: 21.4 us -> 0.07 us
    ppermute x7 -> x0, starting transfers between devices: 10.2 us -> none  [run(): more = [lax.ppermute(rests[0], 'dp', pairs(groups, k)) for k in more]]
    ppermute x12, waiting for transfers between devices: 2.2 us -> 6.04 us  [run(): lax.ppermute(sums[k], 'mp', pairs(mp, k))]
  transfers between devices with their start and end apart: 52 -> 45, of which waited for: 18 -> 17; matrix products, arithmetic and copies ran while one was open for 3% -> 1% of each run, Pallas kernels for 23% -> 39%
where the time goes in v4:
time: 197 us; the launch traced here: 193 us
  Pallas kernels  76 us (39%)
  waiting for transfers between devices  47.3 us (24%)
  starting transfers between devices  38 us (19%)
  between operations  15.6 us (8%)
  blocking collectives  12.4 us (6%)
    ppermute x8, waiting for transfers between devices, run(): lax.ppermute(sent, 'mp', pairs(mp, k))  38.7 us
    pallas_call x8, Pallas kernels, expand(): pl.pallas_call(functools.partial(step_kernel, step), out_shape=(struct((s...  32.4 us
    ppermute x8, starting transfers between devices, run(): lax.ppermute(sent, 'mp', pairs(mp, k))  13.7 us
    ppermute x7, starting transfers between devices, shards(): lax.ppermute(blocks[k], 'dp', pairs(groups, k))  12.5 us
    all_to_all x1, blocking collectives, shards(): table = lax.all_to_all(table, 'dp', split_axis=0, concat_axis=0, tiled=True)  12.4 us
    pallas_call x8, Pallas kernels, project_own(): pl.pallas_call(project_kernel, out_shape=struct((rows, w_out.shape[1] //...  11 us
    pallas_call x2, Pallas kernels, score(): pl.pallas_call(functools.partial(score_kernel, steps, load, mp), out_shap...  10.9 us
    pallas_call x8, Pallas kernels, begin(): pl.pallas_call(begin_kernel, out_shape=struct((slots, w_query.shape[1] +...  10 us
  transfers between devices with their start and end apart: 45, of which 17 were waited for; matrix products, arithmetic and copies ran while one was open for 1% of the time, Pallas kernels for 39%

profile of v4, /device:TPU:0, one launch (start us, length us, event | category | flops | bytes accessed | tf_op | source)
XLA Modules:
  0.0 193.0 jit_solution(10001065745820205462)
XLA Ops:
  9.4 3.0 %collective-permute-start.37 = (bf16[8,3072]{1,0:T(8,128)(2,1)S(1)}, bf16[8,3072]{1,0:T(8,128)(2,1)S(1)}, u32[]{:S(2)}, u32[]{:S(2)}) collective-permute-start(bf16[8,3072]{1,0:T(8,128)(2,1)S(1)} %get-tuple-element.270), channel_id=1, source_target_pairs={{0,4},{4,0},{8,12},{12,8},{16,20},{20,16},{24,28},{28,24},{1,5},{5... | collective-permute-start | bytes 147464 | tf_op jit(solution)/shard_map/ppermute | solution.py:536
  14.1 3.0 %collective-permute-start.40 = (bf16[8,3072]{1,0:T(8,128)(2,1)S(1)}, bf16[8,3072]{1,0:T(8,128)(2,1)S(1)}, u32[]{:S(2)}, u32[]{:S(2)}) collective-permute-start(bf16[8,3072]{1,0:T(8,128)(2,1)S(1)} %get-tuple-element.273), channel_id=1, source_target_pairs={{0,16},{4,20},{8,24},{12,28},{16,0},{20,4},{24,8},{28,12},{1,17},{... | collective-permute-start | bytes 147464 | tf_op jit(solution)/shard_map/ppermute | solution.py:536
  18.3 3.6 %collective-permute-start.42 = (bf16[8,3072]{1,0:T(8,128)(2,1)S(1)}, bf16[8,3072]{1,0:T(8,128)(2,1)S(1)}, u32[]{:S(2)}, u32[]{:S(2)}) collective-permute-start(bf16[8,3072]{1,0:T(8,128)(2,1)S(1)} %get-tuple-element.275), channel_id=1, source_target_pairs={{0,24},{4,28},{8,16},{12,20},{16,8},{20,12},{24,0},{28,4},{1,25},{... | collective-permute-start | bytes 147464 | tf_op jit(solution)/shard_map/ppermute | solution.py:536
  21.9 7.7 %load.3 = (bf16[5120,768]{1,0:T(8,128)(2,1)S(1)}, bf16[5120,256]{1,0:T(8,128)(2,1)S(1)}, bf16[5120,256]{1,0:T(8,128)(2,1)S(1)}, bf16[2048,256]{1,0:T(8,128)(2,1)...) custom-call(bf16[5120,768]{1,0:T(8,128)(2,1)} %refs_0_, bf16[5120,256]{1,0:T(8,128)(2,1)} %refs_1_, ...), custom_call_target="tpu_custom_call" | custom-call | bytes 25165824 | tf_op jit(solution)/shard_map/load/pallas_call | solution.py:223
  32.3 4.5 %expand.24 = (bf16[48,2560]{1,0:T(8,128)(2,1)S(1)}, bf16[64,768]{1,0:T(8,128)(2,1)S(1)}, bf16[48,256]{1,0:T(8,128)(2,1)S(1)}, bf16[48,256]{1,0:T(8,128)(2,1)S(1)}, f32[48,128]{1,0:T(8,128)}) custom-call(bf16[48,2560]{1,0:T(8,128)(2,1)S(1)} %get-tuple-element.298.own, bf16[48,2560]{1,0:T(8,128)(2,1)S(1)} %collective-permute-done.44.peer, ...), custom_call_target="tpu_custom_call" | custom-call | tf_op jit(solution)/shard_map/expand/pallas_call | solution.py:334
  38.4 1.7 collective-permute-start.46
  42.0 4.0 %collective-permute-done.49.refs_7_ = f32[8,128]{1,0:T(8,128)S(1)} collective-permute-done((f32[8,128]{1,0:T(8,128)S(1)}, f32[8,128]{1,0:T(8,128)S(1)}, u32[]{:S(2)}, u32[]{:S(2)}) %collective-permute-start.49) | collective-permute-done | bytes 4128 | tf_op jit(solution)/shard_map/ppermute | solution.py:554
  48.5 3.9 %expand.25 = (bf16[48,2560]{1,0:T(8,128)(2,1)S(1)}, bf16[64,768]{1,0:T(8,128)(2,1)S(1)}, bf16[48,256]{1,0:T(8,128)(2,1)S(1)}, bf16[48,256]{1,0:T(8,128)(2,1)S(1)}, f32[48,128]{1,0:T(8,128)S(1)}) custom-call(bf16[48,2560]{1,0:T(8,128)(2,1)S(1)} %fusion.4.own.refs_0_, bf16[48,2560]{1,0:T(8,128)(2,1)S(1)} %collective-permute-done.50.peer.refs_7_, ...), custom_call_target="tpu_custom_call" | custom-call | tf_op jit(solution)/shard_map/expand/pallas_call | solution.py:334
  54.1 1.7 collective-permute-start.52
  55.8 6.5 %collective-permute-done.52 = bf16[48,2560]{1,0:T(8,128)(2,1)S(1)} collective-permute-done((bf16[48,2560]{1,0:T(8,128)(2,1)S(1)}, bf16[48,2560]{1,0:T(8,128)(2,1)S(1)}, u32[]{:S(2)}, u32[]{:S(2)}) %collective-permute-start.52) | collective-permute-done | bytes 245792 | tf_op jit(solution)/shard_map/ppermute | solution.py:567
  64.0 3.9 %expand.26 = (bf16[48,2560]{1,0:T(8,128)(2,1)S(1)}, bf16[64,768]{1,0:T(8,128)(2,1)S(1)}, bf16[48,256]{1,0:T(8,128)(2,1)S(1)}, bf16[48,256]{1,0:T(8,128)(2,1)S(1)}, f32[48,128]{1,0:T(8,128)S(1)}) custom-call(bf16[48,2560]{1,0:T(8,128)(2,1)S(1)} %get-tuple-element.397.own.refs_1_, bf16[48,2560]{1,0:T(8,128)(2,1)S(1)} %collective-permute-done.53.peer.refs_8_, ...), custom_call_target="tpu_custom_call" | custom-call | tf_op jit(solution)/shard_map/expand/pallas_call | solution.py:334
  69.6 1.7 collective-permute-start.55
  71.3 6.5 %collective-permute-done.55 = bf16[48,2560]{1,0:T(8,128)(2,1)S(1)} collective-permute-done((bf16[48,2560]{1,0:T(8,128)(2,1)S(1)}, bf16[48,2560]{1,0:T(8,128)(2,1)S(1)}, u32[]{:S(2)}, u32[]{:S(2)}) %collective-permute-start.55) | collective-permute-done | bytes 245792 | tf_op jit(solution)/shard_map/ppermute | solution.py:567
  79.4 3.9 %expand.27 = (bf16[48,2560]{1,0:T(8,128)(2,1)S(1)}, bf16[64,768]{1,0:T(8,128)(2,1)S(1)}, bf16[48,256]{1,0:T(8,128)(2,1)S(1)}, bf16[48,256]{1,0:T(8,128)(2,1)S(1)}, f32[48,128]{1,0:T(8,128)S(1)}) custom-call(bf16[48,2560]{1,0:T(8,128)(2,1)S(1)} %fusion.5.own.refs_2_, bf16[48,2560]{1,0:T(8,128)(2,1)S(1)} %collective-permute-done.56.peer.refs_9_, ...), custom_call_target="tpu_custom_call" | custom-call | tf_op jit(solution)/shard_map/expand/pallas_call | solution.py:334
  83.7 1.8 project_own.27
  85.6 1.7 collective-permute-start.58
  87.3 6.5 %collective-permute-done.58 = bf16[48,2560]{1,0:T(8,128)(2,1)S(1)} collective-permute-done((bf16[48,2560]{1,0:T(8,128)(2,1)S(1)}, bf16[48,2560]{1,0:T(8,128)(2,1)S(1)}, u32[]{:S(2)}, u32[]{:S(2)}) %collective-permute-start.58) | collective-permute-done | bytes 245792 | tf_op jit(solution)/shard_map/ppermute | solution.py:567
  95.5 3.9 %expand.28 = (bf16[48,2560]{1,0:T(8,128)(2,1)S(1)}, bf16[64,768]{1,0:T(8,128)(2,1)S(1)}, bf16[48,256]{1,0:T(8,128)(2,1)S(1)}, bf16[48,256]{1,0:T(8,128)(2,1)S(1)}, f32[48,128]{1,0:T(8,128)S(1)}) custom-call(bf16[48,2560]{1,0:T(8,128)(2,1)S(1)} %get-tuple-element.395.own.refs_3_, bf16[48,2560]{1,0:T(8,128)(2,1)S(1)} %collective-permute-done.59.peer.refs_10_, ...), custom_call_target="tpu_custom_call" | custom-call | tf_op jit(solution)/shard_map/expand/pallas_call | solution.py:334
  101.1 1.7 collective-permute-start.61
  102.9 6.4 %collective-permute-done.61 = bf16[48,2560]{1,0:T(8,128)(2,1)S(1)} collective-permute-done((bf16[48,2560]{1,0:T(8,128)(2,1)S(1)}, bf16[48,2560]{1,0:T(8,128)(2,1)S(1)}, u32[]{:S(2)}, u32[]{:S(2)}) %collective-permute-start.61) | collective-permute-done | bytes 245792 | tf_op jit(solution)/shard_map/ppermute | solution.py:567
  111.0 4.0 %expand.29 = (bf16[48,2560]{1,0:T(8,128)(2,1)S(1)}, bf16[64,768]{1,0:T(8,128)(2,1)S(1)}, bf16[48,256]{1,0:T(8,128)(2,1)S(1)}, bf16[48,256]{1,0:T(8,128)(2,1)S(1)}, f32[48,128]{1,0:T(8,128)S(1)}) custom-call(bf16[48,2560]{1,0:T(8,128)(2,1)S(1)} %fusion.6.own.refs_4_, bf16[48,2560]{1,0:T(8,128)(2,1)S(1)} %collective-permute-done.62.peer.refs_11_, ...), custom_call_target="tpu_custom_call" | custom-call | tf_op jit(solution)/shard_map/expand/pallas_call | solution.py:334
  116.7 1.7 collective-permute-start.64
  118.4 6.5 %collective-permute-done.64 = bf16[48,2560]{1,0:T(8,128)(2,1)S(1)} collective-permute-done((bf16[48,2560]{1,0:T(8,128)(2,1)S(1)}, bf16[48,2560]{1,0:T(8,128)(2,1)S(1)}, u32[]{:S(2)}, u32[]{:S(2)}) %collective-permute-start.64) | collective-permute-done | bytes 245792 | tf_op jit(solution)/shard_map/ppermute | solution.py:567
  126.6 4.0 %expand.30 = (bf16[48,2560]{1,0:T(8,128)(2,1)S(1)}, bf16[64,768]{1,0:T(8,128)(2,1)S(1)}, bf16[48,256]{1,0:T(8,128)(2,1)S(1)}, bf16[48,256]{1,0:T(8,128)(2,1)S(1)}, f32[48,128]{1,0:T(8,128)S(1)}) custom-call(bf16[48,2560]{1,0:T(8,128)(2,1)S(1)} %get-tuple-element.393.own.refs_5_, bf16[48,2560]{1,0:T(8,128)(2,1)S(1)} %collective-permute-done.65.peer.refs_12_, ...), custom_call_target="tpu_custom_call" | custom-call | tf_op jit(solution)/shard_map/expand/pallas_call | solution.py:334
  132.5 1.7 collective-permute-start.67
  134.2 6.5 %collective-permute-done.67 = bf16[48,2560]{1,0:T(8,128)(2,1)S(1)} collective-permute-done((bf16[48,2560]{1,0:T(8,128)(2,1)S(1)}, bf16[48,2560]{1,0:T(8,128)(2,1)S(1)}, u32[]{:S(2)}, u32[]{:S(2)}) %collective-permute-start.67) | collective-permute-done | bytes 245792 | tf_op jit(solution)/shard_map/ppermute | solution.py:567
  142.3 4.4 %expand.31 = (bf16[48,2560]{1,0:T(8,128)(2,1)S(1)}, bf16[64,768]{1,0:T(8,128)(2,1)S(1)}, bf16[48,256]{1,0:T(8,128)(2,1)}, bf16[48,256]{1,0:T(8,128)(2,1)}, f32[48,128]{1,0:T(8,128)S(1)}) custom-call(bf16[48,2560]{1,0:T(8,128)(2,1)S(1)} %fusion.7.own.refs_6_, bf16[48,2560]{1,0:T(8,128)(2,1)S(1)} %collective-permute-done.68.peer.refs_13_, ...), custom_call_target="tpu_custom_call" | custom-call | tf_op jit(solution)/shard_map/expand/pallas_call | solution.py:334
  148.4 1.7 collective-permute-start.70
  150.1 9.0 %score.6 = (bf16[336,128]{1,0:T(8,128)(2,1)S(1)}, bf16[336,128]{1,0:T(8,128)(2,1)S(1)}, bf16[336,128]{1,0:T(8,128)(2,1)S(1)}, bf16[336,128]{1,0:T(8,128)(2,1)S(1)}, bf16[8,1280,512]{2,1,0:T(8,128)(2,1)S(1)}) custom-call(f32[48,128]{1,0:T(8,128)S(1)} %get-tuple-element.297.notes, bf16[8,1280,512]{2,1,0:T(8,128)(2,1)} %all-gather.2.cloned.1.call-done.up, ...), custom_call_target="tpu_custom_call" | custom-call | tf_op jit(solution)/shard_map/score/pallas_call | solution.py:423
  161.2 1.9 %score.7.refs_8_ = bf16[48,512]{1,0:T(8,128)(2,1)S(1)} custom-call(f32[48,128]{1,0:T(8,128)S(1)} %get-tuple-element.297.notes, bf16[8,1280,512]{2,1,0:T(8,128)(2,1)S(1)} %get-tuple-element.340.up, bf16[48,2560]{1,0:T(8,128)(2,1)S(1)} %add_convert_fusion.9.refs_0_.own_row, bf16[48,2560]{1,0:T(8,128)(2,1)S(1)} %collective-permute-done.71.refs_1_.peer_row), custom_call_target="tpu_custom_call" | custom-call | tf_op jit(solution)/shard_map/score/pallas_call | solution.py:423
  163.9 1.7 collective-permute-start.73
  173.0 12.4 %all_to_all.9 = f32[8,8,128]{2,1,0:T(8,128)S(1)} all-to-all(f32[8,8,128]{2,1,0:T(8,128)S(1)} %bitcast.30), channel_id=1, replica_groups=mesh['dp'=8,'mp'=4] {'dp'}, dimensions={0} | all-to-all | bytes 65536 | tf_op jit(solution)/shard_map/all_to_all | solution.py:592
  (144 shorter events, 44.5 us)
Async XLA Ops:
  6.5 143.5 %all-gather.2.cloned.1.call-start = ((), (), s32[]{:S(2)}) async-start(), calls=%async_computation.1 | async-start | bytes 11796480 | tf_op jit(solution)/shard_map/all_gather | solution.py:529
  9.4 8.9 %collective-permute-start.37 = (bf16[8,3072]{1,0:T(8,128)(2,1)S(1)}, bf16[8,3072]{1,0:T(8,128)(2,1)S(1)}, u32[]{:S(2)}, u32[]{:S(2)}) collective-permute-start(bf16[8,3072]{1,0:T(8,128)(2,1)S(1)} %get-tuple-element.270), channel_id=1, source_target_pairs={{0,4},{4,0},{8,12},{12,8},{16,20},{20,16},{24,28},{28,24},{1,5},{5... | collective-permute-start | bytes 147464 | tf_op jit(solution)/shard_map/ppermute | solution.py:536
  12.5 9.5 %collective-permute-start.38 = (bf16[8,3072]{1,0:T(8,128)(2,1)S(1)}, bf16[8,3072]{1,0:T(8,128)(2,1)S(1)}, u32[]{:S(2)}, u32[]{:S(2)}) collective-permute-start(bf16[8,3072]{1,0:T(8,128)(2,1)S(1)} %get-tuple-element.271), channel_id=1, source_target_pairs={{0,8},{4,12},{8,0},{12,4},{16,24},{20,28},{24,16},{28,20},{1,9},{5... | collective-permute-start | bytes 147464 | tf_op jit(solution)/shard_map/ppermute | solution.py:536
  14.1 15.6 %collective-permute-start.39 = (bf16[8,3072]{1,0:T(8,128)(2,1)S(1)}, bf16[8,3072]{1,0:T(8,128)(2,1)S(1)}, u32[]{:S(2)}, u32[]{:S(2)}) collective-permute-start(bf16[8,3072]{1,0:T(8,128)(2,1)S(1)} %get-tuple-element.272), channel_id=1, source_target_pairs={{0,12},{4,8},{8,4},{12,0},{16,28},{20,24},{24,20},{28,16},{1,13},{... | collective-permute-start | bytes 147464 | tf_op jit(solution)/shard_map/ppermute | solution.py:536
  14.1 15.6 %collective-permute-start.40 = (bf16[8,3072]{1,0:T(8,128)(2,1)S(1)}, bf16[8,3072]{1,0:T(8,128)(2,1)S(1)}, u32[]{:S(2)}, u32[]{:S(2)}) collective-permute-start(bf16[8,3072]{1,0:T(8,128)(2,1)S(1)} %get-tuple-element.273), channel_id=1, source_target_pairs={{0,16},{4,20},{8,24},{12,28},{16,0},{20,4},{24,8},{28,12},{1,17},{... | collective-permute-start | bytes 147464 | tf_op jit(solution)/shard_map/ppermute | solution.py:536
  17.0 12.7 %collective-permute-start.41 = (bf16[8,3072]{1,0:T(8,128)(2,1)S(1)}, bf16[8,3072]{1,0:T(8,128)(2,1)S(1)}, u32[]{:S(2)}, u32[]{:S(2)}) collective-permute-start(bf16[8,3072]{1,0:T(8,128)(2,1)S(1)} %get-tuple-element.274), channel_id=1, source_target_pairs={{0,20},{4,16},{8,28},{12,24},{16,4},{20,0},{24,12},{28,8},{1,21},{... | collective-permute-start | bytes 147464 | tf_op jit(solution)/shard_map/ppermute | solution.py:536
  18.3 11.4 %collective-permute-start.42 = (bf16[8,3072]{1,0:T(8,128)(2,1)S(1)}, bf16[8,3072]{1,0:T(8,128)(2,1)S(1)}, u32[]{:S(2)}, u32[]{:S(2)}) collective-permute-start(bf16[8,3072]{1,0:T(8,128)(2,1)S(1)} %get-tuple-element.275), channel_id=1, source_target_pairs={{0,24},{4,28},{8,16},{12,20},{16,8},{20,12},{24,0},{28,4},{1,25},{... | collective-permute-start | bytes 147464 | tf_op jit(solution)/shard_map/ppermute | solution.py:536
  21.9 7.8 %collective-permute-start.43 = (bf16[8,3072]{1,0:T(8,128)(2,1)S(1)}, bf16[8,3072]{1,0:T(8,128)(2,1)S(1)}, u32[]{:S(2)}, u32[]{:S(2)}) collective-permute-start(bf16[8,3072]{1,0:T(8,128)(2,1)S(1)} %get-tuple-element.276), channel_id=1, source_target_pairs={{0,28},{4,24},{8,20},{12,16},{16,12},{20,8},{24,4},{28,0},{1,29},{... | collective-permute-start | bytes 147464 | tf_op jit(solution)/shard_map/ppermute | solution.py:536
  38.4 8.4 %collective-permute-start.46 = (bf16[48,2560]{1,0:T(8,128)(2,1)S(1)}, bf16[48,2560]{1,0:T(8,128)(2,1)S(1)}, u32[]{:S(2)}, u32[]{:S(2)}) collective-permute-start(bf16[48,2560]{1,0:T(8,128)(2,1)S(1)} %add_convert_fusion.17), channel_id=1, source_target_pairs={{0,2},{1,3},{2,0},{3,1},{4,6},{5,7},{6,4},{7,5},{8,10},{9,11},{10,... | collective-permute-start | bytes 737288 | tf_op jit(solution)/shard_map/ppermute | solution.py:567
  40.2 5.9 %collective-permute-start.49 = (f32[8,128]{1,0:T(8,128)S(1)}, f32[8,128]{1,0:T(8,128)S(1)}, u32[]{:S(2)}, u32[]{:S(2)}) collective-permute-start(f32[8,128]{1,0:T(8,128)S(1)} %get-tuple-element.360.scale.refs_4_), channel_id=1, source_target_pairs={{0,3},{1,2},{2,1},{3,0},{4,7},{5,6},{6,5},{7,4},{8,11},{9,10},{10,... | collective-permute-start | bytes 12296 | tf_op jit(solution)/shard_map/ppermute | solution.py:554
  40.2 6.6 %collective-permute-start.48 = (f32[8,128]{1,0:T(8,128)S(1)}, f32[8,128]{1,0:T(8,128)S(1)}, u32[]{:S(2)}, u32[]{:S(2)}) collective-permute-start(f32[8,128]{1,0:T(8,128)S(1)} %get-tuple-element.360.scale.refs_4_), channel_id=1, source_target_pairs={{0,2},{1,3},{2,0},{3,1},{4,6},{5,7},{6,4},{7,5},{8,10},{9,11},{10,... | collective-permute-start | bytes 12296 | tf_op jit(solution)/shard_map/ppermute | solution.py:554
  41.8 5.0 %collective-permute-start.47 = (f32[8,128]{1,0:T(8,128)S(1)}, f32[8,128]{1,0:T(8,128)S(1)}, u32[]{:S(2)}, u32[]{:S(2)}) collective-permute-start(f32[8,128]{1,0:T(8,128)S(1)} %get-tuple-element.360.scale.refs_4_), channel_id=1, source_target_pairs={{0,1},{1,0},{2,3},{3,2},{4,5},{5,4},{6,7},{7,6},{8,9},{9,8},{10,11... | collective-permute-start | bytes 12296 | tf_op jit(solution)/shard_map/ppermute | solution.py:554
  54.1 8.2 %collective-permute-start.52 = (bf16[48,2560]{1,0:T(8,128)(2,1)S(1)}, bf16[48,2560]{1,0:T(8,128)(2,1)S(1)}, u32[]{:S(2)}, u32[]{:S(2)}) collective-permute-start(bf16[48,2560]{1,0:T(8,128)(2,1)S(1)} %add_convert_fusion.16), channel_id=1, source_target_pairs={{0,2},{1,3},{2,0},{3,1},{4,6},{5,7},{6,4},{7,5},{8,10},{9,11},{10,... | collective-permute-start | bytes 737288 | tf_op jit(solution)/shard_map/ppermute | solution.py:567
  69.6 8.2 %collective-permute-start.55 = (bf16[48,2560]{1,0:T(8,128)(2,1)S(1)}, bf16[48,2560]{1,0:T(8,128)(2,1)S(1)}, u32[]{:S(2)}, u32[]{:S(2)}) collective-permute-start(bf16[48,2560]{1,0:T(8,128)(2,1)S(1)} %add_convert_fusion.15), channel_id=1, source_target_pairs={{0,2},{1,3},{2,0},{3,1},{4,6},{5,7},{6,4},{7,5},{8,10},{9,11},{10,... | collective-permute-start | bytes 737288 | tf_op jit(solution)/shard_map/ppermute | solution.py:567
  83.4 2.2 %collective-permute-start.57 = (bf16[48,2560]{1,0:T(8,128)(2,1)S(1)}, bf16[48,2560]{1,0:T(8,128)(2,1)S(1)}, u32[]{:S(2)}, u32[]{:S(2)}) collective-permute-start(bf16[48,2560]{1,0:T(8,128)(2,1)S(1)} %get-tuple-element.322), channel_id=1, source_target_pairs={{0,1},{1,0},{2,3},{3,2},{4,5},{5,4},{6,7},{7,6},{8,9},{9,8},{10,11... | collective-permute-start | bytes 737288 | tf_op jit(solution)/shard_map/ppermute | solution.py:564
  85.6 8.2 %collective-permute-start.58 = (bf16[48,2560]{1,0:T(8,128)(2,1)S(1)}, bf16[48,2560]{1,0:T(8,128)(2,1)S(1)}, u32[]{:S(2)}, u32[]{:S(2)}) collective-permute-start(bf16[48,2560]{1,0:T(8,128)(2,1)S(1)} %add_convert_fusion.14), channel_id=1, source_target_pairs={{0,2},{1,3},{2,0},{3,1},{4,6},{5,7},{6,4},{7,5},{8,10},{9,11},{10,... | collective-permute-start | bytes 737288 | tf_op jit(solution)/shard_map/ppermute | solution.py:567
  99.4 1.7 collective-permute-start.60
  101.1 8.2 %collective-permute-start.61 = (bf16[48,2560]{1,0:T(8,128)(2,1)S(1)}, bf16[48,2560]{1,0:T(8,128)(2,1)S(1)}, u32[]{:S(2)}, u32[]{:S(2)}) collective-permute-start(bf16[48,2560]{1,0:T(8,128)(2,1)S(1)} %add_convert_fusion.13), channel_id=1, source_target_pairs={{0,2},{1,3},{2,0},{3,1},{4,6},{5,7},{6,4},{7,5},{8,10},{9,11},{10,... | collective-permute-start | bytes 737288 | tf_op jit(solution)/shard_map/ppermute | solution.py:567
  116.7 8.2 %collective-permute-start.64 = (bf16[48,2560]{1,0:T(8,128)(2,1)S(1)}, bf16[48,2560]{1,0:T(8,128)(2,1)S(1)}, u32[]{:S(2)}, u32[]{:S(2)}) collective-permute-start(bf16[48,2560]{1,0:T(8,128)(2,1)S(1)} %add_convert_fusion.12), channel_id=1, source_target_pairs={{0,2},{1,3},{2,0},{3,1},{4,6},{5,7},{6,4},{7,5},{8,10},{9,11},{10,... | collective-permute-start | bytes 737288 | tf_op jit(solution)/shard_map/ppermute | solution.py:567
  130.6 1.8 collective-permute-start.66
  132.5 8.2 %collective-permute-start.67 = (bf16[48,2560]{1,0:T(8,128)(2,1)S(1)}, bf16[48,2560]{1,0:T(8,128)(2,1)S(1)}, u32[]{:S(2)}, u32[]{:S(2)}) collective-permute-start(bf16[48,2560]{1,0:T(8,128)(2,1)S(1)} %add_convert_fusion.11), channel_id=1, source_target_pairs={{0,2},{1,3},{2,0},{3,1},{4,6},{5,7},{6,4},{7,5},{8,10},{9,11},{10,... | collective-permute-start | bytes 737288 | tf_op jit(solution)/shard_map/ppermute | solution.py:567
  148.4 10.7 %collective-permute-start.70 = (bf16[48,2560]{1,0:T(8,128)(2,1)S(1)}, bf16[48,2560]{1,0:T(8,128)(2,1)S(1)}, u32[]{:S(2)}, u32[]{:S(2)}) collective-permute-start(bf16[48,2560]{1,0:T(8,128)(2,1)S(1)} %add_convert_fusion.10), channel_id=1, source_target_pairs={{0,2},{1,3},{2,0},{3,1},{4,6},{5,7},{6,4},{7,5},{8,10},{9,11},{10,... | collective-permute-start | bytes 737288 | tf_op jit(solution)/shard_map/ppermute | solution.py:567
  159.2 2.0 %collective-permute-start.71 = (bf16[48,2560]{1,0:T(8,128)(2,1)S(1)}, bf16[48,2560]{1,0:T(8,128)(2,1)S(1)}, u32[]{:S(2)}, u32[]{:S(2)}) collective-permute-start(bf16[48,2560]{1,0:T(8,128)(2,1)S(1)} %add_convert_fusion.9.refs_0_.own_row), channel_id=1, source_target_pairs={{0,1},{1,0},{2,3},{3,2},{4,5},{5,4},{6,7},{7,6},{8,9},{9,8},{10,11... | collective-permute-start | bytes 737288 | tf_op jit(solution)/shard_map/ppermute | solution.py:576
  159.3 6.3 %collective-permute-start.75 = (bf16[336,128]{1,0:T(8,128)(2,1)S(1)}, bf16[336,128]{1,0:T(8,128)(2,1)S(1)}, u32[]{:S(2)}, u32[]{:S(2)}) collective-permute-start(bf16[336,128]{1,0:T(8,128)(2,1)S(1)} %get-tuple-element.357), channel_id=1, source_target_pairs={{0,1},{1,0},{2,3},{3,2},{4,5},{5,4},{6,7},{7,6},{8,9},{9,8},{10,11... | collective-permute-start | bytes 258056 | tf_op jit(solution)/shard_map/ppermute | solution.py:554
  159.8 5.8 %collective-permute-start.76 = (bf16[336,128]{1,0:T(8,128)(2,1)S(1)}, bf16[336,128]{1,0:T(8,128)(2,1)S(1)}, u32[]{:S(2)}, u32[]{:S(2)}) collective-permute-start(bf16[336,128]{1,0:T(8,128)(2,1)S(1)} %get-tuple-element.358), channel_id=1, source_target_pairs={{0,2},{1,3},{2,0},{3,1},{4,6},{5,7},{6,4},{7,5},{8,10},{9,11},{10,... | collective-permute-start | bytes 258056 | tf_op jit(solution)/shard_map/ppermute | solution.py:554
  160.2 5.4 %collective-permute-start.77 = (bf16[336,128]{1,0:T(8,128)(2,1)S(1)}, bf16[336,128]{1,0:T(8,128)(2,1)S(1)}, u32[]{:S(2)}, u32[]{:S(2)}) collective-permute-start(bf16[336,128]{1,0:T(8,128)(2,1)S(1)} %get-tuple-element.359), channel_id=1, source_target_pairs={{0,3},{1,2},{2,1},{3,0},{4,7},{5,6},{6,5},{7,4},{8,11},{9,10},{10,... | collective-permute-start | bytes 258056 | tf_op jit(solution)/shard_map/ppermute | solution.py:554
  163.2 5.5 %collective-permute-start.74 = (bf16[48,512]{1,0:T(8,128)(2,1)S(1)}, bf16[48,512]{1,0:T(8,128)(2,1)S(1)}, u32[]{:S(2)}, u32[]{:S(2)}) collective-permute-start(bf16[48,512]{1,0:T(8,128)(2,1)S(1)} %score.7.refs_8_), channel_id=1, source_target_pairs={{0,3},{1,2},{2,1},{3,0},{4,7},{5,6},{6,5},{7,4},{8,11},{9,10},{10,... | collective-permute-start | bytes 147464 | tf_op jit(solution)/shard_map/ppermute | solution.py:554
  163.9 5.3 %collective-permute-start.73 = (bf16[48,512]{1,0:T(8,128)(2,1)S(1)}, bf16[48,512]{1,0:T(8,128)(2,1)S(1)}, u32[]{:S(2)}, u32[]{:S(2)}) collective-permute-start(bf16[48,512]{1,0:T(8,128)(2,1)S(1)} %score.7.refs_8_), channel_id=1, source_target_pairs={{0,2},{1,3},{2,0},{3,1},{4,6},{5,7},{6,4},{7,5},{8,10},{9,11},{10,... | collective-permute-start | bytes 147464 | tf_op jit(solution)/shard_map/ppermute | solution.py:554
  165.6 3.6 %collective-permute-start.72 = (bf16[48,512]{1,0:T(8,128)(2,1)S(1)}, bf16[48,512]{1,0:T(8,128)(2,1)S(1)}, u32[]{:S(2)}, u32[]{:S(2)}) collective-permute-start(bf16[48,512]{1,0:T(8,128)(2,1)S(1)} %score.7.refs_8_), channel_id=1, source_target_pairs={{0,1},{1,0},{2,3},{3,2},{4,5},{5,4},{6,7},{7,6},{8,9},{9,8},{10,11... | collective-permute-start | bytes 147464 | tf_op jit(solution)/shard_map/ppermute | solution.py:554
  166.5 3.4 %collective-permute-start.80 = (f32[48,128]{1,0:T(8,128)S(1)}, f32[48,128]{1,0:T(8,128)S(1)}, u32[]{:S(2)}, u32[]{:S(2)}) collective-permute-start(f32[48,128]{1,0:T(8,128)S(1)} %finish.3.refs_0_), channel_id=1, source_target_pairs={{0,3},{1,2},{2,1},{3,0},{4,7},{5,6},{6,5},{7,4},{8,11},{9,10},{10,... | collective-permute-start | bytes 73736 | tf_op jit(solution)/shard_map/ppermute | solution.py:554
  167.2 3.8 %collective-permute-start.79 = (f32[48,128]{1,0:T(8,128)S(1)}, f32[48,128]{1,0:T(8,128)S(1)}, u32[]{:S(2)}, u32[]{:S(2)}) collective-permute-start(f32[48,128]{1,0:T(8,128)S(1)} %finish.3.refs_0_), channel_id=1, source_target_pairs={{0,2},{1,3},{2,0},{3,1},{4,6},{5,7},{6,4},{7,5},{8,10},{9,11},{10,... | collective-permute-start | bytes 73736 | tf_op jit(solution)/shard_map/ppermute | solution.py:554
  168.6 2.4 %collective-permute-start.78 = (f32[48,128]{1,0:T(8,128)S(1)}, f32[48,128]{1,0:T(8,128)S(1)}, u32[]{:S(2)}, u32[]{:S(2)}) collective-permute-start(f32[48,128]{1,0:T(8,128)S(1)} %finish.3.refs_0_), channel_id=1, source_target_pairs={{0,1},{1,0},{2,3},{3,2},{4,5},{5,4},{6,7},{7,6},{8,9},{9,8},{10,11... | collective-permute-start | bytes 73736 | tf_op jit(solution)/shard_map/ppermute | solution.py:554
  (30 other events, 150.0 us)
Sparse Core Ops, SparseCore 0:
  8.9 112.7 all-gather.1

commit v5 on v4

--- a/solution.py
+++ b/solution.py
@@ -386,16 +386,20 @@
                         target[...] = source[...]
 
     if load:
-        for i, r in enumerate(ring_order(groups)):
-            pltpu.make_async_copy(up.at[i], kept[0].at[r], sems[1].at[r]).start()
-        up = kept[0]
+        order = ring_order(groups)
+        fetch = lambda r: pltpu.make_async_copy(arrived.at[order.index(r)], kept[0].at[r], sems[1].at[r])
+        arrived, up = up, kept[0]
+        for r in range(3):
+            fetch(r).start()
         for t in range(steps):
             target = flat.at[t * rows : (t + 1) * rows]
             pltpu.make_async_copy(target, target, sems[0].at[t]).wait()
     shard = jnp.concatenate([notes[:, SHARD : SHARD + 1].astype(jnp.int32)] * steps, 0)
     for r in range(groups):
         if load:
-            pltpu.make_async_copy(up.at[r], up.at[r], sems[1].at[r]).wait()
+            fetch(r).wait()
+            if r + 3 < groups:
+                fetch(r + 3).start()
         for at in range(0, hidden, COLUMNS):
             end = min(at + COLUMNS, hidden)
             here = jnp.where(shard == r, dot(flat[...], up[r, :, at:end]), 0.0)

time: 197 us -> 195 us (0.990)
  Pallas kernels: 76 us -> 73.9 us
    pallas_call x2, Pallas kernels: 10.9 us -> 8.84 us  [score(): pl.pallas_call(functools.partial(score_kernel, steps, load, mp), out_shap...]
  transfers between devices with their start and end apart: 45 -> 45, of which waited for: 17 -> 19; matrix products, arithmetic and copies ran while one was open for 1% -> 1% of each run, Pallas kernels for 39% -> 38%
where the time goes in v5:
time: 195 us; the launch traced here: 191 us
  Pallas kernels  73.9 us (38%)
  waiting for transfers between devices  47.9 us (25%)
  starting transfers between devices  37.9 us (19%)
  between operations  15.6 us (8%)
  blocking collectives  12.3 us (6%)
    ppermute x8, waiting for transfers between devices, run(): lax.ppermute(sent, 'mp', pairs(mp, k))  38.7 us
    pallas_call x8, Pallas kernels, expand(): pl.pallas_call(functools.partial(step_kernel, step), out_shape=(struct((s...  32.4 us
    ppermute x8, starting transfers between devices, run(): lax.ppermute(sent, 'mp', pairs(mp, k))  13.7 us
    ppermute x7, starting transfers between devices, shards(): lax.ppermute(blocks[k], 'dp', pairs(groups, k))  12.5 us
    all_to_all x1, blocking collectives, shards(): table = lax.all_to_all(table, 'dp', split_axis=0, concat_axis=0, tiled=True)  12.3 us
    pallas_call x8, Pallas kernels, project_own(): pl.pallas_call(project_kernel, out_shape=struct((rows, w_out.shape[1] //...  11 us
    pallas_call x8, Pallas kernels, begin(): pl.pallas_call(begin_kernel, out_shape=struct((slots, w_query.shape[1] +...  10 us
    pallas_call x2, Pallas kernels, score(): pl.pallas_call(functools.partial(score_kernel, steps, load, mp), out_shap...  8.84 us
  transfers between devices with their start and end apart: 45, of which 19 were waited for; matrix products, arithmetic and copies ran while one was open for 1% of the time, Pallas kernels for 38%

profile of v5, /device:TPU:0, one launch (start us, length us, event | category | flops | bytes accessed | tf_op | source)
XLA Modules:
  0.0 191.4 jit_solution(9045239765324419123)
XLA Ops:
  9.4 3.0 %collective-permute-start.37 = (bf16[8,3072]{1,0:T(8,128)(2,1)S(1)}, bf16[8,3072]{1,0:T(8,128)(2,1)S(1)}, u32[]{:S(2)}, u32[]{:S(2)}) collective-permute-start(bf16[8,3072]{1,0:T(8,128)(2,1)S(1)} %get-tuple-element.270), channel_id=1, source_target_pairs={{0,4},{4,0},{8,12},{12,8},{16,20},{20,16},{24,28},{28,24},{1,5},{5... | collective-permute-start | bytes 147464 | tf_op jit(solution)/shard_map/ppermute | solution.py:540
  14.1 3.0 %collective-permute-start.40 = (bf16[8,3072]{1,0:T(8,128)(2,1)S(1)}, bf16[8,3072]{1,0:T(8,128)(2,1)S(1)}, u32[]{:S(2)}, u32[]{:S(2)}) collective-permute-start(bf16[8,3072]{1,0:T(8,128)(2,1)S(1)} %get-tuple-element.273), channel_id=1, source_target_pairs={{0,16},{4,20},{8,24},{12,28},{16,0},{20,4},{24,8},{28,12},{1,17},{... | collective-permute-start | bytes 147464 | tf_op jit(solution)/shard_map/ppermute | solution.py:540
  18.3 3.6 %collective-permute-start.42 = (bf16[8,3072]{1,0:T(8,128)(2,1)S(1)}, bf16[8,3072]{1,0:T(8,128)(2,1)S(1)}, u32[]{:S(2)}, u32[]{:S(2)}) collective-permute-start(bf16[8,3072]{1,0:T(8,128)(2,1)S(1)} %get-tuple-element.275), channel_id=1, source_target_pairs={{0,24},{4,28},{8,16},{12,20},{16,8},{20,12},{24,0},{28,4},{1,25},{... | collective-permute-start | bytes 147464 | tf_op jit(solution)/shard_map/ppermute | solution.py:540
  21.9 7.7 %load.3 = (bf16[5120,768]{1,0:T(8,128)(2,1)S(1)}, bf16[5120,256]{1,0:T(8,128)(2,1)S(1)}, bf16[5120,256]{1,0:T(8,128)(2,1)S(1)}, bf16[2048,256]{1,0:T(8,128)(2,1)...) custom-call(bf16[5120,768]{1,0:T(8,128)(2,1)} %refs_0_, bf16[5120,256]{1,0:T(8,128)(2,1)} %refs_1_, ...), custom_call_target="tpu_custom_call" | custom-call | bytes 25165824 | tf_op jit(solution)/shard_map/load/pallas_call | solution.py:223
  32.3 4.5 %expand.24 = (bf16[48,2560]{1,0:T(8,128)(2,1)S(1)}, bf16[64,768]{1,0:T(8,128)(2,1)S(1)}, bf16[48,256]{1,0:T(8,128)(2,1)S(1)}, bf16[48,256]{1,0:T(8,128)(2,1)S(1)}, f32[48,128]{1,0:T(8,128)}) custom-call(bf16[48,2560]{1,0:T(8,128)(2,1)S(1)} %get-tuple-element.298.own, bf16[48,2560]{1,0:T(8,128)(2,1)S(1)} %collective-permute-done.44.peer, ...), custom_call_target="tpu_custom_call" | custom-call | tf_op jit(solution)/shard_map/expand/pallas_call | solution.py:334
  38.4 1.7 collective-permute-start.46
  42.0 4.0 %collective-permute-done.49.refs_7_ = f32[8,128]{1,0:T(8,128)S(1)} collective-permute-done((f32[8,128]{1,0:T(8,128)S(1)}, f32[8,128]{1,0:T(8,128)S(1)}, u32[]{:S(2)}, u32[]{:S(2)}) %collective-permute-start.49) | collective-permute-done | bytes 4128 | tf_op jit(solution)/shard_map/ppermute | solution.py:558
  48.5 3.9 %expand.25 = (bf16[48,2560]{1,0:T(8,128)(2,1)S(1)}, bf16[64,768]{1,0:T(8,128)(2,1)S(1)}, bf16[48,256]{1,0:T(8,128)(2,1)S(1)}, bf16[48,256]{1,0:T(8,128)(2,1)S(1)}, f32[48,128]{1,0:T(8,128)S(1)}) custom-call(bf16[48,2560]{1,0:T(8,128)(2,1)S(1)} %fusion.4.own.refs_0_, bf16[48,2560]{1,0:T(8,128)(2,1)S(1)} %collective-permute-done.50.peer.refs_7_, ...), custom_call_target="tpu_custom_call" | custom-call | tf_op jit(solution)/shard_map/expand/pallas_call | solution.py:334
  54.1 1.7 collective-permute-start.52
  55.8 6.5 %collective-permute-done.52 = bf16[48,2560]{1,0:T(8,128)(2,1)S(1)} collective-permute-done((bf16[48,2560]{1,0:T(8,128)(2,1)S(1)}, bf16[48,2560]{1,0:T(8,128)(2,1)S(1)}, u32[]{:S(2)}, u32[]{:S(2)}) %collective-permute-start.52) | collective-permute-done | bytes 245792 | tf_op jit(solution)/shard_map/ppermute | solution.py:571
  64.0 3.9 %expand.26 = (bf16[48,2560]{1,0:T(8,128)(2,1)S(1)}, bf16[64,768]{1,0:T(8,128)(2,1)S(1)}, bf16[48,256]{1,0:T(8,128)(2,1)S(1)}, bf16[48,256]{1,0:T(8,128)(2,1)S(1)}, f32[48,128]{1,0:T(8,128)S(1)}) custom-call(bf16[48,2560]{1,0:T(8,128)(2,1)S(1)} %get-tuple-element.397.own.refs_1_, bf16[48,2560]{1,0:T(8,128)(2,1)S(1)} %collective-permute-done.53.peer.refs_8_, ...), custom_call_target="tpu_custom_call" | custom-call | tf_op jit(solution)/shard_map/expand/pallas_call | solution.py:334
  69.6 1.7 collective-permute-start.55
  71.3 6.5 %collective-permute-done.55 = bf16[48,2560]{1,0:T(8,128)(2,1)S(1)} collective-permute-done((bf16[48,2560]{1,0:T(8,128)(2,1)S(1)}, bf16[48,2560]{1,0:T(8,128)(2,1)S(1)}, u32[]{:S(2)}, u32[]{:S(2)}) %collective-permute-start.55) | collective-permute-done | bytes 245792 | tf_op jit(solution)/shard_map/ppermute | solution.py:571
  79.4 3.9 %expand.27 = (bf16[48,2560]{1,0:T(8,128)(2,1)S(1)}, bf16[64,768]{1,0:T(8,128)(2,1)S(1)}, bf16[48,256]{1,0:T(8,128)(2,1)S(1)}, bf16[48,256]{1,0:T(8,128)(2,1)S(1)}, f32[48,128]{1,0:T(8,128)S(1)}) custom-call(bf16[48,2560]{1,0:T(8,128)(2,1)S(1)} %fusion.5.own.refs_2_, bf16[48,2560]{1,0:T(8,128)(2,1)S(1)} %collective-permute-done.56.peer.refs_9_, ...), custom_call_target="tpu_custom_call" | custom-call | tf_op jit(solution)/shard_map/expand/pallas_call | solution.py:334
  83.7 1.8 project_own.27
  85.6 1.7 collective-permute-start.58
  87.3 6.5 %collective-permute-done.58 = bf16[48,2560]{1,0:T(8,128)(2,1)S(1)} collective-permute-done((bf16[48,2560]{1,0:T(8,128)(2,1)S(1)}, bf16[48,2560]{1,0:T(8,128)(2,1)S(1)}, u32[]{:S(2)}, u32[]{:S(2)}) %collective-permute-start.58) | collective-permute-done | bytes 245792 | tf_op jit(solution)/shard_map/ppermute | solution.py:571
  95.5 3.9 %expand.28 = (bf16[48,2560]{1,0:T(8,128)(2,1)S(1)}, bf16[64,768]{1,0:T(8,128)(2,1)S(1)}, bf16[48,256]{1,0:T(8,128)(2,1)S(1)}, bf16[48,256]{1,0:T(8,128)(2,1)S(1)}, f32[48,128]{1,0:T(8,128)S(1)}) custom-call(bf16[48,2560]{1,0:T(8,128)(2,1)S(1)} %get-tuple-element.395.own.refs_3_, bf16[48,2560]{1,0:T(8,128)(2,1)S(1)} %collective-permute-done.59.peer.refs_10_, ...), custom_call_target="tpu_custom_call" | custom-call | tf_op jit(solution)/shard_map/expand/pallas_call | solution.py:334
  101.1 1.7 collective-permute-start.61
  102.9 6.4 %collective-permute-done.61 = bf16[48,2560]{1,0:T(8,128)(2,1)S(1)} collective-permute-done((bf16[48,2560]{1,0:T(8,128)(2,1)S(1)}, bf16[48,2560]{1,0:T(8,128)(2,1)S(1)}, u32[]{:S(2)}, u32[]{:S(2)}) %collective-permute-start.61) | collective-permute-done | bytes 245792 | tf_op jit(solution)/shard_map/ppermute | solution.py:571
  111.0 4.0 %expand.29 = (bf16[48,2560]{1,0:T(8,128)(2,1)S(1)}, bf16[64,768]{1,0:T(8,128)(2,1)S(1)}, bf16[48,256]{1,0:T(8,128)(2,1)S(1)}, bf16[48,256]{1,0:T(8,128)(2,1)S(1)}, f32[48,128]{1,0:T(8,128)S(1)}) custom-call(bf16[48,2560]{1,0:T(8,128)(2,1)S(1)} %fusion.6.own.refs_4_, bf16[48,2560]{1,0:T(8,128)(2,1)S(1)} %collective-permute-done.62.peer.refs_11_, ...), custom_call_target="tpu_custom_call" | custom-call | tf_op jit(solution)/shard_map/expand/pallas_call | solution.py:334
  116.7 1.7 collective-permute-start.64
  118.4 6.5 %collective-permute-done.64 = bf16[48,2560]{1,0:T(8,128)(2,1)S(1)} collective-permute-done((bf16[48,2560]{1,0:T(8,128)(2,1)S(1)}, bf16[48,2560]{1,0:T(8,128)(2,1)S(1)}, u32[]{:S(2)}, u32[]{:S(2)}) %collective-permute-start.64) | collective-permute-done | bytes 245792 | tf_op jit(solution)/shard_map/ppermute | solution.py:571
  126.6 4.0 %expand.30 = (bf16[48,2560]{1,0:T(8,128)(2,1)S(1)}, bf16[64,768]{1,0:T(8,128)(2,1)S(1)}, bf16[48,256]{1,0:T(8,128)(2,1)S(1)}, bf16[48,256]{1,0:T(8,128)(2,1)S(1)}, f32[48,128]{1,0:T(8,128)S(1)}) custom-call(bf16[48,2560]{1,0:T(8,128)(2,1)S(1)} %get-tuple-element.393.own.refs_5_, bf16[48,2560]{1,0:T(8,128)(2,1)S(1)} %collective-permute-done.65.peer.refs_12_, ...), custom_call_target="tpu_custom_call" | custom-call | tf_op jit(solution)/shard_map/expand/pallas_call | solution.py:334
  132.5 1.7 collective-permute-start.67
  134.2 6.5 %collective-permute-done.67 = bf16[48,2560]{1,0:T(8,128)(2,1)S(1)} collective-permute-done((bf16[48,2560]{1,0:T(8,128)(2,1)S(1)}, bf16[48,2560]{1,0:T(8,128)(2,1)S(1)}, u32[]{:S(2)}, u32[]{:S(2)}) %collective-permute-start.67) | collective-permute-done | bytes 245792 | tf_op jit(solution)/shard_map/ppermute | solution.py:571
  142.3 4.4 %expand.31 = (bf16[48,2560]{1,0:T(8,128)(2,1)S(1)}, bf16[64,768]{1,0:T(8,128)(2,1)S(1)}, bf16[48,256]{1,0:T(8,128)(2,1)}, bf16[48,256]{1,0:T(8,128)(2,1)}, f32[48,128]{1,0:T(8,128)S(1)}) custom-call(bf16[48,2560]{1,0:T(8,128)(2,1)S(1)} %fusion.7.own.refs_6_, bf16[48,2560]{1,0:T(8,128)(2,1)S(1)} %collective-permute-done.68.peer.refs_13_, ...), custom_call_target="tpu_custom_call" | custom-call | tf_op jit(solution)/shard_map/expand/pallas_call | solution.py:334
  148.4 1.7 collective-permute-start.70
  150.1 6.9 %score.6 = (bf16[336,128]{1,0:T(8,128)(2,1)S(1)}, bf16[336,128]{1,0:T(8,128)(2,1)S(1)}, bf16[336,128]{1,0:T(8,128)(2,1)S(1)}, bf16[336,128]{1,0:T(8,128)(2,1)S(1)}, bf16[8,1280,512]{2,1,0:T(8,128)(2,1)S(1)}) custom-call(f32[48,128]{1,0:T(8,128)S(1)} %get-tuple-element.297.notes, bf16[8,1280,512]{2,1,0:T(8,128)(2,1)} %all-gather.2.cloned.1.call-done.up, ...), custom_call_target="tpu_custom_call" | custom-call | tf_op jit(solution)/shard_map/score/pallas_call | solution.py:427
  159.2 1.9 %score.7.refs_8_ = bf16[48,512]{1,0:T(8,128)(2,1)S(1)} custom-call(f32[48,128]{1,0:T(8,128)S(1)} %get-tuple-element.297.notes, bf16[8,1280,512]{2,1,0:T(8,128)(2,1)S(1)} %get-tuple-element.340.up, bf16[48,2560]{1,0:T(8,128)(2,1)S(1)} %add_convert_fusion.9.refs_0_.own_row, bf16[48,2560]{1,0:T(8,128)(2,1)S(1)} %collective-permute-done.71.refs_1_.peer_row), custom_call_target="tpu_custom_call" | custom-call | tf_op jit(solution)/shard_map/score/pallas_call | solution.py:427
  167.8 1.7 collective-permute-done.79.refs_2_
  171.4 12.3 %all_to_all.9 = f32[8,8,128]{2,1,0:T(8,128)S(1)} all-to-all(f32[8,8,128]{2,1,0:T(8,128)S(1)} %bitcast.30), channel_id=1, replica_groups=mesh['dp'=8,'mp'=4] {'dp'}, dimensions={0} | all-to-all | bytes 65536 | tf_op jit(solution)/shard_map/all_to_all | solution.py:596
  (144 shorter events, 45.0 us)
Async XLA Ops:
  6.5 143.5 %all-gather.2.cloned.1.call-start = ((), (), s32[]{:S(2)}) async-start(), calls=%async_computation.1 | async-start | bytes 11796480 | tf_op jit(solution)/shard_map/all_gather | solution.py:533
  9.4 8.9 %collective-permute-start.37 = (bf16[8,3072]{1,0:T(8,128)(2,1)S(1)}, bf16[8,3072]{1,0:T(8,128)(2,1)S(1)}, u32[]{:S(2)}, u32[]{:S(2)}) collective-permute-start(bf16[8,3072]{1,0:T(8,128)(2,1)S(1)} %get-tuple-element.270), channel_id=1, source_target_pairs={{0,4},{4,0},{8,12},{12,8},{16,20},{20,16},{24,28},{28,24},{1,5},{5... | collective-permute-start | bytes 147464 | tf_op jit(solution)/shard_map/ppermute | solution.py:540
  12.5 9.5 %collective-permute-start.38 = (bf16[8,3072]{1,0:T(8,128)(2,1)S(1)}, bf16[8,3072]{1,0:T(8,128)(2,1)S(1)}, u32[]{:S(2)}, u32[]{:S(2)}) collective-permute-start(bf16[8,3072]{1,0:T(8,128)(2,1)S(1)} %get-tuple-element.271), channel_id=1, source_target_pairs={{0,8},{4,12},{8,0},{12,4},{16,24},{20,28},{24,16},{28,20},{1,9},{5... | collective-permute-start | bytes 147464 | tf_op jit(solution)/shard_map/ppermute | solution.py:540
  14.1 15.6 %collective-permute-start.39 = (bf16[8,3072]{1,0:T(8,128)(2,1)S(1)}, bf16[8,3072]{1,0:T(8,128)(2,1)S(1)}, u32[]{:S(2)}, u32[]{:S(2)}) collective-permute-start(bf16[8,3072]{1,0:T(8,128)(2,1)S(1)} %get-tuple-element.272), channel_id=1, source_target_pairs={{0,12},{4,8},{8,4},{12,0},{16,28},{20,24},{24,20},{28,16},{1,13},{... | collective-permute-start | bytes 147464 | tf_op jit(solution)/shard_map/ppermute | solution.py:540
  14.1 15.6 %collective-permute-start.40 = (bf16[8,3072]{1,0:T(8,128)(2,1)S(1)}, bf16[8,3072]{1,0:T(8,128)(2,1)S(1)}, u32[]{:S(2)}, u32[]{:S(2)}) collective-permute-start(bf16[8,3072]{1,0:T(8,128)(2,1)S(1)} %get-tuple-element.273), channel_id=1, source_target_pairs={{0,16},{4,20},{8,24},{12,28},{16,0},{20,4},{24,8},{28,12},{1,17},{... | collective-permute-start | bytes 147464 | tf_op jit(solution)/shard_map/ppermute | solution.py:540
  17.0 12.7 %collective-permute-start.41 = (bf16[8,3072]{1,0:T(8,128)(2,1)S(1)}, bf16[8,3072]{1,0:T(8,128)(2,1)S(1)}, u32[]{:S(2)}, u32[]{:S(2)}) collective-permute-start(bf16[8,3072]{1,0:T(8,128)(2,1)S(1)} %get-tuple-element.274), channel_id=1, source_target_pairs={{0,20},{4,16},{8,28},{12,24},{16,4},{20,0},{24,12},{28,8},{1,21},{... | collective-permute-start | bytes 147464 | tf_op jit(solution)/shard_map/ppermute | solution.py:540
  18.3 11.4 %collective-permute-start.42 = (bf16[8,3072]{1,0:T(8,128)(2,1)S(1)}, bf16[8,3072]{1,0:T(8,128)(2,1)S(1)}, u32[]{:S(2)}, u32[]{:S(2)}) collective-permute-start(bf16[8,3072]{1,0:T(8,128)(2,1)S(1)} %get-tuple-element.275), channel_id=1, source_target_pairs={{0,24},{4,28},{8,16},{12,20},{16,8},{20,12},{24,0},{28,4},{1,25},{... | collective-permute-start | bytes 147464 | tf_op jit(solution)/shard_map/ppermute | solution.py:540
  21.9 7.8 %collective-permute-start.43 = (bf16[8,3072]{1,0:T(8,128)(2,1)S(1)}, bf16[8,3072]{1,0:T(8,128)(2,1)S(1)}, u32[]{:S(2)}, u32[]{:S(2)}) collective-permute-start(bf16[8,3072]{1,0:T(8,128)(2,1)S(1)} %get-tuple-element.276), channel_id=1, source_target_pairs={{0,28},{4,24},{8,20},{12,16},{16,12},{20,8},{24,4},{28,0},{1,29},{... | collective-permute-start | bytes 147464 | tf_op jit(solution)/shard_map/ppermute | solution.py:540
  38.4 8.4 %collective-permute-start.46 = (bf16[48,2560]{1,0:T(8,128)(2,1)S(1)}, bf16[48,2560]{1,0:T(8,128)(2,1)S(1)}, u32[]{:S(2)}, u32[]{:S(2)}) collective-permute-start(bf16[48,2560]{1,0:T(8,128)(2,1)S(1)} %add_convert_fusion.17), channel_id=1, source_target_pairs={{0,2},{1,3},{2,0},{3,1},{4,6},{5,7},{6,4},{7,5},{8,10},{9,11},{10,... | collective-permute-start | bytes 737288 | tf_op jit(solution)/shard_map/ppermute | solution.py:571
  40.2 5.9 %collective-permute-start.49 = (f32[8,128]{1,0:T(8,128)S(1)}, f32[8,128]{1,0:T(8,128)S(1)}, u32[]{:S(2)}, u32[]{:S(2)}) collective-permute-start(f32[8,128]{1,0:T(8,128)S(1)} %get-tuple-element.360.scale.refs_4_), channel_id=1, source_target_pairs={{0,3},{1,2},{2,1},{3,0},{4,7},{5,6},{6,5},{7,4},{8,11},{9,10},{10,... | collective-permute-start | bytes 12296 | tf_op jit(solution)/shard_map/ppermute | solution.py:558
  40.2 6.6 %collective-permute-start.48 = (f32[8,128]{1,0:T(8,128)S(1)}, f32[8,128]{1,0:T(8,128)S(1)}, u32[]{:S(2)}, u32[]{:S(2)}) collective-permute-start(f32[8,128]{1,0:T(8,128)S(1)} %get-tuple-element.360.scale.refs_4_), channel_id=1, source_target_pairs={{0,2},{1,3},{2,0},{3,1},{4,6},{5,7},{6,4},{7,5},{8,10},{9,11},{10,... | collective-permute-start | bytes 12296 | tf_op jit(solution)/shard_map/ppermute | solution.py:558
  41.8 5.0 %collective-permute-start.47 = (f32[8,128]{1,0:T(8,128)S(1)}, f32[8,128]{1,0:T(8,128)S(1)}, u32[]{:S(2)}, u32[]{:S(2)}) collective-permute-start(f32[8,128]{1,0:T(8,128)S(1)} %get-tuple-element.360.scale.refs_4_), channel_id=1, source_target_pairs={{0,1},{1,0},{2,3},{3,2},{4,5},{5,4},{6,7},{7,6},{8,9},{9,8},{10,11... | collective-permute-start | bytes 12296 | tf_op jit(solution)/shard_map/ppermute | solution.py:558
  54.1 8.2 %collective-permute-start.52 = (bf16[48,2560]{1,0:T(8,128)(2,1)S(1)}, bf16[48,2560]{1,0:T(8,128)(2,1)S(1)}, u32[]{:S(2)}, u32[]{:S(2)}) collective-permute-start(bf16[48,2560]{1,0:T(8,128)(2,1)S(1)} %add_convert_fusion.16), channel_id=1, source_target_pairs={{0,2},{1,3},{2,0},{3,1},{4,6},{5,7},{6,4},{7,5},{8,10},{9,11},{10,... | collective-permute-start | bytes 737288 | tf_op jit(solution)/shard_map/ppermute | solution.py:571
  69.6 8.2 %collective-permute-start.55 = (bf16[48,2560]{1,0:T(8,128)(2,1)S(1)}, bf16[48,2560]{1,0:T(8,128)(2,1)S(1)}, u32[]{:S(2)}, u32[]{:S(2)}) collective-permute-start(bf16[48,2560]{1,0:T(8,128)(2,1)S(1)} %add_convert_fusion.15), channel_id=1, source_target_pairs={{0,2},{1,3},{2,0},{3,1},{4,6},{5,7},{6,4},{7,5},{8,10},{9,11},{10,... | collective-permute-start | bytes 737288 | tf_op jit(solution)/shard_map/ppermute | solution.py:571
  83.4 2.2 %collective-permute-start.57 = (bf16[48,2560]{1,0:T(8,128)(2,1)S(1)}, bf16[48,2560]{1,0:T(8,128)(2,1)S(1)}, u32[]{:S(2)}, u32[]{:S(2)}) collective-permute-start(bf16[48,2560]{1,0:T(8,128)(2,1)S(1)} %get-tuple-element.322), channel_id=1, source_target_pairs={{0,1},{1,0},{2,3},{3,2},{4,5},{5,4},{6,7},{7,6},{8,9},{9,8},{10,11... | collective-permute-start | bytes 737288 | tf_op jit(solution)/shard_map/ppermute | solution.py:568
  85.6 8.2 %collective-permute-start.58 = (bf16[48,2560]{1,0:T(8,128)(2,1)S(1)}, bf16[48,2560]{1,0:T(8,128)(2,1)S(1)}, u32[]{:S(2)}, u32[]{:S(2)}) collective-permute-start(bf16[48,2560]{1,0:T(8,128)(2,1)S(1)} %add_convert_fusion.14), channel_id=1, source_target_pairs={{0,2},{1,3},{2,0},{3,1},{4,6},{5,7},{6,4},{7,5},{8,10},{9,11},{10,... | collective-permute-start | bytes 737288 | tf_op jit(solution)/shard_map/ppermute | solution.py:571
  99.4 1.7 collective-permute-start.60
  101.1 8.2 %collective-permute-start.61 = (bf16[48,2560]{1,0:T(8,128)(2,1)S(1)}, bf16[48,2560]{1,0:T(8,128)(2,1)S(1)}, u32[]{:S(2)}, u32[]{:S(2)}) collective-permute-start(bf16[48,2560]{1,0:T(8,128)(2,1)S(1)} %add_convert_fusion.13), channel_id=1, source_target_pairs={{0,2},{1,3},{2,0},{3,1},{4,6},{5,7},{6,4},{7,5},{8,10},{9,11},{10,... | collective-permute-start | bytes 737288 | tf_op jit(solution)/shard_map/ppermute | solution.py:571
  116.7 8.2 %collective-permute-start.64 = (bf16[48,2560]{1,0:T(8,128)(2,1)S(1)}, bf16[48,2560]{1,0:T(8,128)(2,1)S(1)}, u32[]{:S(2)}, u32[]{:S(2)}) collective-permute-start(bf16[48,2560]{1,0:T(8,128)(2,1)S(1)} %add_convert_fusion.12), channel_id=1, source_target_pairs={{0,2},{1,3},{2,0},{3,1},{4,6},{5,7},{6,4},{7,5},{8,10},{9,11},{10,... | collective-permute-start | bytes 737288 | tf_op jit(solution)/shard_map/ppermute | solution.py:571
  130.6 1.8 collective-permute-start.66
  132.5 8.2 %collective-permute-start.67 = (bf16[48,2560]{1,0:T(8,128)(2,1)S(1)}, bf16[48,2560]{1,0:T(8,128)(2,1)S(1)}, u32[]{:S(2)}, u32[]{:S(2)}) collective-permute-start(bf16[48,2560]{1,0:T(8,128)(2,1)S(1)} %add_convert_fusion.11), channel_id=1, source_target_pairs={{0,2},{1,3},{2,0},{3,1},{4,6},{5,7},{6,4},{7,5},{8,10},{9,11},{10,... | collective-permute-start | bytes 737288 | tf_op jit(solution)/shard_map/ppermute | solution.py:571
  148.4 8.6 %collective-permute-start.70 = (bf16[48,2560]{1,0:T(8,128)(2,1)S(1)}, bf16[48,2560]{1,0:T(8,128)(2,1)S(1)}, u32[]{:S(2)}, u32[]{:S(2)}) collective-permute-start(bf16[48,2560]{1,0:T(8,128)(2,1)S(1)} %add_convert_fusion.10), channel_id=1, source_target_pairs={{0,2},{1,3},{2,0},{3,1},{4,6},{5,7},{6,4},{7,5},{8,10},{9,11},{10,... | collective-permute-start | bytes 737288 | tf_op jit(solution)/shard_map/ppermute | solution.py:571
  157.1 2.0 %collective-permute-start.71 = (bf16[48,2560]{1,0:T(8,128)(2,1)S(1)}, bf16[48,2560]{1,0:T(8,128)(2,1)S(1)}, u32[]{:S(2)}, u32[]{:S(2)}) collective-permute-start(bf16[48,2560]{1,0:T(8,128)(2,1)S(1)} %add_convert_fusion.9.refs_0_.own_row), channel_id=1, source_target_pairs={{0,1},{1,0},{2,3},{3,2},{4,5},{5,4},{6,7},{7,6},{8,9},{9,8},{10,11... | collective-permute-start | bytes 737288 | tf_op jit(solution)/shard_map/ppermute | solution.py:580
  157.2 6.3 %collective-permute-start.75 = (bf16[336,128]{1,0:T(8,128)(2,1)S(1)}, bf16[336,128]{1,0:T(8,128)(2,1)S(1)}, u32[]{:S(2)}, u32[]{:S(2)}) collective-permute-start(bf16[336,128]{1,0:T(8,128)(2,1)S(1)} %get-tuple-element.357), channel_id=1, source_target_pairs={{0,1},{1,0},{2,3},{3,2},{4,5},{5,4},{6,7},{7,6},{8,9},{9,8},{10,11... | collective-permute-start | bytes 258056 | tf_op jit(solution)/shard_map/ppermute | solution.py:558
  157.7 5.8 %collective-permute-start.76 = (bf16[336,128]{1,0:T(8,128)(2,1)S(1)}, bf16[336,128]{1,0:T(8,128)(2,1)S(1)}, u32[]{:S(2)}, u32[]{:S(2)}) collective-permute-start(bf16[336,128]{1,0:T(8,128)(2,1)S(1)} %get-tuple-element.358), channel_id=1, source_target_pairs={{0,2},{1,3},{2,0},{3,1},{4,6},{5,7},{6,4},{7,5},{8,10},{9,11},{10,... | collective-permute-start | bytes 258056 | tf_op jit(solution)/shard_map/ppermute | solution.py:558
  158.9 4.8 %collective-permute-start.77 = (bf16[336,128]{1,0:T(8,128)(2,1)S(1)}, bf16[336,128]{1,0:T(8,128)(2,1)S(1)}, u32[]{:S(2)}, u32[]{:S(2)}) collective-permute-start(bf16[336,128]{1,0:T(8,128)(2,1)S(1)} %get-tuple-element.359), channel_id=1, source_target_pairs={{0,3},{1,2},{2,1},{3,0},{4,7},{5,6},{6,5},{7,4},{8,11},{9,10},{10,... | collective-permute-start | bytes 258056 | tf_op jit(solution)/shard_map/ppermute | solution.py:558
  161.1 5.5 %collective-permute-start.74 = (bf16[48,512]{1,0:T(8,128)(2,1)S(1)}, bf16[48,512]{1,0:T(8,128)(2,1)S(1)}, u32[]{:S(2)}, u32[]{:S(2)}) collective-permute-start(bf16[48,512]{1,0:T(8,128)(2,1)S(1)} %score.7.refs_8_), channel_id=1, source_target_pairs={{0,3},{1,2},{2,1},{3,0},{4,7},{5,6},{6,5},{7,4},{8,11},{9,10},{10,... | collective-permute-start | bytes 147464 | tf_op jit(solution)/shard_map/ppermute | solution.py:558
  162.6 4.5 %collective-permute-start.73 = (bf16[48,512]{1,0:T(8,128)(2,1)S(1)}, bf16[48,512]{1,0:T(8,128)(2,1)S(1)}, u32[]{:S(2)}, u32[]{:S(2)}) collective-permute-start(bf16[48,512]{1,0:T(8,128)(2,1)S(1)} %score.7.refs_8_), channel_id=1, source_target_pairs={{0,2},{1,3},{2,0},{3,1},{4,6},{5,7},{6,4},{7,5},{8,10},{9,11},{10,... | collective-permute-start | bytes 147464 | tf_op jit(solution)/shard_map/ppermute | solution.py:558
  163.5 3.6 %collective-permute-start.72 = (bf16[48,512]{1,0:T(8,128)(2,1)S(1)}, bf16[48,512]{1,0:T(8,128)(2,1)S(1)}, u32[]{:S(2)}, u32[]{:S(2)}) collective-permute-start(bf16[48,512]{1,0:T(8,128)(2,1)S(1)} %score.7.refs_8_), channel_id=1, source_target_pairs={{0,1},{1,0},{2,3},{3,2},{4,5},{5,4},{6,7},{7,6},{8,9},{9,8},{10,11... | collective-permute-start | bytes 147464 | tf_op jit(solution)/shard_map/ppermute | solution.py:558
  164.5 3.3 %collective-permute-start.80 = (f32[48,128]{1,0:T(8,128)S(1)}, f32[48,128]{1,0:T(8,128)S(1)}, u32[]{:S(2)}, u32[]{:S(2)}) collective-permute-start(f32[48,128]{1,0:T(8,128)S(1)} %finish.3.refs_0_), channel_id=1, source_target_pairs={{0,3},{1,2},{2,1},{3,0},{4,7},{5,6},{6,5},{7,4},{8,11},{9,10},{10,... | collective-permute-start | bytes 73736 | tf_op jit(solution)/shard_map/ppermute | solution.py:558
  165.7 3.8 %collective-permute-start.79 = (f32[48,128]{1,0:T(8,128)S(1)}, f32[48,128]{1,0:T(8,128)S(1)}, u32[]{:S(2)}, u32[]{:S(2)}) collective-permute-start(f32[48,128]{1,0:T(8,128)S(1)} %finish.3.refs_0_), channel_id=1, source_target_pairs={{0,2},{1,3},{2,0},{3,1},{4,6},{5,7},{6,4},{7,5},{8,10},{9,11},{10,... | collective-permute-start | bytes 73736 | tf_op jit(solution)/shard_map/ppermute | solution.py:558
  166.6 2.9 %collective-permute-start.78 = (f32[48,128]{1,0:T(8,128)S(1)}, f32[48,128]{1,0:T(8,128)S(1)}, u32[]{:S(2)}, u32[]{:S(2)}) collective-permute-start(f32[48,128]{1,0:T(8,128)S(1)} %finish.3.refs_0_), channel_id=1, source_target_pairs={{0,1},{1,0},{2,3},{3,2},{4,5},{5,4},{6,7},{7,6},{8,9},{9,8},{10,11... | collective-permute-start | bytes 73736 | tf_op jit(solution)/shard_map/ppermute | solution.py:558
  (30 other events, 150.0 us)
Sparse Core Ops, SparseCore 0:
  8.9 112.7 all-gather.1

commit v6 on v5

--- a/solution.py
+++ b/solution.py
@@ -63,7 +63,7 @@
 
 def dispatch_kernel(parents, groups, count, parent_far, shard_far, tokens_far, reward_far, *rest):
     core, own, me = coordinates()
-    blocks, near = rest[:groups], rest[groups:]
+    stay, cross, near = rest[: groups // 2], rest[groups // 2], rest[groups // 2 + 1 :]
     parent_row, shard_row, tokens, reward_out, sems = near
     children, half = tokens.shape
     sources = (parent_far, shard_far, tokens_far.at[:, pl.ds(pl.multiple_of(core * half, half), half)], reward_far)
@@ -72,7 +72,7 @@
         copy.start()
     for copy in copies:
         copy.wait()
-    capacity = blocks[0].shape[0]
+    capacity = stay[0].shape[0]
     everyone = parent_row.shape[1]
     int32, float32, bfloat16 = jnp.int32, jnp.float32, jnp.bfloat16
 
@@ -100,7 +100,7 @@
     for at, value in ((RANK, reward_rank), (SHARD, shard_c), (PARENT, lax.rem(parent_c, parents)), (SOURCE, own)):
         notes = jnp.where(lane == at, value, notes)
 
-    width = blocks[0].shape[1] - half - NOTES
+    width = cross.shape[1] - half - NOTES
     hidden = width // 3
     rest = jnp.zeros((1, hidden), float32)
     for m in range(reward_out.shape[1] // hidden):
@@ -118,19 +118,24 @@
     row = lax.broadcasted_iota(int32, note_rows.shape, 0)
     lane = lax.broadcasted_iota(int32, note_rows.shape, 1)
     note_rows = jnp.where((lax.rem(row, capacity) == 0) & (lane == COUNT), count[0].astype(float32), note_rows)
-    for k, block in enumerate(blocks):
+    every = []
+    for k in range(groups):
         at = slice(k * capacity, (k + 1) * capacity)
-        block[...] = jnp.concatenate([token_rows[at], note_rows[at], shared], 1).astype(bfloat16)
+        every.append(jnp.concatenate([token_rows[at], note_rows[at], shared], 1))
+    for j, block in enumerate(stay):
+        block[...] = every[2 * j].astype(bfloat16)
+    cross[...] = jnp.concatenate(every[1::2], 0).astype(bfloat16)
 
 
 def dispatch(parents, child_count, child_parent, node_shard, tokens, reward_out, groups, capacity, hidden):
     children, half = tokens.shape[0], tokens.shape[1] // 2
+    width = half + NOTES + 3 * hidden
     tables = (child_parent[None], node_shard[None])
     return pl.pallas_call(
         functools.partial(dispatch_kernel, parents, groups),
-        out_shape=(struct((capacity, half + NOTES + 3 * hidden)),) * groups,
+        out_shape=(struct((capacity, width)),) * (groups // 2) + (struct((groups // 2 * capacity, width)),),
         in_specs=[SCALARS] + [FAR] * 4,
-        out_specs=(WHOLE,) * groups,
+        out_specs=(WHOLE,) * (groups // 2 + 1),
         scratch_shapes=[VMEM(x.shape, x.dtype) for x in tables]
         + [VMEM((children, half), tokens.dtype), VMEM(reward_out.shape, reward_out.dtype)]
         + [pltpu.SemaphoreType.DMA((4,))],
@@ -140,6 +145,29 @@
     )(child_count, *map(far, (*tables, tokens, reward_out)))
 
 
+def regroup_kernel(*refs):
+    count = len(refs) // 2
+    stay, cross, pairs = refs[:count], refs[count], refs[count + 1 :]
+    capacity = stay[0].shape[0]
+    for j, (block, pair) in enumerate(zip(stay, pairs)):
+        mine = block[...].astype(jnp.float32)
+        other = cross[...].astype(jnp.float32)[j * capacity : (j + 1) * capacity]
+        pair[...] = jnp.concatenate([mine, other], 0).astype(jnp.bfloat16)
+
+
+def regroup(stay, cross):
+    capacity, width = stay[0].shape
+    return pl.pallas_call(
+        regroup_kernel,
+        out_shape=(struct((2 * capacity, width)),) * len(stay),
+        in_specs=[WHOLE] * (len(stay) + 1),
+        out_specs=(WHOLE,) * len(stay),
+        compiler_params=pltpu.CompilerParams(vmem_limit_bytes=8 << 20),
+        cost_estimate=SMALL,
+        name="regroup",
+    )(*stay, cross)
+
+
 def crossing_first(groups):
     return sorted(range(groups), key=lambda k: -(k ^ (k & 1)))
 
@@ -148,7 +176,7 @@
     blocks, (row, notes, bias, scale, over) = rest[:-5], rest[-5:]
     blocks = [block for _, block in sorted(zip(crossing_first(len(blocks)), blocks), key=lambda pair: pair[0])]
     _, own, _ = coordinates()
-    groups, capacity = len(blocks), blocks[0].shape[0]
+    groups, capacity = 2 * len(blocks), blocks[0].shape[0] // 2
     rows, half = row.shape
     slots = groups * capacity
     arrived = jnp.concatenate([block[...].astype(jnp.float32) for block in blocks], 0)
@@ -190,7 +218,7 @@
 
 def pack(offset, rows, hidden, prefix, blocks_held, child_parent, blocks):
     half = D // 2
-    groups = len(blocks)
+    groups = 2 * len(blocks)
     parents = blocks_held.shape[0] // groups
     return pl.pallas_call(
         functools.partial(pack_kernel, offset, hidden, prefix),
@@ -201,12 +229,12 @@
             struct((groups, hidden), jnp.float32),
             struct((8, 128), jnp.int32),
         ),
-        in_specs=[SCALARS] + [WHOLE] * (1 + groups),
+        in_specs=[SCALARS] + [WHOLE] * (1 + len(blocks)),
         out_specs=[WHOLE] * 5,
         compiler_params=pltpu.CompilerParams(vmem_limit_bytes=12 << 20),
         cost_estimate=SMALL,
         name="pack",
-    )(blocks_held, child_parent[None], *[blocks[k] for k in crossing_first(groups)])
+    )(blocks_held, child_parent[None], *[blocks[k] for k in crossing_first(len(blocks))])
 
 
 def load_kernel(*refs):
@@ -532,13 +560,18 @@
 
     up = lax.all_gather(reward_up[0], "dp", axis=0, axis_index_groups=[ring_order(groups)])
 
-    blocks = dispatch(parents, child_count, child_parent, node_shard, tokens, reward_out, groups, capacity, hidden)
+    *stay, cross = dispatch(
+        parents, child_count, child_parent, node_shard, tokens, reward_out, groups, capacity, hidden
+    )
     keys = parent_keys.reshape(parents * prefix, kv_cols)
     values = parent_values.reshape(parents * prefix, kv_cols)
     raw = (w_query, w_key, w_value, keys, values, w_out)
-    blocks, raw = lax.optimization_barrier((blocks, raw))
-    blocks = [blocks[0]] + [lax.ppermute(blocks[k], "dp", pairs(groups, k)) for k in range(1, groups)]
-    blocks, weights = lax.optimization_barrier((blocks, load(*raw)))
+    cross, raw = lax.optimization_barrier((cross, raw))
+    cross = lax.ppermute(cross, "dp", pairs(groups, 1))
+    stay, cross, early, late = lax.optimization_barrier((stay, cross, load(*raw[:2]), raw[2:]))
+    blocks, late = lax.optimization_barrier((regroup(stay, cross), late))
+    blocks = [blocks[0]] + [lax.ppermute(blocks[j], "dp", pairs(groups, 2 * j)) for j in range(1, groups // 2)]
+    blocks, weights = lax.optimization_barrier((blocks, (*early, *load(*late))))
     gain = attn_gain.reshape(1, width)
 
     def run(offset, weights, blocks, up, gain, child_parent, parent_blocks):

time: 195 us -> 199 us (1.021)
  waiting for transfers between devices: 47.9 us -> 57.9 us
  starting transfers between devices: 37.9 us -> 31.9 us
    ppermute x7 -> x4, waiting for transfers between devices: 0.05 us -> 9.23 us  [the longest x3 8.39 us: shards(): lax.ppermute(blocks[j], 'dp', pairs(groups, 2 * j))]
    ppermute x7 -> x4, starting transfers between devices: 12.5 us -> 7.52 us  [the longest x3 4.46 us: shards(): lax.ppermute(blocks[j], 'dp', pairs(groups, 2 * j))]
    pallas_call x1 -> x2, Pallas kernels: 7.72 us -> 8.75 us  [load(): pl.pallas_call(load_kernel, out_shape=tuple((VMEM(x.shape, x.dtype) for x...]
  transfers between devices with their start and end apart: 45 -> 42, of which waited for: 19 -> 21; matrix products, arithmetic and copies ran while one was open for 1% -> 1% of each run, Pallas kernels for 38% -> 38%
where the time goes in v6:
time: 199 us; the launch traced here: 195 us
  Pallas kernels  75 us (38%)
  waiting for transfers between devices  57.9 us (29%)
  starting transfers between devices  31.9 us (16%)
  between operations  15.6 us (8%)
  blocking collectives  10.7 us (5%)
    ppermute x8, waiting for transfers between devices, run(): lax.ppermute(sent, 'mp', pairs(mp, k))  39.5 us
    pallas_call x8, Pallas kernels, expand(): pl.pallas_call(functools.partial(step_kernel, step), out_shape=(struct((s...  32.5 us
    ppermute x8, starting transfers between devices, run(): lax.ppermute(sent, 'mp', pairs(mp, k))  12.6 us
    pallas_call x8, Pallas kernels, project_own(): pl.pallas_call(project_kernel, out_shape=struct((rows, w_out.shape[1] //...  11 us
    all_to_all x1, blocking collectives, shards(): table = lax.all_to_all(table, 'dp', split_axis=0, concat_axis=0, tiled=True)  10.7 us
    pallas_call x8, Pallas kernels, begin(): pl.pallas_call(begin_kernel, out_shape=struct((slots, w_query.shape[1] +...  10 us
    pallas_call x2, Pallas kernels, score(): pl.pallas_call(functools.partial(score_kernel, steps, load, mp), out_shap...  8.84 us
    pallas_call x2, Pallas kernels, load(): pl.pallas_call(load_kernel, out_shape=tuple((VMEM(x.shape, x.dtype) for x...  8.75 us
  transfers between devices with their start and end apart: 42, of which 21 were waited for; matrix products, arithmetic and copies ran while one was open for 1% of the time, Pallas kernels for 38%

profile of v6, /device:TPU:0, one launch (start us, length us, event | category | flops | bytes accessed | tf_op | source)
XLA Modules:
  0.0 194.9 jit_solution(4644946122476861603)
XLA Ops:
  9.4 3.1 %collective-permute-start.37 = (bf16[32,3072]{1,0:T(8,128)(2,1)S(1)}, bf16[32,3072]{1,0:T(8,128)(2,1)S(1)}, u32[]{:S(2)}, u32[]{:S(2)}) collective-permute-start(bf16[32,3072]{1,0:T(8,128)(2,1)S(1)} %get-tuple-element.259), channel_id=1, source_target_pairs={{0,4},{4,0},{8,12},{12,8},{16,20},{20,16},{24,28},{28,24},{1,5},{5... | collective-permute-start | bytes 589832 | tf_op jit(solution)/shard_map/ppermute | solution.py:570
  12.5 4.0 %load.4 = (bf16[5120,768]{1,0:T(8,128)(2,1)S(1)}, bf16[5120,256]{1,0:T(8,128)(2,1)S(1)}) custom-call(bf16[5120,768]{1,0:T(8,128)(2,1)} %refs_0_, bf16[5120,256]{1,0:T(8,128)(2,1)} %refs_1_), custom_call_target="tpu_custom_call" | custom-call | bytes 25165824 | tf_op jit(solution)/shard_map/load/pallas_call | solution.py:251
  17.4 1.9 collective-permute-start.38
  19.2 2.6 %collective-permute-start.39 = (bf16[16,3072]{1,0:T(8,128)(2,1)S(1)}, bf16[16,3072]{1,0:T(8,128)(2,1)S(1)}, u32[]{:S(2)}, u32[]{:S(2)}) collective-permute-start(bf16[16,3072]{1,0:T(8,128)(2,1)S(1)} %get-tuple-element.283), channel_id=1, source_target_pairs={{0,16},{4,20},{8,24},{12,28},{16,0},{20,4},{24,8},{28,12},{1,17},{... | collective-permute-start | bytes 294920 | tf_op jit(solution)/shard_map/ppermute | solution.py:573
  21.8 4.8 %load.5 = (bf16[5120,256]{1,0:T(8,128)(2,1)S(1)}, bf16[2048,256]{1,0:T(8,128)(2,1)S(1)}, bf16[2048,256]{1,0:T(8,128)(2,1)S(1)}, bf16[768,5120]{1,0:T(8,128)(2,1)S(1)}) custom-call(bf16[5120,256]{1,0:T(8,128)(2,1)} %refs_0_.1, bf16[2048,256]{1,0:T(8,128)(2,1)} %bitcast.26, bf16[2048,256]{1,0:T(8,128)(2,1)} %bitcast.28, bf16[768,5120]{1,0:T(8,128)(2,1)} %refs_3_), custom_call_target="tpu_custom_call" | custom-call | bytes 25165824 | tf_op jit(solution)/shard_map/load/pallas_call | solution.py:251
  26.6 3.3 %collective-permute-done.39.rest_0_ = bf16[16,3072]{1,0:T(8,128)(2,1)S(1)} collective-permute-done((bf16[16,3072]{1,0:T(8,128)(2,1)S(1)}, bf16[16,3072]{1,0:T(8,128)(2,1)S(1)}, u32[]{:S(2)}, u32[]{:S(2)}) %collective-permute-start.39) | collective-permute-done | bytes 98336 | tf_op jit(solution)/shard_map/ppermute | solution.py:573
  29.9 5.1 %collective-permute-done.40.rest_1_ = bf16[16,3072]{1,0:T(8,128)(2,1)S(1)} collective-permute-done((bf16[16,3072]{1,0:T(8,128)(2,1)S(1)}, bf16[16,3072]{1,0:T(8,128)(2,1)S(1)}, u32[]{:S(2)}, u32[]{:S(2)}) %collective-permute-start.40) | collective-permute-done | bytes 98336 | tf_op jit(solution)/shard_map/ppermute | solution.py:573
  37.5 4.5 %expand.24 = (bf16[48,2560]{1,0:T(8,128)(2,1)S(1)}, bf16[64,768]{1,0:T(8,128)(2,1)S(1)}, bf16[48,256]{1,0:T(8,128)(2,1)S(1)}, bf16[48,256]{1,0:T(8,128)(2,1)S(1)}, f32[48,128]{1,0:T(8,128)}) custom-call(bf16[48,2560]{1,0:T(8,128)(2,1)S(1)} %get-tuple-element.300.own, bf16[48,2560]{1,0:T(8,128)(2,1)S(1)} %collective-permute-done.41.peer, ...), custom_call_target="tpu_custom_call" | custom-call | tf_op jit(solution)/shard_map/expand/pallas_call | solution.py:362
  43.7 1.6 collective-permute-start.43
  47.1 4.1 %collective-permute-done.46.refs_7_ = f32[8,128]{1,0:T(8,128)S(1)} collective-permute-done((f32[8,128]{1,0:T(8,128)S(1)}, f32[8,128]{1,0:T(8,128)S(1)}, u32[]{:S(2)}, u32[]{:S(2)}) %collective-permute-start.46) | collective-permute-done | bytes 4128 | tf_op jit(solution)/shard_map/ppermute | solution.py:591
  53.7 3.9 %expand.25 = (bf16[48,2560]{1,0:T(8,128)(2,1)S(1)}, bf16[64,768]{1,0:T(8,128)(2,1)S(1)}, bf16[48,256]{1,0:T(8,128)(2,1)S(1)}, bf16[48,256]{1,0:T(8,128)(2,1)S(1)}, f32[48,128]{1,0:T(8,128)S(1)}) custom-call(bf16[48,2560]{1,0:T(8,128)(2,1)S(1)} %fusion.4.own.refs_0_, bf16[48,2560]{1,0:T(8,128)(2,1)S(1)} %collective-permute-done.47.peer.refs_7_, ...), custom_call_target="tpu_custom_call" | custom-call | tf_op jit(solution)/shard_map/expand/pallas_call | solution.py:362
  59.3 1.6 collective-permute-start.49
  60.9 6.6 %collective-permute-done.49 = bf16[48,2560]{1,0:T(8,128)(2,1)S(1)} collective-permute-done((bf16[48,2560]{1,0:T(8,128)(2,1)S(1)}, bf16[48,2560]{1,0:T(8,128)(2,1)S(1)}, u32[]{:S(2)}, u32[]{:S(2)}) %collective-permute-start.49) | collective-permute-done | bytes 245792 | tf_op jit(solution)/shard_map/ppermute | solution.py:604
  69.3 3.9 %expand.26 = (bf16[48,2560]{1,0:T(8,128)(2,1)S(1)}, bf16[64,768]{1,0:T(8,128)(2,1)S(1)}, bf16[48,256]{1,0:T(8,128)(2,1)S(1)}, bf16[48,256]{1,0:T(8,128)(2,1)S(1)}, f32[48,128]{1,0:T(8,128)S(1)}) custom-call(bf16[48,2560]{1,0:T(8,128)(2,1)S(1)} %get-tuple-element.395.own.refs_1_, bf16[48,2560]{1,0:T(8,128)(2,1)S(1)} %collective-permute-done.50.peer.refs_8_, ...), custom_call_target="tpu_custom_call" | custom-call | tf_op jit(solution)/shard_map/expand/pallas_call | solution.py:362
  74.9 1.6 collective-permute-start.52
  76.4 6.6 %collective-permute-done.52 = bf16[48,2560]{1,0:T(8,128)(2,1)S(1)} collective-permute-done((bf16[48,2560]{1,0:T(8,128)(2,1)S(1)}, bf16[48,2560]{1,0:T(8,128)(2,1)S(1)}, u32[]{:S(2)}, u32[]{:S(2)}) %collective-permute-start.52) | collective-permute-done | bytes 245792 | tf_op jit(solution)/shard_map/ppermute | solution.py:604
  84.7 3.9 %expand.27 = (bf16[48,2560]{1,0:T(8,128)(2,1)S(1)}, bf16[64,768]{1,0:T(8,128)(2,1)S(1)}, bf16[48,256]{1,0:T(8,128)(2,1)S(1)}, bf16[48,256]{1,0:T(8,128)(2,1)S(1)}, f32[48,128]{1,0:T(8,128)S(1)}) custom-call(bf16[48,2560]{1,0:T(8,128)(2,1)S(1)} %fusion.5.own.refs_2_, bf16[48,2560]{1,0:T(8,128)(2,1)S(1)} %collective-permute-done.53.peer.refs_9_, ...), custom_call_target="tpu_custom_call" | custom-call | tf_op jit(solution)/shard_map/expand/pallas_call | solution.py:362
  89.0 1.8 project_own.27
  90.8 1.6 collective-permute-start.55
  92.4 6.6 %collective-permute-done.55 = bf16[48,2560]{1,0:T(8,128)(2,1)S(1)} collective-permute-done((bf16[48,2560]{1,0:T(8,128)(2,1)S(1)}, bf16[48,2560]{1,0:T(8,128)(2,1)S(1)}, u32[]{:S(2)}, u32[]{:S(2)}) %collective-permute-start.55) | collective-permute-done | bytes 245792 | tf_op jit(solution)/shard_map/ppermute | solution.py:604
  100.7 3.9 %expand.28 = (bf16[48,2560]{1,0:T(8,128)(2,1)S(1)}, bf16[64,768]{1,0:T(8,128)(2,1)S(1)}, bf16[48,256]{1,0:T(8,128)(2,1)S(1)}, bf16[48,256]{1,0:T(8,128)(2,1)S(1)}, f32[48,128]{1,0:T(8,128)S(1)}) custom-call(bf16[48,2560]{1,0:T(8,128)(2,1)S(1)} %get-tuple-element.393.own.refs_3_, bf16[48,2560]{1,0:T(8,128)(2,1)S(1)} %collective-permute-done.56.peer.refs_10_, ...), custom_call_target="tpu_custom_call" | custom-call | tf_op jit(solution)/shard_map/expand/pallas_call | solution.py:362
  108.0 6.6 %collective-permute-done.58 = bf16[48,2560]{1,0:T(8,128)(2,1)S(1)} collective-permute-done((bf16[48,2560]{1,0:T(8,128)(2,1)S(1)}, bf16[48,2560]{1,0:T(8,128)(2,1)S(1)}, u32[]{:S(2)}, u32[]{:S(2)}) %collective-permute-start.58) | collective-permute-done | bytes 245792 | tf_op jit(solution)/shard_map/ppermute | solution.py:604
  116.2 4.0 %expand.29 = (bf16[48,2560]{1,0:T(8,128)(2,1)S(1)}, bf16[64,768]{1,0:T(8,128)(2,1)S(1)}, bf16[48,256]{1,0:T(8,128)(2,1)S(1)}, bf16[48,256]{1,0:T(8,128)(2,1)S(1)}, f32[48,128]{1,0:T(8,128)S(1)}) custom-call(bf16[48,2560]{1,0:T(8,128)(2,1)S(1)} %fusion.6.own.refs_4_, bf16[48,2560]{1,0:T(8,128)(2,1)S(1)} %collective-permute-done.59.peer.refs_11_, ...), custom_call_target="tpu_custom_call" | custom-call | tf_op jit(solution)/shard_map/expand/pallas_call | solution.py:362
  123.5 6.6 %collective-permute-done.61 = bf16[48,2560]{1,0:T(8,128)(2,1)S(1)} collective-permute-done((bf16[48,2560]{1,0:T(8,128)(2,1)S(1)}, bf16[48,2560]{1,0:T(8,128)(2,1)S(1)}, u32[]{:S(2)}, u32[]{:S(2)}) %collective-permute-start.61) | collective-permute-done | bytes 245792 | tf_op jit(solution)/shard_map/ppermute | solution.py:604
  131.8 4.0 %expand.30 = (bf16[48,2560]{1,0:T(8,128)(2,1)S(1)}, bf16[64,768]{1,0:T(8,128)(2,1)S(1)}, bf16[48,256]{1,0:T(8,128)(2,1)S(1)}, bf16[48,256]{1,0:T(8,128)(2,1)S(1)}, f32[48,128]{1,0:T(8,128)S(1)}) custom-call(bf16[48,2560]{1,0:T(8,128)(2,1)S(1)} %get-tuple-element.391.own.refs_5_, bf16[48,2560]{1,0:T(8,128)(2,1)S(1)} %collective-permute-done.62.peer.refs_12_, ...), custom_call_target="tpu_custom_call" | custom-call | tf_op jit(solution)/shard_map/expand/pallas_call | solution.py:362
  137.7 1.6 collective-permute-start.64
  139.3 6.6 %collective-permute-done.64 = bf16[48,2560]{1,0:T(8,128)(2,1)S(1)} collective-permute-done((bf16[48,2560]{1,0:T(8,128)(2,1)S(1)}, bf16[48,2560]{1,0:T(8,128)(2,1)S(1)}, u32[]{:S(2)}, u32[]{:S(2)}) %collective-permute-start.64) | collective-permute-done | bytes 245792 | tf_op jit(solution)/shard_map/ppermute | solution.py:604
  147.6 4.4 %expand.31 = (bf16[48,2560]{1,0:T(8,128)(2,1)S(1)}, bf16[64,768]{1,0:T(8,128)(2,1)S(1)}, bf16[48,256]{1,0:T(8,128)(2,1)}, bf16[48,256]{1,0:T(8,128)(2,1)}, f32[48,128]{1,0:T(8,128)S(1)}) custom-call(bf16[48,2560]{1,0:T(8,128)(2,1)S(1)} %fusion.7.own.refs_6_, bf16[48,2560]{1,0:T(8,128)(2,1)S(1)} %collective-permute-done.65.peer.refs_13_, ...), custom_call_target="tpu_custom_call" | custom-call | tf_op jit(solution)/shard_map/expand/pallas_call | solution.py:362
  155.2 6.9 %score.6 = (bf16[336,128]{1,0:T(8,128)(2,1)S(1)}, bf16[336,128]{1,0:T(8,128)(2,1)S(1)}, bf16[336,128]{1,0:T(8,128)(2,1)S(1)}, bf16[336,128]{1,0:T(8,128)(2,1)S(1)}, bf16[8,1280,512]{2,1,0:T(8,128)(2,1)S(1)}) custom-call(f32[48,128]{1,0:T(8,128)S(1)} %get-tuple-element.299.notes, bf16[8,1280,512]{2,1,0:T(8,128)(2,1)} %all-gather.2.cloned.1.call-done.up, ...), custom_call_target="tpu_custom_call" | custom-call | tf_op jit(solution)/shard_map/score/pallas_call | solution.py:455
  164.3 1.9 score.7.refs_8_
  172.9 1.7 collective-permute-done.76.refs_2_
  176.5 10.7 %all_to_all.9 = f32[8,8,128]{2,1,0:T(8,128)S(1)} all-to-all(f32[8,8,128]{2,1,0:T(8,128)S(1)} %bitcast.30), channel_id=1, replica_groups=mesh['dp'=8,'mp'=4] {'dp'}, dimensions={0} | all-to-all | bytes 65536 | tf_op jit(solution)/shard_map/all_to_all | solution.py:629
  (140 shorter events, 47.6 us)
Async XLA Ops:
  6.5 148.7 %all-gather.2.cloned.1.call-start = ((), (), s32[]{:S(2)}) async-start(), calls=%async_computation.1 | async-start | bytes 11796480 | tf_op jit(solution)/shard_map/all_gather | solution.py:561
  9.4 7.9 %collective-permute-start.37 = (bf16[32,3072]{1,0:T(8,128)(2,1)S(1)}, bf16[32,3072]{1,0:T(8,128)(2,1)S(1)}, u32[]{:S(2)}, u32[]{:S(2)}) collective-permute-start(bf16[32,3072]{1,0:T(8,128)(2,1)S(1)} %get-tuple-element.259), channel_id=1, source_target_pairs={{0,4},{4,0},{8,12},{12,8},{16,20},{20,16},{24,28},{28,24},{1,5},{5... | collective-permute-start | bytes 589832 | tf_op jit(solution)/shard_map/ppermute | solution.py:570
  17.4 9.2 %collective-permute-start.38 = (bf16[16,3072]{1,0:T(8,128)(2,1)S(1)}, bf16[16,3072]{1,0:T(8,128)(2,1)S(1)}, u32[]{:S(2)}, u32[]{:S(2)}) collective-permute-start(bf16[16,3072]{1,0:T(8,128)(2,1)S(1)} %get-tuple-element.282), channel_id=1, source_target_pairs={{0,8},{4,12},{8,0},{12,4},{16,24},{20,28},{24,16},{28,20},{1,9},{5... | collective-permute-start | bytes 294920 | tf_op jit(solution)/shard_map/ppermute | solution.py:573
  19.2 10.7 %collective-permute-start.39 = (bf16[16,3072]{1,0:T(8,128)(2,1)S(1)}, bf16[16,3072]{1,0:T(8,128)(2,1)S(1)}, u32[]{:S(2)}, u32[]{:S(2)}) collective-permute-start(bf16[16,3072]{1,0:T(8,128)(2,1)S(1)} %get-tuple-element.283), channel_id=1, source_target_pairs={{0,16},{4,20},{8,24},{12,28},{16,0},{20,4},{24,8},{28,12},{1,17},{... | collective-permute-start | bytes 294920 | tf_op jit(solution)/shard_map/ppermute | solution.py:573
  21.8 13.2 %collective-permute-start.40 = (bf16[16,3072]{1,0:T(8,128)(2,1)S(1)}, bf16[16,3072]{1,0:T(8,128)(2,1)S(1)}, u32[]{:S(2)}, u32[]{:S(2)}) collective-permute-start(bf16[16,3072]{1,0:T(8,128)(2,1)S(1)} %get-tuple-element.284), channel_id=1, source_target_pairs={{0,24},{4,28},{8,16},{12,20},{16,8},{20,12},{24,0},{28,4},{1,25},{... | collective-permute-start | bytes 294920 | tf_op jit(solution)/shard_map/ppermute | solution.py:573
  43.7 8.3 %collective-permute-start.43 = (bf16[48,2560]{1,0:T(8,128)(2,1)S(1)}, bf16[48,2560]{1,0:T(8,128)(2,1)S(1)}, u32[]{:S(2)}, u32[]{:S(2)}) collective-permute-start(bf16[48,2560]{1,0:T(8,128)(2,1)S(1)} %add_convert_fusion.17), channel_id=1, source_target_pairs={{0,2},{1,3},{2,0},{3,1},{4,6},{5,7},{6,4},{7,5},{8,10},{9,11},{10,... | collective-permute-start | bytes 737288 | tf_op jit(solution)/shard_map/ppermute | solution.py:604
  45.3 6.0 %collective-permute-start.46 = (f32[8,128]{1,0:T(8,128)S(1)}, f32[8,128]{1,0:T(8,128)S(1)}, u32[]{:S(2)}, u32[]{:S(2)}) collective-permute-start(f32[8,128]{1,0:T(8,128)S(1)} %get-tuple-element.362.scale.refs_4_), channel_id=1, source_target_pairs={{0,3},{1,2},{2,1},{3,0},{4,7},{5,6},{6,5},{7,4},{8,11},{9,10},{10,... | collective-permute-start | bytes 12296 | tf_op jit(solution)/shard_map/ppermute | solution.py:591
  45.4 6.7 %collective-permute-start.45 = (f32[8,128]{1,0:T(8,128)S(1)}, f32[8,128]{1,0:T(8,128)S(1)}, u32[]{:S(2)}, u32[]{:S(2)}) collective-permute-start(f32[8,128]{1,0:T(8,128)S(1)} %get-tuple-element.362.scale.refs_4_), channel_id=1, source_target_pairs={{0,2},{1,3},{2,0},{3,1},{4,6},{5,7},{6,4},{7,5},{8,10},{9,11},{10,... | collective-permute-start | bytes 12296 | tf_op jit(solution)/shard_map/ppermute | solution.py:591
  46.9 5.2 %collective-permute-start.44 = (f32[8,128]{1,0:T(8,128)S(1)}, f32[8,128]{1,0:T(8,128)S(1)}, u32[]{:S(2)}, u32[]{:S(2)}) collective-permute-start(f32[8,128]{1,0:T(8,128)S(1)} %get-tuple-element.362.scale.refs_4_), channel_id=1, source_target_pairs={{0,1},{1,0},{2,3},{3,2},{4,5},{5,4},{6,7},{7,6},{8,9},{9,8},{10,11... | collective-permute-start | bytes 12296 | tf_op jit(solution)/shard_map/ppermute | solution.py:591
  57.6 1.6 collective-permute-start.48
  59.3 8.2 %collective-permute-start.49 = (bf16[48,2560]{1,0:T(8,128)(2,1)S(1)}, bf16[48,2560]{1,0:T(8,128)(2,1)S(1)}, u32[]{:S(2)}, u32[]{:S(2)}) collective-permute-start(bf16[48,2560]{1,0:T(8,128)(2,1)S(1)} %add_convert_fusion.16), channel_id=1, source_target_pairs={{0,2},{1,3},{2,0},{3,1},{4,6},{5,7},{6,4},{7,5},{8,10},{9,11},{10,... | collective-permute-start | bytes 737288 | tf_op jit(solution)/shard_map/ppermute | solution.py:604
  73.2 1.6 collective-permute-start.51
  74.9 8.2 %collective-permute-start.52 = (bf16[48,2560]{1,0:T(8,128)(2,1)S(1)}, bf16[48,2560]{1,0:T(8,128)(2,1)S(1)}, u32[]{:S(2)}, u32[]{:S(2)}) collective-permute-start(bf16[48,2560]{1,0:T(8,128)(2,1)S(1)} %add_convert_fusion.15), channel_id=1, source_target_pairs={{0,2},{1,3},{2,0},{3,1},{4,6},{5,7},{6,4},{7,5},{8,10},{9,11},{10,... | collective-permute-start | bytes 737288 | tf_op jit(solution)/shard_map/ppermute | solution.py:604
  88.6 2.2 %collective-permute-start.54 = (bf16[48,2560]{1,0:T(8,128)(2,1)S(1)}, bf16[48,2560]{1,0:T(8,128)(2,1)S(1)}, u32[]{:S(2)}, u32[]{:S(2)}) collective-permute-start(bf16[48,2560]{1,0:T(8,128)(2,1)S(1)} %get-tuple-element.324), channel_id=1, source_target_pairs={{0,1},{1,0},{2,3},{3,2},{4,5},{5,4},{6,7},{7,6},{8,9},{9,8},{10,11... | collective-permute-start | bytes 737288 | tf_op jit(solution)/shard_map/ppermute | solution.py:601
  90.8 8.2 %collective-permute-start.55 = (bf16[48,2560]{1,0:T(8,128)(2,1)S(1)}, bf16[48,2560]{1,0:T(8,128)(2,1)S(1)}, u32[]{:S(2)}, u32[]{:S(2)}) collective-permute-start(bf16[48,2560]{1,0:T(8,128)(2,1)S(1)} %add_convert_fusion.14), channel_id=1, source_target_pairs={{0,2},{1,3},{2,0},{3,1},{4,6},{5,7},{6,4},{7,5},{8,10},{9,11},{10,... | collective-permute-start | bytes 737288 | tf_op jit(solution)/shard_map/ppermute | solution.py:604
  104.7 1.7 collective-permute-start.57
  106.4 8.2 %collective-permute-start.58 = (bf16[48,2560]{1,0:T(8,128)(2,1)S(1)}, bf16[48,2560]{1,0:T(8,128)(2,1)S(1)}, u32[]{:S(2)}, u32[]{:S(2)}) collective-permute-start(bf16[48,2560]{1,0:T(8,128)(2,1)S(1)} %add_convert_fusion.13), channel_id=1, source_target_pairs={{0,2},{1,3},{2,0},{3,1},{4,6},{5,7},{6,4},{7,5},{8,10},{9,11},{10,... | collective-permute-start | bytes 737288 | tf_op jit(solution)/shard_map/ppermute | solution.py:604
  120.2 1.6 collective-permute-start.60
  121.9 8.2 %collective-permute-start.61 = (bf16[48,2560]{1,0:T(8,128)(2,1)S(1)}, bf16[48,2560]{1,0:T(8,128)(2,1)S(1)}, u32[]{:S(2)}, u32[]{:S(2)}) collective-permute-start(bf16[48,2560]{1,0:T(8,128)(2,1)S(1)} %add_convert_fusion.12), channel_id=1, source_target_pairs={{0,2},{1,3},{2,0},{3,1},{4,6},{5,7},{6,4},{7,5},{8,10},{9,11},{10,... | collective-permute-start | bytes 737288 | tf_op jit(solution)/shard_map/ppermute | solution.py:604
  135.9 1.8 collective-permute-start.63
  137.7 8.2 %collective-permute-start.64 = (bf16[48,2560]{1,0:T(8,128)(2,1)S(1)}, bf16[48,2560]{1,0:T(8,128)(2,1)S(1)}, u32[]{:S(2)}, u32[]{:S(2)}) collective-permute-start(bf16[48,2560]{1,0:T(8,128)(2,1)S(1)} %add_convert_fusion.11), channel_id=1, source_target_pairs={{0,2},{1,3},{2,0},{3,1},{4,6},{5,7},{6,4},{7,5},{8,10},{9,11},{10,... | collective-permute-start | bytes 737288 | tf_op jit(solution)/shard_map/ppermute | solution.py:604
  153.6 8.5 %collective-permute-start.67 = (bf16[48,2560]{1,0:T(8,128)(2,1)S(1)}, bf16[48,2560]{1,0:T(8,128)(2,1)S(1)}, u32[]{:S(2)}, u32[]{:S(2)}) collective-permute-start(bf16[48,2560]{1,0:T(8,128)(2,1)S(1)} %add_convert_fusion.10), channel_id=1, source_target_pairs={{0,2},{1,3},{2,0},{3,1},{4,6},{5,7},{6,4},{7,5},{8,10},{9,11},{10,... | collective-permute-start | bytes 737288 | tf_op jit(solution)/shard_map/ppermute | solution.py:604
  162.3 2.0 %collective-permute-start.68 = (bf16[48,2560]{1,0:T(8,128)(2,1)S(1)}, bf16[48,2560]{1,0:T(8,128)(2,1)S(1)}, u32[]{:S(2)}, u32[]{:S(2)}) collective-permute-start(bf16[48,2560]{1,0:T(8,128)(2,1)S(1)} %add_convert_fusion.9.refs_0_.own_row), channel_id=1, source_target_pairs={{0,1},{1,0},{2,3},{3,2},{4,5},{5,4},{6,7},{7,6},{8,9},{9,8},{10,11... | collective-permute-start | bytes 737288 | tf_op jit(solution)/shard_map/ppermute | solution.py:613
  162.3 6.3 %collective-permute-start.72 = (bf16[336,128]{1,0:T(8,128)(2,1)S(1)}, bf16[336,128]{1,0:T(8,128)(2,1)S(1)}, u32[]{:S(2)}, u32[]{:S(2)}) collective-permute-start(bf16[336,128]{1,0:T(8,128)(2,1)S(1)} %get-tuple-element.359), channel_id=1, source_target_pairs={{0,1},{1,0},{2,3},{3,2},{4,5},{5,4},{6,7},{7,6},{8,9},{9,8},{10,11... | collective-permute-start | bytes 258056 | tf_op jit(solution)/shard_map/ppermute | solution.py:591
  162.8 5.8 %collective-permute-start.73 = (bf16[336,128]{1,0:T(8,128)(2,1)S(1)}, bf16[336,128]{1,0:T(8,128)(2,1)S(1)}, u32[]{:S(2)}, u32[]{:S(2)}) collective-permute-start(bf16[336,128]{1,0:T(8,128)(2,1)S(1)} %get-tuple-element.360), channel_id=1, source_target_pairs={{0,2},{1,3},{2,0},{3,1},{4,6},{5,7},{6,4},{7,5},{8,10},{9,11},{10,... | collective-permute-start | bytes 258056 | tf_op jit(solution)/shard_map/ppermute | solution.py:591
  164.0 4.8 %collective-permute-start.74 = (bf16[336,128]{1,0:T(8,128)(2,1)S(1)}, bf16[336,128]{1,0:T(8,128)(2,1)S(1)}, u32[]{:S(2)}, u32[]{:S(2)}) collective-permute-start(bf16[336,128]{1,0:T(8,128)(2,1)S(1)} %get-tuple-element.361), channel_id=1, source_target_pairs={{0,3},{1,2},{2,1},{3,0},{4,7},{5,6},{6,5},{7,4},{8,11},{9,10},{10,... | collective-permute-start | bytes 258056 | tf_op jit(solution)/shard_map/ppermute | solution.py:591
  166.2 5.5 %collective-permute-start.71 = (bf16[48,512]{1,0:T(8,128)(2,1)S(1)}, bf16[48,512]{1,0:T(8,128)(2,1)S(1)}, u32[]{:S(2)}, u32[]{:S(2)}) collective-permute-start(bf16[48,512]{1,0:T(8,128)(2,1)S(1)} %score.7.refs_8_), channel_id=1, source_target_pairs={{0,3},{1,2},{2,1},{3,0},{4,7},{5,6},{6,5},{7,4},{8,11},{9,10},{10,... | collective-permute-start | bytes 147464 | tf_op jit(solution)/shard_map/ppermute | solution.py:591
  167.7 4.5 %collective-permute-start.70 = (bf16[48,512]{1,0:T(8,128)(2,1)S(1)}, bf16[48,512]{1,0:T(8,128)(2,1)S(1)}, u32[]{:S(2)}, u32[]{:S(2)}) collective-permute-start(bf16[48,512]{1,0:T(8,128)(2,1)S(1)} %score.7.refs_8_), channel_id=1, source_target_pairs={{0,2},{1,3},{2,0},{3,1},{4,6},{5,7},{6,4},{7,5},{8,10},{9,11},{10,... | collective-permute-start | bytes 147464 | tf_op jit(solution)/shard_map/ppermute | solution.py:591
  168.6 3.6 %collective-permute-start.69 = (bf16[48,512]{1,0:T(8,128)(2,1)S(1)}, bf16[48,512]{1,0:T(8,128)(2,1)S(1)}, u32[]{:S(2)}, u32[]{:S(2)}) collective-permute-start(bf16[48,512]{1,0:T(8,128)(2,1)S(1)} %score.7.refs_8_), channel_id=1, source_target_pairs={{0,1},{1,0},{2,3},{3,2},{4,5},{5,4},{6,7},{7,6},{8,9},{9,8},{10,11... | collective-permute-start | bytes 147464 | tf_op jit(solution)/shard_map/ppermute | solution.py:591
  169.6 3.3 %collective-permute-start.77 = (f32[48,128]{1,0:T(8,128)S(1)}, f32[48,128]{1,0:T(8,128)S(1)}, u32[]{:S(2)}, u32[]{:S(2)}) collective-permute-start(f32[48,128]{1,0:T(8,128)S(1)} %finish.3.refs_0_), channel_id=1, source_target_pairs={{0,3},{1,2},{2,1},{3,0},{4,7},{5,6},{6,5},{7,4},{8,11},{9,10},{10,... | collective-permute-start | bytes 73736 | tf_op jit(solution)/shard_map/ppermute | solution.py:591
  170.8 3.8 %collective-permute-start.76 = (f32[48,128]{1,0:T(8,128)S(1)}, f32[48,128]{1,0:T(8,128)S(1)}, u32[]{:S(2)}, u32[]{:S(2)}) collective-permute-start(f32[48,128]{1,0:T(8,128)S(1)} %finish.3.refs_0_), channel_id=1, source_target_pairs={{0,2},{1,3},{2,0},{3,1},{4,6},{5,7},{6,4},{7,5},{8,10},{9,11},{10,... | collective-permute-start | bytes 73736 | tf_op jit(solution)/shard_map/ppermute | solution.py:591
  171.7 2.9 %collective-permute-start.75 = (f32[48,128]{1,0:T(8,128)S(1)}, f32[48,128]{1,0:T(8,128)S(1)}, u32[]{:S(2)}, u32[]{:S(2)}) collective-permute-start(f32[48,128]{1,0:T(8,128)S(1)} %finish.3.refs_0_), channel_id=1, source_target_pairs={{0,1},{1,0},{2,3},{3,2},{4,5},{5,4},{6,7},{7,6},{8,9},{9,8},{10,11... | collective-permute-start | bytes 73736 | tf_op jit(solution)/shard_map/ppermute | solution.py:591
  (27 other events, 139.6 us)
Sparse Core Ops, SparseCore 0:
  8.9 115.5 all-gather.1

commit v7 on v5

--- a/solution.py
+++ b/solution.py
@@ -16,7 +16,7 @@
 GROUP = HEADS // KVH
 CHUNK = 512
 COLUMNS = 256
-ROWS = 64
+ROWS = 16
 MASKED = -1e30
 EXPONENT = HD ** (-0.5) * math.log2(math.e)
 VMEM = pltpu.VMEM

time: 195 us -> 194 us (level)
  no operation moved by 1% of the time
where the time goes in v7:
time: 194 us; the launch traced here: 191 us
  Pallas kernels  72.7 us (37%)
  waiting for transfers between devices  48.2 us (25%)
  starting transfers between devices  37.8 us (19%)
  between operations  15.8 us (8%)
  blocking collectives  12.3 us (6%)
  other arithmetic  1.97 us (1%)
    ppermute x8, waiting for transfers between devices, run(): lax.ppermute(sent, 'mp', pairs(mp, k))  38.8 us
    pallas_call x8, Pallas kernels, expand(): pl.pallas_call(functools.partial(step_kernel, step), out_shape=(struct((s...  32.1 us
    ppermute x8, starting transfers between devices, run(): lax.ppermute(sent, 'mp', pairs(mp, k))  13.7 us
    ppermute x7, starting transfers between devices, shards(): lax.ppermute(blocks[k], 'dp', pairs(groups, k))  12.5 us
    all_to_all x1, blocking collectives, shards(): table = lax.all_to_all(table, 'dp', split_axis=0, concat_axis=0, tiled=True)  12.3 us
    pallas_call x8, Pallas kernels, project_own(): pl.pallas_call(project_kernel, out_shape=struct((rows, w_out.shape[1] //...  10.2 us
    pallas_call x8, Pallas kernels, begin(): pl.pallas_call(begin_kernel, out_shape=struct((slots, w_query.shape[1] +...  9.95 us
    pallas_call x2, Pallas kernels, score(): pl.pallas_call(functools.partial(score_kernel, steps, load, mp), out_shap...  8.84 us
  transfers between devices with their start and end apart: 45, of which 19 were waited for; matrix products, arithmetic and copies ran while one was open for 1% of the time, Pallas kernels for 38%

profile of v7, /device:TPU:0, one launch (start us, length us, event | category | flops | bytes accessed | tf_op | source)
XLA Modules:
  0.0 190.8 jit_solution(17948518040822122971)
XLA Ops:
  9.4 3.0 %collective-permute-start.37 = (bf16[8,3072]{1,0:T(8,128)(2,1)S(1)}, bf16[8,3072]{1,0:T(8,128)(2,1)S(1)}, u32[]{:S(2)}, u32[]{:S(2)}) collective-permute-start(bf16[8,3072]{1,0:T(8,128)(2,1)S(1)} %get-tuple-element.270), channel_id=1, source_target_pairs={{0,4},{4,0},{8,12},{12,8},{16,20},{20,16},{24,28},{28,24},{1,5},{5... | collective-permute-start | bytes 147464 | tf_op jit(solution)/shard_map/ppermute | solution.py:540
  14.1 3.0 %collective-permute-start.40 = (bf16[8,3072]{1,0:T(8,128)(2,1)S(1)}, bf16[8,3072]{1,0:T(8,128)(2,1)S(1)}, u32[]{:S(2)}, u32[]{:S(2)}) collective-permute-start(bf16[8,3072]{1,0:T(8,128)(2,1)S(1)} %get-tuple-element.273), channel_id=1, source_target_pairs={{0,16},{4,20},{8,24},{12,28},{16,0},{20,4},{24,8},{28,12},{1,17},{... | collective-permute-start | bytes 147464 | tf_op jit(solution)/shard_map/ppermute | solution.py:540
  18.3 3.6 %collective-permute-start.42 = (bf16[8,3072]{1,0:T(8,128)(2,1)S(1)}, bf16[8,3072]{1,0:T(8,128)(2,1)S(1)}, u32[]{:S(2)}, u32[]{:S(2)}) collective-permute-start(bf16[8,3072]{1,0:T(8,128)(2,1)S(1)} %get-tuple-element.275), channel_id=1, source_target_pairs={{0,24},{4,28},{8,16},{12,20},{16,8},{20,12},{24,0},{28,4},{1,25},{... | collective-permute-start | bytes 147464 | tf_op jit(solution)/shard_map/ppermute | solution.py:540
  22.0 7.7 %load.3 = (bf16[5120,768]{1,0:T(8,128)(2,1)S(1)}, bf16[5120,256]{1,0:T(8,128)(2,1)S(1)}, bf16[5120,256]{1,0:T(8,128)(2,1)S(1)}, bf16[2048,256]{1,0:T(8,128)(2,1)...) custom-call(bf16[5120,768]{1,0:T(8,128)(2,1)} %refs_0_, bf16[5120,256]{1,0:T(8,128)(2,1)} %refs_1_, ...), custom_call_target="tpu_custom_call" | custom-call | bytes 25165824 | tf_op jit(solution)/shard_map/load/pallas_call | solution.py:223
  32.3 4.7 %expand.24 = (bf16[48,2560]{1,0:T(8,128)(2,1)S(1)}, bf16[48,768]{1,0:T(8,128)(2,1)S(1)}, bf16[48,256]{1,0:T(8,128)(2,1)S(1)}, bf16[48,256]{1,0:T(8,128)(2,1)S(1)}, f32[48,128]{1,0:T(8,128)}) custom-call(bf16[48,2560]{1,0:T(8,128)(2,1)S(1)} %get-tuple-element.298.own, bf16[48,2560]{1,0:T(8,128)(2,1)S(1)} %collective-permute-done.44.peer, ...), custom_call_target="tpu_custom_call" | custom-call | tf_op jit(solution)/shard_map/expand/pallas_call | solution.py:334
  38.6 1.7 collective-permute-start.46
  40.3 1.6 collective-permute-start.48
  42.2 4.0 %collective-permute-done.49.refs_7_ = f32[8,128]{1,0:T(8,128)S(1)} collective-permute-done((f32[8,128]{1,0:T(8,128)S(1)}, f32[8,128]{1,0:T(8,128)S(1)}, u32[]{:S(2)}, u32[]{:S(2)}) %collective-permute-start.49) | collective-permute-done | bytes 4128 | tf_op jit(solution)/shard_map/ppermute | solution.py:558
  48.6 3.8 %expand.25 = (bf16[48,2560]{1,0:T(8,128)(2,1)S(1)}, bf16[48,768]{1,0:T(8,128)(2,1)S(1)}, bf16[48,256]{1,0:T(8,128)(2,1)S(1)}, bf16[48,256]{1,0:T(8,128)(2,1)S(1)}, f32[48,128]{1,0:T(8,128)S(1)}) custom-call(bf16[48,2560]{1,0:T(8,128)(2,1)S(1)} %fusion.4.own.refs_0_, bf16[48,2560]{1,0:T(8,128)(2,1)S(1)} %collective-permute-done.50.peer.refs_7_, ...), custom_call_target="tpu_custom_call" | custom-call | tf_op jit(solution)/shard_map/expand/pallas_call | solution.py:334
  54.1 1.7 collective-permute-start.52
  55.8 6.5 %collective-permute-done.52 = bf16[48,2560]{1,0:T(8,128)(2,1)S(1)} collective-permute-done((bf16[48,2560]{1,0:T(8,128)(2,1)S(1)}, bf16[48,2560]{1,0:T(8,128)(2,1)S(1)}, u32[]{:S(2)}, u32[]{:S(2)}) %collective-permute-start.52) | collective-permute-done | bytes 245792 | tf_op jit(solution)/shard_map/ppermute | solution.py:571
  64.1 3.8 %expand.26 = (bf16[48,2560]{1,0:T(8,128)(2,1)S(1)}, bf16[48,768]{1,0:T(8,128)(2,1)S(1)}, bf16[48,256]{1,0:T(8,128)(2,1)S(1)}, bf16[48,256]{1,0:T(8,128)(2,1)S(1)}, f32[48,128]{1,0:T(8,128)S(1)}) custom-call(bf16[48,2560]{1,0:T(8,128)(2,1)S(1)} %get-tuple-element.397.own.refs_1_, bf16[48,2560]{1,0:T(8,128)(2,1)S(1)} %collective-permute-done.53.peer.refs_8_, ...), custom_call_target="tpu_custom_call" | custom-call | tf_op jit(solution)/shard_map/expand/pallas_call | solution.py:334
  69.5 1.7 collective-permute-start.55
  71.3 6.5 %collective-permute-done.55 = bf16[48,2560]{1,0:T(8,128)(2,1)S(1)} collective-permute-done((bf16[48,2560]{1,0:T(8,128)(2,1)S(1)}, bf16[48,2560]{1,0:T(8,128)(2,1)S(1)}, u32[]{:S(2)}, u32[]{:S(2)}) %collective-permute-start.55) | collective-permute-done | bytes 245792 | tf_op jit(solution)/shard_map/ppermute | solution.py:571
  79.4 3.8 %expand.27 = (bf16[48,2560]{1,0:T(8,128)(2,1)S(1)}, bf16[48,768]{1,0:T(8,128)(2,1)S(1)}, bf16[48,256]{1,0:T(8,128)(2,1)S(1)}, bf16[48,256]{1,0:T(8,128)(2,1)S(1)}, f32[48,128]{1,0:T(8,128)S(1)}) custom-call(bf16[48,2560]{1,0:T(8,128)(2,1)S(1)} %fusion.5.own.refs_2_, bf16[48,2560]{1,0:T(8,128)(2,1)S(1)} %collective-permute-done.56.peer.refs_9_, ...), custom_call_target="tpu_custom_call" | custom-call | tf_op jit(solution)/shard_map/expand/pallas_call | solution.py:334
  85.1 1.7 collective-permute-start.58
  86.8 6.5 %collective-permute-done.58 = bf16[48,2560]{1,0:T(8,128)(2,1)S(1)} collective-permute-done((bf16[48,2560]{1,0:T(8,128)(2,1)S(1)}, bf16[48,2560]{1,0:T(8,128)(2,1)S(1)}, u32[]{:S(2)}, u32[]{:S(2)}) %collective-permute-start.58) | collective-permute-done | bytes 245792 | tf_op jit(solution)/shard_map/ppermute | solution.py:571
  95.0 3.8 %expand.28 = (bf16[48,2560]{1,0:T(8,128)(2,1)S(1)}, bf16[48,768]{1,0:T(8,128)(2,1)S(1)}, bf16[48,256]{1,0:T(8,128)(2,1)S(1)}, bf16[48,256]{1,0:T(8,128)(2,1)S(1)}, f32[48,128]{1,0:T(8,128)S(1)}) custom-call(bf16[48,2560]{1,0:T(8,128)(2,1)S(1)} %get-tuple-element.395.own.refs_3_, bf16[48,2560]{1,0:T(8,128)(2,1)S(1)} %collective-permute-done.59.peer.refs_10_, ...), custom_call_target="tpu_custom_call" | custom-call | tf_op jit(solution)/shard_map/expand/pallas_call | solution.py:334
  100.5 1.7 collective-permute-start.61
  102.2 6.5 %collective-permute-done.61 = bf16[48,2560]{1,0:T(8,128)(2,1)S(1)} collective-permute-done((bf16[48,2560]{1,0:T(8,128)(2,1)S(1)}, bf16[48,2560]{1,0:T(8,128)(2,1)S(1)}, u32[]{:S(2)}, u32[]{:S(2)}) %collective-permute-start.61) | collective-permute-done | bytes 245792 | tf_op jit(solution)/shard_map/ppermute | solution.py:571
  110.4 3.9 %expand.29 = (bf16[48,2560]{1,0:T(8,128)(2,1)S(1)}, bf16[48,768]{1,0:T(8,128)(2,1)S(1)}, bf16[48,256]{1,0:T(8,128)(2,1)S(1)}, bf16[48,256]{1,0:T(8,128)(2,1)S(1)}, f32[48,128]{1,0:T(8,128)S(1)}) custom-call(bf16[48,2560]{1,0:T(8,128)(2,1)S(1)} %fusion.6.own.refs_4_, bf16[48,2560]{1,0:T(8,128)(2,1)S(1)} %collective-permute-done.62.peer.refs_11_, ...), custom_call_target="tpu_custom_call" | custom-call | tf_op jit(solution)/shard_map/expand/pallas_call | solution.py:334
  115.9 1.7 collective-permute-start.64
  117.7 6.5 %collective-permute-done.64 = bf16[48,2560]{1,0:T(8,128)(2,1)S(1)} collective-permute-done((bf16[48,2560]{1,0:T(8,128)(2,1)S(1)}, bf16[48,2560]{1,0:T(8,128)(2,1)S(1)}, u32[]{:S(2)}, u32[]{:S(2)}) %collective-permute-start.64) | collective-permute-done | bytes 245792 | tf_op jit(solution)/shard_map/ppermute | solution.py:571
  125.9 3.9 %expand.30 = (bf16[48,2560]{1,0:T(8,128)(2,1)S(1)}, bf16[48,768]{1,0:T(8,128)(2,1)S(1)}, bf16[48,256]{1,0:T(8,128)(2,1)S(1)}, bf16[48,256]{1,0:T(8,128)(2,1)S(1)}, f32[48,128]{1,0:T(8,128)S(1)}) custom-call(bf16[48,2560]{1,0:T(8,128)(2,1)S(1)} %get-tuple-element.393.own.refs_5_, bf16[48,2560]{1,0:T(8,128)(2,1)S(1)} %collective-permute-done.65.peer.refs_12_, ...), custom_call_target="tpu_custom_call" | custom-call | tf_op jit(solution)/shard_map/expand/pallas_call | solution.py:334
  131.7 1.7 collective-permute-start.67
  133.4 6.5 %collective-permute-done.67 = bf16[48,2560]{1,0:T(8,128)(2,1)S(1)} collective-permute-done((bf16[48,2560]{1,0:T(8,128)(2,1)S(1)}, bf16[48,2560]{1,0:T(8,128)(2,1)S(1)}, u32[]{:S(2)}, u32[]{:S(2)}) %collective-permute-start.67) | collective-permute-done | bytes 245792 | tf_op jit(solution)/shard_map/ppermute | solution.py:571
  141.5 4.3 %expand.31 = (bf16[48,2560]{1,0:T(8,128)(2,1)S(1)}, bf16[48,768]{1,0:T(8,128)(2,1)S(1)}, bf16[48,256]{1,0:T(8,128)(2,1)}, bf16[48,256]{1,0:T(8,128)(2,1)}, f32[48,128]{1,0:T(8,128)S(1)}) custom-call(bf16[48,2560]{1,0:T(8,128)(2,1)S(1)} %fusion.7.own.refs_6_, bf16[48,2560]{1,0:T(8,128)(2,1)S(1)} %collective-permute-done.68.peer.refs_13_, ...), custom_call_target="tpu_custom_call" | custom-call | tf_op jit(solution)/shard_map/expand/pallas_call | solution.py:334
  147.5 1.7 collective-permute-start.70
  149.2 6.9 %score.6 = (bf16[336,128]{1,0:T(8,128)(2,1)S(1)}, bf16[336,128]{1,0:T(8,128)(2,1)S(1)}, bf16[336,128]{1,0:T(8,128)(2,1)S(1)}, bf16[336,128]{1,0:T(8,128)(2,1)S(1)}, bf16[8,1280,512]{2,1,0:T(8,128)(2,1)S(1)}) custom-call(f32[48,128]{1,0:T(8,128)S(1)} %get-tuple-element.297.notes, bf16[8,1280,512]{2,1,0:T(8,128)(2,1)} %all-gather.2.cloned.1.call-done.up, ...), custom_call_target="tpu_custom_call" | custom-call | tf_op jit(solution)/shard_map/score/pallas_call | solution.py:427
  158.2 1.9 %score.7.refs_8_ = bf16[48,512]{1,0:T(8,128)(2,1)S(1)} custom-call(f32[48,128]{1,0:T(8,128)S(1)} %get-tuple-element.297.notes, bf16[8,1280,512]{2,1,0:T(8,128)(2,1)S(1)} %get-tuple-element.340.up, bf16[48,2560]{1,0:T(8,128)(2,1)S(1)} %add_convert_fusion.9.refs_0_.own_row, bf16[48,2560]{1,0:T(8,128)(2,1)S(1)} %collective-permute-done.71.refs_1_.peer_row), custom_call_target="tpu_custom_call" | custom-call | tf_op jit(solution)/shard_map/score/pallas_call | solution.py:427
  167.0 1.7 collective-permute-done.79.refs_2_
  170.5 12.3 %all_to_all.9 = f32[8,8,128]{2,1,0:T(8,128)S(1)} all-to-all(f32[8,8,128]{2,1,0:T(8,128)S(1)} %bitcast.30), channel_id=1, replica_groups=mesh['dp'=8,'mp'=4] {'dp'}, dimensions={0} | all-to-all | bytes 65536 | tf_op jit(solution)/shard_map/all_to_all | solution.py:596
  (144 shorter events, 44.5 us)
Async XLA Ops:
  6.5 142.6 %all-gather.2.cloned.1.call-start = ((), (), s32[]{:S(2)}) async-start(), calls=%async_computation.1 | async-start | bytes 11796480 | tf_op jit(solution)/shard_map/all_gather | solution.py:533
  9.4 8.9 %collective-permute-start.37 = (bf16[8,3072]{1,0:T(8,128)(2,1)S(1)}, bf16[8,3072]{1,0:T(8,128)(2,1)S(1)}, u32[]{:S(2)}, u32[]{:S(2)}) collective-permute-start(bf16[8,3072]{1,0:T(8,128)(2,1)S(1)} %get-tuple-element.270), channel_id=1, source_target_pairs={{0,4},{4,0},{8,12},{12,8},{16,20},{20,16},{24,28},{28,24},{1,5},{5... | collective-permute-start | bytes 147464 | tf_op jit(solution)/shard_map/ppermute | solution.py:540
  12.5 9.5 %collective-permute-start.38 = (bf16[8,3072]{1,0:T(8,128)(2,1)S(1)}, bf16[8,3072]{1,0:T(8,128)(2,1)S(1)}, u32[]{:S(2)}, u32[]{:S(2)}) collective-permute-start(bf16[8,3072]{1,0:T(8,128)(2,1)S(1)} %get-tuple-element.271), channel_id=1, source_target_pairs={{0,8},{4,12},{8,0},{12,4},{16,24},{20,28},{24,16},{28,20},{1,9},{5... | collective-permute-start | bytes 147464 | tf_op jit(solution)/shard_map/ppermute | solution.py:540
  14.1 15.6 %collective-permute-start.39 = (bf16[8,3072]{1,0:T(8,128)(2,1)S(1)}, bf16[8,3072]{1,0:T(8,128)(2,1)S(1)}, u32[]{:S(2)}, u32[]{:S(2)}) collective-permute-start(bf16[8,3072]{1,0:T(8,128)(2,1)S(1)} %get-tuple-element.272), channel_id=1, source_target_pairs={{0,12},{4,8},{8,4},{12,0},{16,28},{20,24},{24,20},{28,16},{1,13},{... | collective-permute-start | bytes 147464 | tf_op jit(solution)/shard_map/ppermute | solution.py:540
  14.1 15.6 %collective-permute-start.40 = (bf16[8,3072]{1,0:T(8,128)(2,1)S(1)}, bf16[8,3072]{1,0:T(8,128)(2,1)S(1)}, u32[]{:S(2)}, u32[]{:S(2)}) collective-permute-start(bf16[8,3072]{1,0:T(8,128)(2,1)S(1)} %get-tuple-element.273), channel_id=1, source_target_pairs={{0,16},{4,20},{8,24},{12,28},{16,0},{20,4},{24,8},{28,12},{1,17},{... | collective-permute-start | bytes 147464 | tf_op jit(solution)/shard_map/ppermute | solution.py:540
  17.0 12.7 %collective-permute-start.41 = (bf16[8,3072]{1,0:T(8,128)(2,1)S(1)}, bf16[8,3072]{1,0:T(8,128)(2,1)S(1)}, u32[]{:S(2)}, u32[]{:S(2)}) collective-permute-start(bf16[8,3072]{1,0:T(8,128)(2,1)S(1)} %get-tuple-element.274), channel_id=1, source_target_pairs={{0,20},{4,16},{8,28},{12,24},{16,4},{20,0},{24,12},{28,8},{1,21},{... | collective-permute-start | bytes 147464 | tf_op jit(solution)/shard_map/ppermute | solution.py:540
  18.3 11.4 %collective-permute-start.42 = (bf16[8,3072]{1,0:T(8,128)(2,1)S(1)}, bf16[8,3072]{1,0:T(8,128)(2,1)S(1)}, u32[]{:S(2)}, u32[]{:S(2)}) collective-permute-start(bf16[8,3072]{1,0:T(8,128)(2,1)S(1)} %get-tuple-element.275), channel_id=1, source_target_pairs={{0,24},{4,28},{8,16},{12,20},{16,8},{20,12},{24,0},{28,4},{1,25},{... | collective-permute-start | bytes 147464 | tf_op jit(solution)/shard_map/ppermute | solution.py:540
  21.9 7.8 %collective-permute-start.43 = (bf16[8,3072]{1,0:T(8,128)(2,1)S(1)}, bf16[8,3072]{1,0:T(8,128)(2,1)S(1)}, u32[]{:S(2)}, u32[]{:S(2)}) collective-permute-start(bf16[8,3072]{1,0:T(8,128)(2,1)S(1)} %get-tuple-element.276), channel_id=1, source_target_pairs={{0,28},{4,24},{8,20},{12,16},{16,12},{20,8},{24,4},{28,0},{1,29},{... | collective-permute-start | bytes 147464 | tf_op jit(solution)/shard_map/ppermute | solution.py:540
  38.6 8.4 %collective-permute-start.46 = (bf16[48,2560]{1,0:T(8,128)(2,1)S(1)}, bf16[48,2560]{1,0:T(8,128)(2,1)S(1)}, u32[]{:S(2)}, u32[]{:S(2)}) collective-permute-start(bf16[48,2560]{1,0:T(8,128)(2,1)S(1)} %add_convert_fusion.17), channel_id=1, source_target_pairs={{0,2},{1,3},{2,0},{3,1},{4,6},{5,7},{6,4},{7,5},{8,10},{9,11},{10,... | collective-permute-start | bytes 737288 | tf_op jit(solution)/shard_map/ppermute | solution.py:571
  40.3 5.9 %collective-permute-start.49 = (f32[8,128]{1,0:T(8,128)S(1)}, f32[8,128]{1,0:T(8,128)S(1)}, u32[]{:S(2)}, u32[]{:S(2)}) collective-permute-start(f32[8,128]{1,0:T(8,128)S(1)} %get-tuple-element.360.scale.refs_4_), channel_id=1, source_target_pairs={{0,3},{1,2},{2,1},{3,0},{4,7},{5,6},{6,5},{7,4},{8,11},{9,10},{10,... | collective-permute-start | bytes 12296 | tf_op jit(solution)/shard_map/ppermute | solution.py:558
  40.3 6.6 %collective-permute-start.48 = (f32[8,128]{1,0:T(8,128)S(1)}, f32[8,128]{1,0:T(8,128)S(1)}, u32[]{:S(2)}, u32[]{:S(2)}) collective-permute-start(f32[8,128]{1,0:T(8,128)S(1)} %get-tuple-element.360.scale.refs_4_), channel_id=1, source_target_pairs={{0,2},{1,3},{2,0},{3,1},{4,6},{5,7},{6,4},{7,5},{8,10},{9,11},{10,... | collective-permute-start | bytes 12296 | tf_op jit(solution)/shard_map/ppermute | solution.py:558
  41.9 5.0 %collective-permute-start.47 = (f32[8,128]{1,0:T(8,128)S(1)}, f32[8,128]{1,0:T(8,128)S(1)}, u32[]{:S(2)}, u32[]{:S(2)}) collective-permute-start(f32[8,128]{1,0:T(8,128)S(1)} %get-tuple-element.360.scale.refs_4_), channel_id=1, source_target_pairs={{0,1},{1,0},{2,3},{3,2},{4,5},{5,4},{6,7},{7,6},{8,9},{9,8},{10,11... | collective-permute-start | bytes 12296 | tf_op jit(solution)/shard_map/ppermute | solution.py:558
  54.1 8.2 %collective-permute-start.52 = (bf16[48,2560]{1,0:T(8,128)(2,1)S(1)}, bf16[48,2560]{1,0:T(8,128)(2,1)S(1)}, u32[]{:S(2)}, u32[]{:S(2)}) collective-permute-start(bf16[48,2560]{1,0:T(8,128)(2,1)S(1)} %add_convert_fusion.16), channel_id=1, source_target_pairs={{0,2},{1,3},{2,0},{3,1},{4,6},{5,7},{6,4},{7,5},{8,10},{9,11},{10,... | collective-permute-start | bytes 737288 | tf_op jit(solution)/shard_map/ppermute | solution.py:571
  69.5 8.2 %collective-permute-start.55 = (bf16[48,2560]{1,0:T(8,128)(2,1)S(1)}, bf16[48,2560]{1,0:T(8,128)(2,1)S(1)}, u32[]{:S(2)}, u32[]{:S(2)}) collective-permute-start(bf16[48,2560]{1,0:T(8,128)(2,1)S(1)} %add_convert_fusion.15), channel_id=1, source_target_pairs={{0,2},{1,3},{2,0},{3,1},{4,6},{5,7},{6,4},{7,5},{8,10},{9,11},{10,... | collective-permute-start | bytes 737288 | tf_op jit(solution)/shard_map/ppermute | solution.py:571
  83.2 1.8 collective-permute-start.57
  85.1 8.2 %collective-permute-start.58 = (bf16[48,2560]{1,0:T(8,128)(2,1)S(1)}, bf16[48,2560]{1,0:T(8,128)(2,1)S(1)}, u32[]{:S(2)}, u32[]{:S(2)}) collective-permute-start(bf16[48,2560]{1,0:T(8,128)(2,1)S(1)} %add_convert_fusion.14), channel_id=1, source_target_pairs={{0,2},{1,3},{2,0},{3,1},{4,6},{5,7},{6,4},{7,5},{8,10},{9,11},{10,... | collective-permute-start | bytes 737288 | tf_op jit(solution)/shard_map/ppermute | solution.py:571
  100.5 8.2 %collective-permute-start.61 = (bf16[48,2560]{1,0:T(8,128)(2,1)S(1)}, bf16[48,2560]{1,0:T(8,128)(2,1)S(1)}, u32[]{:S(2)}, u32[]{:S(2)}) collective-permute-start(bf16[48,2560]{1,0:T(8,128)(2,1)S(1)} %add_convert_fusion.13), channel_id=1, source_target_pairs={{0,2},{1,3},{2,0},{3,1},{4,6},{5,7},{6,4},{7,5},{8,10},{9,11},{10,... | collective-permute-start | bytes 737288 | tf_op jit(solution)/shard_map/ppermute | solution.py:571
  114.3 1.6 collective-permute-start.63
  115.9 8.2 %collective-permute-start.64 = (bf16[48,2560]{1,0:T(8,128)(2,1)S(1)}, bf16[48,2560]{1,0:T(8,128)(2,1)S(1)}, u32[]{:S(2)}, u32[]{:S(2)}) collective-permute-start(bf16[48,2560]{1,0:T(8,128)(2,1)S(1)} %add_convert_fusion.12), channel_id=1, source_target_pairs={{0,2},{1,3},{2,0},{3,1},{4,6},{5,7},{6,4},{7,5},{8,10},{9,11},{10,... | collective-permute-start | bytes 737288 | tf_op jit(solution)/shard_map/ppermute | solution.py:571
  129.8 1.8 collective-permute-start.66
  131.7 8.2 %collective-permute-start.67 = (bf16[48,2560]{1,0:T(8,128)(2,1)S(1)}, bf16[48,2560]{1,0:T(8,128)(2,1)S(1)}, u32[]{:S(2)}, u32[]{:S(2)}) collective-permute-start(bf16[48,2560]{1,0:T(8,128)(2,1)S(1)} %add_convert_fusion.11), channel_id=1, source_target_pairs={{0,2},{1,3},{2,0},{3,1},{4,6},{5,7},{6,4},{7,5},{8,10},{9,11},{10,... | collective-permute-start | bytes 737288 | tf_op jit(solution)/shard_map/ppermute | solution.py:571
  147.5 8.6 %collective-permute-start.70 = (bf16[48,2560]{1,0:T(8,128)(2,1)S(1)}, bf16[48,2560]{1,0:T(8,128)(2,1)S(1)}, u32[]{:S(2)}, u32[]{:S(2)}) collective-permute-start(bf16[48,2560]{1,0:T(8,128)(2,1)S(1)} %add_convert_fusion.10), channel_id=1, source_target_pairs={{0,2},{1,3},{2,0},{3,1},{4,6},{5,7},{6,4},{7,5},{8,10},{9,11},{10,... | collective-permute-start | bytes 737288 | tf_op jit(solution)/shard_map/ppermute | solution.py:571
  156.2 2.0 %collective-permute-start.71 = (bf16[48,2560]{1,0:T(8,128)(2,1)S(1)}, bf16[48,2560]{1,0:T(8,128)(2,1)S(1)}, u32[]{:S(2)}, u32[]{:S(2)}) collective-permute-start(bf16[48,2560]{1,0:T(8,128)(2,1)S(1)} %add_convert_fusion.9.refs_0_.own_row), channel_id=1, source_target_pairs={{0,1},{1,0},{2,3},{3,2},{4,5},{5,4},{6,7},{7,6},{8,9},{9,8},{10,11... | collective-permute-start | bytes 737288 | tf_op jit(solution)/shard_map/ppermute | solution.py:580
  156.3 6.3 %collective-permute-start.75 = (bf16[336,128]{1,0:T(8,128)(2,1)S(1)}, bf16[336,128]{1,0:T(8,128)(2,1)S(1)}, u32[]{:S(2)}, u32[]{:S(2)}) collective-permute-start(bf16[336,128]{1,0:T(8,128)(2,1)S(1)} %get-tuple-element.357), channel_id=1, source_target_pairs={{0,1},{1,0},{2,3},{3,2},{4,5},{5,4},{6,7},{7,6},{8,9},{9,8},{10,11... | collective-permute-start | bytes 258056 | tf_op jit(solution)/shard_map/ppermute | solution.py:558
  156.8 5.8 %collective-permute-start.76 = (bf16[336,128]{1,0:T(8,128)(2,1)S(1)}, bf16[336,128]{1,0:T(8,128)(2,1)S(1)}, u32[]{:S(2)}, u32[]{:S(2)}) collective-permute-start(bf16[336,128]{1,0:T(8,128)(2,1)S(1)} %get-tuple-element.358), channel_id=1, source_target_pairs={{0,2},{1,3},{2,0},{3,1},{4,6},{5,7},{6,4},{7,5},{8,10},{9,11},{10,... | collective-permute-start | bytes 258056 | tf_op jit(solution)/shard_map/ppermute | solution.py:558
  158.0 4.8 %collective-permute-start.77 = (bf16[336,128]{1,0:T(8,128)(2,1)S(1)}, bf16[336,128]{1,0:T(8,128)(2,1)S(1)}, u32[]{:S(2)}, u32[]{:S(2)}) collective-permute-start(bf16[336,128]{1,0:T(8,128)(2,1)S(1)} %get-tuple-element.359), channel_id=1, source_target_pairs={{0,3},{1,2},{2,1},{3,0},{4,7},{5,6},{6,5},{7,4},{8,11},{9,10},{10,... | collective-permute-start | bytes 258056 | tf_op jit(solution)/shard_map/ppermute | solution.py:558
  160.2 5.5 %collective-permute-start.74 = (bf16[48,512]{1,0:T(8,128)(2,1)S(1)}, bf16[48,512]{1,0:T(8,128)(2,1)S(1)}, u32[]{:S(2)}, u32[]{:S(2)}) collective-permute-start(bf16[48,512]{1,0:T(8,128)(2,1)S(1)} %score.7.refs_8_), channel_id=1, source_target_pairs={{0,3},{1,2},{2,1},{3,0},{4,7},{5,6},{6,5},{7,4},{8,11},{9,10},{10,... | collective-permute-start | bytes 147464 | tf_op jit(solution)/shard_map/ppermute | solution.py:558
  161.7 4.5 %collective-permute-start.73 = (bf16[48,512]{1,0:T(8,128)(2,1)S(1)}, bf16[48,512]{1,0:T(8,128)(2,1)S(1)}, u32[]{:S(2)}, u32[]{:S(2)}) collective-permute-start(bf16[48,512]{1,0:T(8,128)(2,1)S(1)} %score.7.refs_8_), channel_id=1, source_target_pairs={{0,2},{1,3},{2,0},{3,1},{4,6},{5,7},{6,4},{7,5},{8,10},{9,11},{10,... | collective-permute-start | bytes 147464 | tf_op jit(solution)/shard_map/ppermute | solution.py:558
  162.6 3.6 %collective-permute-start.72 = (bf16[48,512]{1,0:T(8,128)(2,1)S(1)}, bf16[48,512]{1,0:T(8,128)(2,1)S(1)}, u32[]{:S(2)}, u32[]{:S(2)}) collective-permute-start(bf16[48,512]{1,0:T(8,128)(2,1)S(1)} %score.7.refs_8_), channel_id=1, source_target_pairs={{0,1},{1,0},{2,3},{3,2},{4,5},{5,4},{6,7},{7,6},{8,9},{9,8},{10,11... | collective-permute-start | bytes 147464 | tf_op jit(solution)/shard_map/ppermute | solution.py:558
  163.6 3.3 %collective-permute-start.80 = (f32[48,128]{1,0:T(8,128)S(1)}, f32[48,128]{1,0:T(8,128)S(1)}, u32[]{:S(2)}, u32[]{:S(2)}) collective-permute-start(f32[48,128]{1,0:T(8,128)S(1)} %finish.3.refs_0_), channel_id=1, source_target_pairs={{0,3},{1,2},{2,1},{3,0},{4,7},{5,6},{6,5},{7,4},{8,11},{9,10},{10,... | collective-permute-start | bytes 73736 | tf_op jit(solution)/shard_map/ppermute | solution.py:558
  164.8 3.8 %collective-permute-start.79 = (f32[48,128]{1,0:T(8,128)S(1)}, f32[48,128]{1,0:T(8,128)S(1)}, u32[]{:S(2)}, u32[]{:S(2)}) collective-permute-start(f32[48,128]{1,0:T(8,128)S(1)} %finish.3.refs_0_), channel_id=1, source_target_pairs={{0,2},{1,3},{2,0},{3,1},{4,6},{5,7},{6,4},{7,5},{8,10},{9,11},{10,... | collective-permute-start | bytes 73736 | tf_op jit(solution)/shard_map/ppermute | solution.py:558
  165.7 3.0 %collective-permute-start.78 = (f32[48,128]{1,0:T(8,128)S(1)}, f32[48,128]{1,0:T(8,128)S(1)}, u32[]{:S(2)}, u32[]{:S(2)}) collective-permute-start(f32[48,128]{1,0:T(8,128)S(1)} %finish.3.refs_0_), channel_id=1, source_target_pairs={{0,1},{1,0},{2,3},{3,2},{4,5},{5,4},{6,7},{7,6},{8,9},{9,8},{10,11... | collective-permute-start | bytes 73736 | tf_op jit(solution)/shard_map/ppermute | solution.py:558
  (30 other events, 148.7 us)
Sparse Core Ops, SparseCore 0:
  8.9 112.7 all-gather.1

commit v8 on v7

--- a/solution.py
+++ b/solution.py
@@ -14,7 +14,7 @@
 HD = 128
 STEPS = 8
 GROUP = HEADS // KVH
-CHUNK = 512
+CHUNK = 1280
 COLUMNS = 256
 ROWS = 16
 MASKED = -1e30

time: 194 us -> 191 us (0.985)
  Pallas kernels: 72.7 us -> 68.3 us
    pallas_call x8, Pallas kernels: 32.1 us -> 29.6 us  [expand(): pl.pallas_call(functools.partial(step_kernel, step), out_shape=(struct((s...]
    pallas_call x8, Pallas kernels: 10.2 us -> 7.94 us  [project_own(): pl.pallas_call(project_kernel, out_shape=struct((rows, w_out.shape[1] //...]
  transfers between devices with their start and end apart: 45 -> 45, of which waited for: 19 -> 25; matrix products, arithmetic and copies ran while one was open for 1% -> 1% of each run, Pallas kernels for 38% -> 36%
where the time goes in v8:
time: 191 us; the launch traced here: 187 us
  Pallas kernels  68.3 us (36%)
  waiting for transfers between devices  49.7 us (26%)
  starting transfers between devices  37.9 us (20%)
  between operations  15.4 us (8%)
  blocking collectives  12.3 us (6%)
  other arithmetic  1.95 us (1%)
    ppermute x8, waiting for transfers between devices, run(): lax.ppermute(sent, 'mp', pairs(mp, k))  38.9 us
    pallas_call x8, Pallas kernels, expand(): pl.pallas_call(functools.partial(step_kernel, step), out_shape=(struct((s...  29.6 us
    ppermute x8, starting transfers between devices, run(): lax.ppermute(sent, 'mp', pairs(mp, k))  13.7 us
    ppermute x7, starting transfers between devices, shards(): lax.ppermute(blocks[k], 'dp', pairs(groups, k))  12.5 us
    all_to_all x1, blocking collectives, shards(): table = lax.all_to_all(table, 'dp', split_axis=0, concat_axis=0, tiled=True)  12.3 us
    pallas_call x8, Pallas kernels, begin(): pl.pallas_call(begin_kernel, out_shape=struct((slots, w_query.shape[1] +...  9.95 us
    pallas_call x2, Pallas kernels, score(): pl.pallas_call(functools.partial(score_kernel, steps, load, mp), out_shap...  9.24 us
    ppermute x12, starting transfers between devices, run(): lax.ppermute(sums[k], 'mp', pairs(mp, k))  8.38 us
  transfers between devices with their start and end apart: 45, of which 25 were waited for; matrix products, arithmetic and copies ran while one was open for 1% of the time, Pallas kernels for 36%

profile of v8, /device:TPU:0, one launch (start us, length us, event | category | flops | bytes accessed | tf_op | source)
XLA Modules:
  0.0 187.4 jit_solution(736761215976218140)
XLA Ops:
  9.4 3.0 %collective-permute-start.37 = (bf16[8,3072]{1,0:T(8,128)(2,1)S(1)}, bf16[8,3072]{1,0:T(8,128)(2,1)S(1)}, u32[]{:S(2)}, u32[]{:S(2)}) collective-permute-start(bf16[8,3072]{1,0:T(8,128)(2,1)S(1)} %get-tuple-element.270), channel_id=1, source_target_pairs={{0,4},{4,0},{8,12},{12,8},{16,20},{20,16},{24,28},{28,24},{1,5},{5... | collective-permute-start | bytes 147464 | tf_op jit(solution)/shard_map/ppermute | solution.py:540
  12.5 1.6 collective-permute-start.38
  14.1 3.0 %collective-permute-start.40 = (bf16[8,3072]{1,0:T(8,128)(2,1)S(1)}, bf16[8,3072]{1,0:T(8,128)(2,1)S(1)}, u32[]{:S(2)}, u32[]{:S(2)}) collective-permute-start(bf16[8,3072]{1,0:T(8,128)(2,1)S(1)} %get-tuple-element.273), channel_id=1, source_target_pairs={{0,16},{4,20},{8,24},{12,28},{16,0},{20,4},{24,8},{28,12},{1,17},{... | collective-permute-start | bytes 147464 | tf_op jit(solution)/shard_map/ppermute | solution.py:540
  18.3 3.6 %collective-permute-start.42 = (bf16[8,3072]{1,0:T(8,128)(2,1)S(1)}, bf16[8,3072]{1,0:T(8,128)(2,1)S(1)}, u32[]{:S(2)}, u32[]{:S(2)}) collective-permute-start(bf16[8,3072]{1,0:T(8,128)(2,1)S(1)} %get-tuple-element.275), channel_id=1, source_target_pairs={{0,24},{4,28},{8,16},{12,20},{16,8},{20,12},{24,0},{28,4},{1,25},{... | collective-permute-start | bytes 147464 | tf_op jit(solution)/shard_map/ppermute | solution.py:540
  21.9 7.7 %load.3 = (bf16[5120,768]{1,0:T(8,128)(2,1)S(1)}, bf16[5120,256]{1,0:T(8,128)(2,1)S(1)}, bf16[5120,256]{1,0:T(8,128)(2,1)S(1)}, bf16[2048,256]{1,0:T(8,128)(2,1)...) custom-call(bf16[5120,768]{1,0:T(8,128)(2,1)} %refs_0_, bf16[5120,256]{1,0:T(8,128)(2,1)} %refs_1_, ...), custom_call_target="tpu_custom_call" | custom-call | bytes 25165824 | tf_op jit(solution)/shard_map/load/pallas_call | solution.py:223
  32.3 4.3 %expand.24 = (bf16[48,2560]{1,0:T(8,128)(2,1)S(1)}, bf16[48,768]{1,0:T(8,128)(2,1)S(1)}, bf16[48,256]{1,0:T(8,128)(2,1)S(1)}, bf16[48,256]{1,0:T(8,128)(2,1)S(1)}, f32[48,128]{1,0:T(8,128)}) custom-call(bf16[48,2560]{1,0:T(8,128)(2,1)S(1)} %get-tuple-element.298.own, bf16[48,2560]{1,0:T(8,128)(2,1)S(1)} %collective-permute-done.44.peer, ...), custom_call_target="tpu_custom_call" | custom-call | tf_op jit(solution)/shard_map/expand/pallas_call | solution.py:334
  38.2 1.7 collective-permute-start.46
  39.9 1.6 collective-permute-start.48
  41.8 4.0 %collective-permute-done.49.refs_7_ = f32[8,128]{1,0:T(8,128)S(1)} collective-permute-done((f32[8,128]{1,0:T(8,128)S(1)}, f32[8,128]{1,0:T(8,128)S(1)}, u32[]{:S(2)}, u32[]{:S(2)}) %collective-permute-start.49) | collective-permute-done | bytes 4128 | tf_op jit(solution)/shard_map/ppermute | solution.py:558
  48.2 3.5 %expand.25 = (bf16[48,2560]{1,0:T(8,128)(2,1)S(1)}, bf16[48,768]{1,0:T(8,128)(2,1)S(1)}, bf16[48,256]{1,0:T(8,128)(2,1)S(1)}, bf16[48,256]{1,0:T(8,128)(2,1)S(1)}, f32[48,128]{1,0:T(8,128)S(1)}) custom-call(bf16[48,2560]{1,0:T(8,128)(2,1)S(1)} %fusion.4.own.refs_0_, bf16[48,2560]{1,0:T(8,128)(2,1)S(1)} %collective-permute-done.50.peer.refs_7_, ...), custom_call_target="tpu_custom_call" | custom-call | tf_op jit(solution)/shard_map/expand/pallas_call | solution.py:334
  53.4 1.7 collective-permute-start.52
  55.1 6.5 %collective-permute-done.52 = bf16[48,2560]{1,0:T(8,128)(2,1)S(1)} collective-permute-done((bf16[48,2560]{1,0:T(8,128)(2,1)S(1)}, bf16[48,2560]{1,0:T(8,128)(2,1)S(1)}, u32[]{:S(2)}, u32[]{:S(2)}) %collective-permute-start.52) | collective-permute-done | bytes 245792 | tf_op jit(solution)/shard_map/ppermute | solution.py:571
  63.4 3.5 %expand.26 = (bf16[48,2560]{1,0:T(8,128)(2,1)S(1)}, bf16[48,768]{1,0:T(8,128)(2,1)S(1)}, bf16[48,256]{1,0:T(8,128)(2,1)S(1)}, bf16[48,256]{1,0:T(8,128)(2,1)S(1)}, f32[48,128]{1,0:T(8,128)S(1)}) custom-call(bf16[48,2560]{1,0:T(8,128)(2,1)S(1)} %get-tuple-element.397.own.refs_1_, bf16[48,2560]{1,0:T(8,128)(2,1)S(1)} %collective-permute-done.53.peer.refs_8_, ...), custom_call_target="tpu_custom_call" | custom-call | tf_op jit(solution)/shard_map/expand/pallas_call | solution.py:334
  68.5 1.7 collective-permute-start.55
  70.2 6.5 %collective-permute-done.55 = bf16[48,2560]{1,0:T(8,128)(2,1)S(1)} collective-permute-done((bf16[48,2560]{1,0:T(8,128)(2,1)S(1)}, bf16[48,2560]{1,0:T(8,128)(2,1)S(1)}, u32[]{:S(2)}, u32[]{:S(2)}) %collective-permute-start.55) | collective-permute-done | bytes 245792 | tf_op jit(solution)/shard_map/ppermute | solution.py:571
  78.4 3.6 %expand.27 = (bf16[48,2560]{1,0:T(8,128)(2,1)S(1)}, bf16[48,768]{1,0:T(8,128)(2,1)S(1)}, bf16[48,256]{1,0:T(8,128)(2,1)S(1)}, bf16[48,256]{1,0:T(8,128)(2,1)S(1)}, f32[48,128]{1,0:T(8,128)S(1)}) custom-call(bf16[48,2560]{1,0:T(8,128)(2,1)S(1)} %fusion.5.own.refs_2_, bf16[48,2560]{1,0:T(8,128)(2,1)S(1)} %collective-permute-done.56.peer.refs_9_, ...), custom_call_target="tpu_custom_call" | custom-call | tf_op jit(solution)/shard_map/expand/pallas_call | solution.py:334
  83.6 1.7 collective-permute-start.58
  85.3 6.5 %collective-permute-done.58 = bf16[48,2560]{1,0:T(8,128)(2,1)S(1)} collective-permute-done((bf16[48,2560]{1,0:T(8,128)(2,1)S(1)}, bf16[48,2560]{1,0:T(8,128)(2,1)S(1)}, u32[]{:S(2)}, u32[]{:S(2)}) %collective-permute-start.58) | collective-permute-done | bytes 245792 | tf_op jit(solution)/shard_map/ppermute | solution.py:571
  93.5 3.6 %expand.28 = (bf16[48,2560]{1,0:T(8,128)(2,1)S(1)}, bf16[48,768]{1,0:T(8,128)(2,1)S(1)}, bf16[48,256]{1,0:T(8,128)(2,1)S(1)}, bf16[48,256]{1,0:T(8,128)(2,1)S(1)}, f32[48,128]{1,0:T(8,128)S(1)}) custom-call(bf16[48,2560]{1,0:T(8,128)(2,1)S(1)} %get-tuple-element.395.own.refs_3_, bf16[48,2560]{1,0:T(8,128)(2,1)S(1)} %collective-permute-done.59.peer.refs_10_, ...), custom_call_target="tpu_custom_call" | custom-call | tf_op jit(solution)/shard_map/expand/pallas_call | solution.py:334
  98.7 1.7 collective-permute-start.61
  100.4 6.5 %collective-permute-done.61 = bf16[48,2560]{1,0:T(8,128)(2,1)S(1)} collective-permute-done((bf16[48,2560]{1,0:T(8,128)(2,1)S(1)}, bf16[48,2560]{1,0:T(8,128)(2,1)S(1)}, u32[]{:S(2)}, u32[]{:S(2)}) %collective-permute-start.61) | collective-permute-done | bytes 245792 | tf_op jit(solution)/shard_map/ppermute | solution.py:571
  108.6 3.6 %expand.29 = (bf16[48,2560]{1,0:T(8,128)(2,1)S(1)}, bf16[48,768]{1,0:T(8,128)(2,1)S(1)}, bf16[48,256]{1,0:T(8,128)(2,1)S(1)}, bf16[48,256]{1,0:T(8,128)(2,1)S(1)}, f32[48,128]{1,0:T(8,128)S(1)}) custom-call(bf16[48,2560]{1,0:T(8,128)(2,1)S(1)} %fusion.6.own.refs_4_, bf16[48,2560]{1,0:T(8,128)(2,1)S(1)} %collective-permute-done.62.peer.refs_11_, ...), custom_call_target="tpu_custom_call" | custom-call | tf_op jit(solution)/shard_map/expand/pallas_call | solution.py:334
  113.9 1.7 collective-permute-start.64
  115.6 6.5 %collective-permute-done.64 = bf16[48,2560]{1,0:T(8,128)(2,1)S(1)} collective-permute-done((bf16[48,2560]{1,0:T(8,128)(2,1)S(1)}, bf16[48,2560]{1,0:T(8,128)(2,1)S(1)}, u32[]{:S(2)}, u32[]{:S(2)}) %collective-permute-start.64) | collective-permute-done | bytes 245792 | tf_op jit(solution)/shard_map/ppermute | solution.py:571
  123.8 3.6 %expand.30 = (bf16[48,2560]{1,0:T(8,128)(2,1)S(1)}, bf16[48,768]{1,0:T(8,128)(2,1)S(1)}, bf16[48,256]{1,0:T(8,128)(2,1)S(1)}, bf16[48,256]{1,0:T(8,128)(2,1)S(1)}, f32[48,128]{1,0:T(8,128)S(1)}) custom-call(bf16[48,2560]{1,0:T(8,128)(2,1)S(1)} %get-tuple-element.393.own.refs_5_, bf16[48,2560]{1,0:T(8,128)(2,1)S(1)} %collective-permute-done.65.peer.refs_12_, ...), custom_call_target="tpu_custom_call" | custom-call | tf_op jit(solution)/shard_map/expand/pallas_call | solution.py:334
  129.1 1.7 collective-permute-start.67
  130.8 6.5 %collective-permute-done.67 = bf16[48,2560]{1,0:T(8,128)(2,1)S(1)} collective-permute-done((bf16[48,2560]{1,0:T(8,128)(2,1)S(1)}, bf16[48,2560]{1,0:T(8,128)(2,1)S(1)}, u32[]{:S(2)}, u32[]{:S(2)}) %collective-permute-start.67) | collective-permute-done | bytes 245792 | tf_op jit(solution)/shard_map/ppermute | solution.py:571
  139.0 3.9 %expand.31 = (bf16[48,2560]{1,0:T(8,128)(2,1)S(1)}, bf16[48,768]{1,0:T(8,128)(2,1)S(1)}, bf16[48,256]{1,0:T(8,128)(2,1)}, bf16[48,256]{1,0:T(8,128)(2,1)}, f32[48,128]{1,0:T(8,128)S(1)}) custom-call(bf16[48,2560]{1,0:T(8,128)(2,1)S(1)} %fusion.7.own.refs_6_, bf16[48,2560]{1,0:T(8,128)(2,1)S(1)} %collective-permute-done.68.peer.refs_13_, ...), custom_call_target="tpu_custom_call" | custom-call | tf_op jit(solution)/shard_map/expand/pallas_call | solution.py:334
  144.4 1.7 collective-permute-start.70
  146.1 7.3 %score.6 = (bf16[336,128]{1,0:T(8,128)(2,1)S(1)}, bf16[336,128]{1,0:T(8,128)(2,1)S(1)}, bf16[336,128]{1,0:T(8,128)(2,1)S(1)}, bf16[336,128]{1,0:T(8,128)(2,1)S(1)}, bf16[8,1280,512]{2,1,0:T(8,128)(2,1)S(1)}) custom-call(f32[48,128]{1,0:T(8,128)S(1)} %get-tuple-element.297.notes, bf16[8,1280,512]{2,1,0:T(8,128)(2,1)} %all-gather.2.cloned.1.call-done.up, ...), custom_call_target="tpu_custom_call" | custom-call | tf_op jit(solution)/shard_map/score/pallas_call | solution.py:427
  155.6 1.9 %score.7.refs_8_ = bf16[48,512]{1,0:T(8,128)(2,1)S(1)} custom-call(f32[48,128]{1,0:T(8,128)S(1)} %get-tuple-element.297.notes, bf16[8,1280,512]{2,1,0:T(8,128)(2,1)S(1)} %get-tuple-element.340.up, bf16[48,2560]{1,0:T(8,128)(2,1)S(1)} %add_convert_fusion.9.refs_0_.own_row, bf16[48,2560]{1,0:T(8,128)(2,1)S(1)} %collective-permute-done.71.refs_1_.peer_row), custom_call_target="tpu_custom_call" | custom-call | tf_op jit(solution)/shard_map/score/pallas_call | solution.py:427
  167.4 12.3 %all_to_all.9 = f32[8,8,128]{2,1,0:T(8,128)S(1)} all-to-all(f32[8,8,128]{2,1,0:T(8,128)S(1)} %bitcast.30), channel_id=1, replica_groups=mesh['dp'=8,'mp'=4] {'dp'}, dimensions={0} | all-to-all | bytes 65536 | tf_op jit(solution)/shard_map/all_to_all | solution.py:596
  (144 shorter events, 43.7 us)
Async XLA Ops:
  6.5 139.6 %all-gather.2.cloned.1.call-start = ((), (), s32[]{:S(2)}) async-start(), calls=%async_computation.1 | async-start | bytes 11796480 | tf_op jit(solution)/shard_map/all_gather | solution.py:533
  9.4 8.9 %collective-permute-start.37 = (bf16[8,3072]{1,0:T(8,128)(2,1)S(1)}, bf16[8,3072]{1,0:T(8,128)(2,1)S(1)}, u32[]{:S(2)}, u32[]{:S(2)}) collective-permute-start(bf16[8,3072]{1,0:T(8,128)(2,1)S(1)} %get-tuple-element.270), channel_id=1, source_target_pairs={{0,4},{4,0},{8,12},{12,8},{16,20},{20,16},{24,28},{28,24},{1,5},{5... | collective-permute-start | bytes 147464 | tf_op jit(solution)/shard_map/ppermute | solution.py:540
  12.5 9.5 %collective-permute-start.38 = (bf16[8,3072]{1,0:T(8,128)(2,1)S(1)}, bf16[8,3072]{1,0:T(8,128)(2,1)S(1)}, u32[]{:S(2)}, u32[]{:S(2)}) collective-permute-start(bf16[8,3072]{1,0:T(8,128)(2,1)S(1)} %get-tuple-element.271), channel_id=1, source_target_pairs={{0,8},{4,12},{8,0},{12,4},{16,24},{20,28},{24,16},{28,20},{1,9},{5... | collective-permute-start | bytes 147464 | tf_op jit(solution)/shard_map/ppermute | solution.py:540
  14.1 15.6 %collective-permute-start.39 = (bf16[8,3072]{1,0:T(8,128)(2,1)S(1)}, bf16[8,3072]{1,0:T(8,128)(2,1)S(1)}, u32[]{:S(2)}, u32[]{:S(2)}) collective-permute-start(bf16[8,3072]{1,0:T(8,128)(2,1)S(1)} %get-tuple-element.272), channel_id=1, source_target_pairs={{0,12},{4,8},{8,4},{12,0},{16,28},{20,24},{24,20},{28,16},{1,13},{... | collective-permute-start | bytes 147464 | tf_op jit(solution)/shard_map/ppermute | solution.py:540
  14.1 15.6 %collective-permute-start.40 = (bf16[8,3072]{1,0:T(8,128)(2,1)S(1)}, bf16[8,3072]{1,0:T(8,128)(2,1)S(1)}, u32[]{:S(2)}, u32[]{:S(2)}) collective-permute-start(bf16[8,3072]{1,0:T(8,128)(2,1)S(1)} %get-tuple-element.273), channel_id=1, source_target_pairs={{0,16},{4,20},{8,24},{12,28},{16,0},{20,4},{24,8},{28,12},{1,17},{... | collective-permute-start | bytes 147464 | tf_op jit(solution)/shard_map/ppermute | solution.py:540
  17.0 12.7 %collective-permute-start.41 = (bf16[8,3072]{1,0:T(8,128)(2,1)S(1)}, bf16[8,3072]{1,0:T(8,128)(2,1)S(1)}, u32[]{:S(2)}, u32[]{:S(2)}) collective-permute-start(bf16[8,3072]{1,0:T(8,128)(2,1)S(1)} %get-tuple-element.274), channel_id=1, source_target_pairs={{0,20},{4,16},{8,28},{12,24},{16,4},{20,0},{24,12},{28,8},{1,21},{... | collective-permute-start | bytes 147464 | tf_op jit(solution)/shard_map/ppermute | solution.py:540
  18.3 11.4 %collective-permute-start.42 = (bf16[8,3072]{1,0:T(8,128)(2,1)S(1)}, bf16[8,3072]{1,0:T(8,128)(2,1)S(1)}, u32[]{:S(2)}, u32[]{:S(2)}) collective-permute-start(bf16[8,3072]{1,0:T(8,128)(2,1)S(1)} %get-tuple-element.275), channel_id=1, source_target_pairs={{0,24},{4,28},{8,16},{12,20},{16,8},{20,12},{24,0},{28,4},{1,25},{... | collective-permute-start | bytes 147464 | tf_op jit(solution)/shard_map/ppermute | solution.py:540
  21.9 7.8 %collective-permute-start.43 = (bf16[8,3072]{1,0:T(8,128)(2,1)S(1)}, bf16[8,3072]{1,0:T(8,128)(2,1)S(1)}, u32[]{:S(2)}, u32[]{:S(2)}) collective-permute-start(bf16[8,3072]{1,0:T(8,128)(2,1)S(1)} %get-tuple-element.276), channel_id=1, source_target_pairs={{0,28},{4,24},{8,20},{12,16},{16,12},{20,8},{24,4},{28,0},{1,29},{... | collective-permute-start | bytes 147464 | tf_op jit(solution)/shard_map/ppermute | solution.py:540
  30.7 1.6 collective-permute-start.44
  38.2 8.4 %collective-permute-start.46 = (bf16[48,2560]{1,0:T(8,128)(2,1)S(1)}, bf16[48,2560]{1,0:T(8,128)(2,1)S(1)}, u32[]{:S(2)}, u32[]{:S(2)}) collective-permute-start(bf16[48,2560]{1,0:T(8,128)(2,1)S(1)} %add_convert_fusion.17), channel_id=1, source_target_pairs={{0,2},{1,3},{2,0},{3,1},{4,6},{5,7},{6,4},{7,5},{8,10},{9,11},{10,... | collective-permute-start | bytes 737288 | tf_op jit(solution)/shard_map/ppermute | solution.py:571
  39.9 5.9 %collective-permute-start.49 = (f32[8,128]{1,0:T(8,128)S(1)}, f32[8,128]{1,0:T(8,128)S(1)}, u32[]{:S(2)}, u32[]{:S(2)}) collective-permute-start(f32[8,128]{1,0:T(8,128)S(1)} %get-tuple-element.360.scale.refs_4_), channel_id=1, source_target_pairs={{0,3},{1,2},{2,1},{3,0},{4,7},{5,6},{6,5},{7,4},{8,11},{9,10},{10,... | collective-permute-start | bytes 12296 | tf_op jit(solution)/shard_map/ppermute | solution.py:558
  39.9 6.6 %collective-permute-start.48 = (f32[8,128]{1,0:T(8,128)S(1)}, f32[8,128]{1,0:T(8,128)S(1)}, u32[]{:S(2)}, u32[]{:S(2)}) collective-permute-start(f32[8,128]{1,0:T(8,128)S(1)} %get-tuple-element.360.scale.refs_4_), channel_id=1, source_target_pairs={{0,2},{1,3},{2,0},{3,1},{4,6},{5,7},{6,4},{7,5},{8,10},{9,11},{10,... | collective-permute-start | bytes 12296 | tf_op jit(solution)/shard_map/ppermute | solution.py:558
  41.5 5.0 %collective-permute-start.47 = (f32[8,128]{1,0:T(8,128)S(1)}, f32[8,128]{1,0:T(8,128)S(1)}, u32[]{:S(2)}, u32[]{:S(2)}) collective-permute-start(f32[8,128]{1,0:T(8,128)S(1)} %get-tuple-element.360.scale.refs_4_), channel_id=1, source_target_pairs={{0,1},{1,0},{2,3},{3,2},{4,5},{5,4},{6,7},{7,6},{8,9},{9,8},{10,11... | collective-permute-start | bytes 12296 | tf_op jit(solution)/shard_map/ppermute | solution.py:558
  46.7 1.6 collective-permute-start.50
  53.4 8.2 %collective-permute-start.52 = (bf16[48,2560]{1,0:T(8,128)(2,1)S(1)}, bf16[48,2560]{1,0:T(8,128)(2,1)S(1)}, u32[]{:S(2)}, u32[]{:S(2)}) collective-permute-start(bf16[48,2560]{1,0:T(8,128)(2,1)S(1)} %add_convert_fusion.16), channel_id=1, source_target_pairs={{0,2},{1,3},{2,0},{3,1},{4,6},{5,7},{6,4},{7,5},{8,10},{9,11},{10,... | collective-permute-start | bytes 737288 | tf_op jit(solution)/shard_map/ppermute | solution.py:571
  61.8 1.6 collective-permute-start.53
  68.5 8.2 %collective-permute-start.55 = (bf16[48,2560]{1,0:T(8,128)(2,1)S(1)}, bf16[48,2560]{1,0:T(8,128)(2,1)S(1)}, u32[]{:S(2)}, u32[]{:S(2)}) collective-permute-start(bf16[48,2560]{1,0:T(8,128)(2,1)S(1)} %add_convert_fusion.15), channel_id=1, source_target_pairs={{0,2},{1,3},{2,0},{3,1},{4,6},{5,7},{6,4},{7,5},{8,10},{9,11},{10,... | collective-permute-start | bytes 737288 | tf_op jit(solution)/shard_map/ppermute | solution.py:571
  83.6 8.2 %collective-permute-start.58 = (bf16[48,2560]{1,0:T(8,128)(2,1)S(1)}, bf16[48,2560]{1,0:T(8,128)(2,1)S(1)}, u32[]{:S(2)}, u32[]{:S(2)}) collective-permute-start(bf16[48,2560]{1,0:T(8,128)(2,1)S(1)} %add_convert_fusion.14), channel_id=1, source_target_pairs={{0,2},{1,3},{2,0},{3,1},{4,6},{5,7},{6,4},{7,5},{8,10},{9,11},{10,... | collective-permute-start | bytes 737288 | tf_op jit(solution)/shard_map/ppermute | solution.py:571
  98.7 8.2 %collective-permute-start.61 = (bf16[48,2560]{1,0:T(8,128)(2,1)S(1)}, bf16[48,2560]{1,0:T(8,128)(2,1)S(1)}, u32[]{:S(2)}, u32[]{:S(2)}) collective-permute-start(bf16[48,2560]{1,0:T(8,128)(2,1)S(1)} %add_convert_fusion.13), channel_id=1, source_target_pairs={{0,2},{1,3},{2,0},{3,1},{4,6},{5,7},{6,4},{7,5},{8,10},{9,11},{10,... | collective-permute-start | bytes 737288 | tf_op jit(solution)/shard_map/ppermute | solution.py:571
  113.9 8.2 %collective-permute-start.64 = (bf16[48,2560]{1,0:T(8,128)(2,1)S(1)}, bf16[48,2560]{1,0:T(8,128)(2,1)S(1)}, u32[]{:S(2)}, u32[]{:S(2)}) collective-permute-start(bf16[48,2560]{1,0:T(8,128)(2,1)S(1)} %add_convert_fusion.12), channel_id=1, source_target_pairs={{0,2},{1,3},{2,0},{3,1},{4,6},{5,7},{6,4},{7,5},{8,10},{9,11},{10,... | collective-permute-start | bytes 737288 | tf_op jit(solution)/shard_map/ppermute | solution.py:571
  129.1 8.2 %collective-permute-start.67 = (bf16[48,2560]{1,0:T(8,128)(2,1)S(1)}, bf16[48,2560]{1,0:T(8,128)(2,1)S(1)}, u32[]{:S(2)}, u32[]{:S(2)}) collective-permute-start(bf16[48,2560]{1,0:T(8,128)(2,1)S(1)} %add_convert_fusion.11), channel_id=1, source_target_pairs={{0,2},{1,3},{2,0},{3,1},{4,6},{5,7},{6,4},{7,5},{8,10},{9,11},{10,... | collective-permute-start | bytes 737288 | tf_op jit(solution)/shard_map/ppermute | solution.py:571
  144.4 9.0 %collective-permute-start.70 = (bf16[48,2560]{1,0:T(8,128)(2,1)S(1)}, bf16[48,2560]{1,0:T(8,128)(2,1)S(1)}, u32[]{:S(2)}, u32[]{:S(2)}) collective-permute-start(bf16[48,2560]{1,0:T(8,128)(2,1)S(1)} %add_convert_fusion.10), channel_id=1, source_target_pairs={{0,2},{1,3},{2,0},{3,1},{4,6},{5,7},{6,4},{7,5},{8,10},{9,11},{10,... | collective-permute-start | bytes 737288 | tf_op jit(solution)/shard_map/ppermute | solution.py:571
  153.6 2.0 %collective-permute-start.71 = (bf16[48,2560]{1,0:T(8,128)(2,1)S(1)}, bf16[48,2560]{1,0:T(8,128)(2,1)S(1)}, u32[]{:S(2)}, u32[]{:S(2)}) collective-permute-start(bf16[48,2560]{1,0:T(8,128)(2,1)S(1)} %add_convert_fusion.9.refs_0_.own_row), channel_id=1, source_target_pairs={{0,1},{1,0},{2,3},{3,2},{4,5},{5,4},{6,7},{7,6},{8,9},{9,8},{10,11... | collective-permute-start | bytes 737288 | tf_op jit(solution)/shard_map/ppermute | solution.py:580
  153.7 6.3 %collective-permute-start.75 = (bf16[336,128]{1,0:T(8,128)(2,1)S(1)}, bf16[336,128]{1,0:T(8,128)(2,1)S(1)}, u32[]{:S(2)}, u32[]{:S(2)}) collective-permute-start(bf16[336,128]{1,0:T(8,128)(2,1)S(1)} %get-tuple-element.357), channel_id=1, source_target_pairs={{0,1},{1,0},{2,3},{3,2},{4,5},{5,4},{6,7},{7,6},{8,9},{9,8},{10,11... | collective-permute-start | bytes 258056 | tf_op jit(solution)/shard_map/ppermute | solution.py:558
  154.2 5.8 %collective-permute-start.76 = (bf16[336,128]{1,0:T(8,128)(2,1)S(1)}, bf16[336,128]{1,0:T(8,128)(2,1)S(1)}, u32[]{:S(2)}, u32[]{:S(2)}) collective-permute-start(bf16[336,128]{1,0:T(8,128)(2,1)S(1)} %get-tuple-element.358), channel_id=1, source_target_pairs={{0,2},{1,3},{2,0},{3,1},{4,6},{5,7},{6,4},{7,5},{8,10},{9,11},{10,... | collective-permute-start | bytes 258056 | tf_op jit(solution)/shard_map/ppermute | solution.py:558
  155.0 4.9 %collective-permute-start.77 = (bf16[336,128]{1,0:T(8,128)(2,1)S(1)}, bf16[336,128]{1,0:T(8,128)(2,1)S(1)}, u32[]{:S(2)}, u32[]{:S(2)}) collective-permute-start(bf16[336,128]{1,0:T(8,128)(2,1)S(1)} %get-tuple-element.359), channel_id=1, source_target_pairs={{0,3},{1,2},{2,1},{3,0},{4,7},{5,6},{6,5},{7,4},{8,11},{9,10},{10,... | collective-permute-start | bytes 258056 | tf_op jit(solution)/shard_map/ppermute | solution.py:558
  157.5 5.5 %collective-permute-start.74 = (bf16[48,512]{1,0:T(8,128)(2,1)S(1)}, bf16[48,512]{1,0:T(8,128)(2,1)S(1)}, u32[]{:S(2)}, u32[]{:S(2)}) collective-permute-start(bf16[48,512]{1,0:T(8,128)(2,1)S(1)} %score.7.refs_8_), channel_id=1, source_target_pairs={{0,3},{1,2},{2,1},{3,0},{4,7},{5,6},{6,5},{7,4},{8,11},{9,10},{10,... | collective-permute-start | bytes 147464 | tf_op jit(solution)/shard_map/ppermute | solution.py:558
  158.7 4.8 %collective-permute-start.73 = (bf16[48,512]{1,0:T(8,128)(2,1)S(1)}, bf16[48,512]{1,0:T(8,128)(2,1)S(1)}, u32[]{:S(2)}, u32[]{:S(2)}) collective-permute-start(bf16[48,512]{1,0:T(8,128)(2,1)S(1)} %score.7.refs_8_), channel_id=1, source_target_pairs={{0,2},{1,3},{2,0},{3,1},{4,6},{5,7},{6,4},{7,5},{8,10},{9,11},{10,... | collective-permute-start | bytes 147464 | tf_op jit(solution)/shard_map/ppermute | solution.py:558
  159.9 3.6 %collective-permute-start.72 = (bf16[48,512]{1,0:T(8,128)(2,1)S(1)}, bf16[48,512]{1,0:T(8,128)(2,1)S(1)}, u32[]{:S(2)}, u32[]{:S(2)}) collective-permute-start(bf16[48,512]{1,0:T(8,128)(2,1)S(1)} %score.7.refs_8_), channel_id=1, source_target_pairs={{0,1},{1,0},{2,3},{3,2},{4,5},{5,4},{6,7},{7,6},{8,9},{9,8},{10,11... | collective-permute-start | bytes 147464 | tf_op jit(solution)/shard_map/ppermute | solution.py:558
  160.8 3.4 %collective-permute-start.80 = (f32[48,128]{1,0:T(8,128)S(1)}, f32[48,128]{1,0:T(8,128)S(1)}, u32[]{:S(2)}, u32[]{:S(2)}) collective-permute-start(f32[48,128]{1,0:T(8,128)S(1)} %finish.3.refs_0_), channel_id=1, source_target_pairs={{0,3},{1,2},{2,1},{3,0},{4,7},{5,6},{6,5},{7,4},{8,11},{9,10},{10,... | collective-permute-start | bytes 73736 | tf_op jit(solution)/shard_map/ppermute | solution.py:558
  161.8 3.8 %collective-permute-start.79 = (f32[48,128]{1,0:T(8,128)S(1)}, f32[48,128]{1,0:T(8,128)S(1)}, u32[]{:S(2)}, u32[]{:S(2)}) collective-permute-start(f32[48,128]{1,0:T(8,128)S(1)} %finish.3.refs_0_), channel_id=1, source_target_pairs={{0,2},{1,3},{2,0},{3,1},{4,6},{5,7},{6,4},{7,5},{8,10},{9,11},{10,... | collective-permute-start | bytes 73736 | tf_op jit(solution)/shard_map/ppermute | solution.py:558
  163.0 2.6 %collective-permute-start.78 = (f32[48,128]{1,0:T(8,128)S(1)}, f32[48,128]{1,0:T(8,128)S(1)}, u32[]{:S(2)}, u32[]{:S(2)}) collective-permute-start(f32[48,128]{1,0:T(8,128)S(1)} %finish.3.refs_0_), channel_id=1, source_target_pairs={{0,1},{1,0},{2,3},{3,2},{4,5},{5,4},{6,7},{7,6},{8,9},{9,8},{10,11... | collective-permute-start | bytes 73736 | tf_op jit(solution)/shard_map/ppermute | solution.py:558
  (30 other events, 144.2 us)
Sparse Core Ops, SparseCore 0:
  8.9 112.7 all-gather.1
